TPU v7x, 128 devices: a whole 4x4x4 slice. The times are simulated.
128 devices in a mesh: ax: 8 (over x, core), az: 16 (over y, z).
Axes of the slice: x: 4, y: 4, z: 4, core: 2. Of those that a mesh axis runs over, the one named last changes fastest.
Arguments:
- state: float32 [5, 64, 128, 128], P(None, 'ax', 'az'), may hold values from -6 to 6
- surf_index: int32 [34816], P(('ax', 'az')), may hold values from 0 to 63
- surf_count: int32 [8, 16], P('ax', 'az'), may hold values from 1 to 272, as said below
- delay: int32 [34816, 2048], P(('ax', 'az')), may hold values from 0 to 510
- fraction: float32 [34816, 2048], P(('ax', 'az')), may hold values from 0 to 1
Outputs:
- signal: float32 [2048, 512], P(('ax', 'az'))
Inputs may be any that keep to these rules, and one draw needn't show every extreme that they name: `surf_count`: devices in the first half of the axial index carry exactly 272 live slots; the others carry from 1 to 68.
All inputs are finite; a program needn't handle non-finite values.
Results may differ from a plain program's by a relative error of at most 0.0001.
Values sent between devices are 32-bit elements; how exact they have to be, the bound alone decides.
No kernel may reach another device: no remote copies, remote signals or barrier semaphores. Data moves between devices by JAX's collectives and lax.ppermute only.
A program may use at most 64 MiB of HBM per device.

v0:
```python
import jax
import jax.numpy as jnp
import numpy as np
from jax import lax
from jax.sharding import PartitionSpec as P

NT = 512


MEAN_FLOW = 0.5
TIME_STEP = 0.05
AMPLITUDE = 0.05


def padded_2(x, sides, width, wrap):
    for axis, dim in sides:
        size, length = (lax.axis_size(axis), x.shape[dim])
        up = [(i, (i + 1) % size) for i in range(size if wrap else size - 1)]
        down = [(j, i) for i, j in up]
        last = lax.slice_in_dim(x, length - width, length, axis=dim)
        leading = lax.slice_in_dim(x, 0, width, axis=dim)
        before = lax.ppermute(last, axis, up)
        after = lax.ppermute(leading, axis, down)
        x = jnp.concatenate([before, x, after], axis=dim)
    return x


def lobatto_matrix():
    points = np.array([-1.0, -1.0 / np.sqrt(5.0), 1.0 / np.sqrt(5.0), 1.0])
    table = np.zeros((4, 4))
    for i in range(4):
        for j in range(4):
            if i == j:
                table[i, j] = sum((1.0 / (points[i] - points[m]) for m in range(4) if m != i))
            else:
                a = np.prod([points[i] - points[m] for m in range(4) if m != i])
                b = np.prod([points[j] - points[m] for m in range(4) if m != j])
                table[i, j] = a / (b * (points[i] - points[j]))
    return table


def flux_axial(fields):
    density, vel_axial, vel_azim, vel_radial, pressure = (
        fields[0],
        fields[1],
        fields[2],
        fields[3],
        fields[4],
    )
    return jnp.stack(
        [
            MEAN_FLOW * density + vel_axial,
            MEAN_FLOW * vel_axial + pressure,
            MEAN_FLOW * vel_azim,
            MEAN_FLOW * vel_radial,
            MEAN_FLOW * pressure + vel_axial,
        ]
    )


def flux_azimuthal(fields):
    zeros = jnp.zeros_like(fields[0])
    return jnp.stack([fields[2], zeros, fields[4], zeros, fields[2]])


def flux_radial(fields):
    zeros = jnp.zeros_like(fields[0])
    return jnp.stack([fields[3], zeros, zeros, fields[4], fields[3]])


def fr_derivative(padded, axis, flux_fn, speed):
    length = padded.shape[axis] - 2
    elements = length // 4
    inner = lax.slice_in_dim(padded, 1, length + 1, axis=axis)
    outer_left = lax.slice_in_dim(padded, 0, length, 4, axis)
    outer_right = lax.slice_in_dim(padded, 5, length + 2, 4, axis)
    first_node = lax.slice_in_dim(padded, 1, length + 1, 4, axis)
    last_node = lax.slice_in_dim(padded, 4, length + 2, 4, axis)
    flux_first = flux_fn(first_node)
    flux_last = flux_fn(last_node)
    common_left = 0.5 * (flux_fn(outer_left) + flux_first) - 0.5 * speed * (first_node - outer_left)
    common_right = 0.5 * (flux_last + flux_fn(outer_right)) - 0.5 * speed * (
        outer_right - last_node
    )
    shape = inner.shape
    split = shape[:axis] + (elements, 4) + shape[axis + 1 :]
    blocks = flux_fn(inner).reshape(split)
    table = lobatto_matrix()
    bshape = [1] * len(split)
    bshape[axis + 1] = 4
    result = jnp.zeros(split, jnp.float32)
    for j in range(4):
        column = lax.slice_in_dim(blocks, j, j + 1, axis=axis + 1)
        result = result + jnp.asarray(table[:, j].reshape(bshape), jnp.float32) * column
    lift_right = jnp.asarray(np.array([0.0, 0.0, 0.0, 6.0]).reshape(bshape), jnp.float32)
    lift_left = jnp.asarray(np.array([6.0, 0.0, 0.0, 0.0]).reshape(bshape), jnp.float32)
    result = result + lift_right * jnp.expand_dims(common_right - flux_last, axis + 1)
    result = result - lift_left * jnp.expand_dims(common_left - flux_first, axis + 1)
    return result.reshape(shape)


def accumulate(values, delays, fracs):
    observers = delays.shape[1]
    samples = NT
    width = min(128, observers)
    count_blocks = observers // width
    times = jnp.arange(samples, dtype=jnp.int32)

    def one_block(number):
        start = number * width
        block_delay = lax.dynamic_slice_in_dim(delays, start, width, 1)
        block_frac = lax.dynamic_slice_in_dim(fracs, start, width, 1)
        amplitude = AMPLITUDE * samples / (samples + block_delay.astype(jnp.float32))
        weighted = values[:, None] * amplitude
        lower_weight = (1.0 - block_frac) * weighted
        upper_weight = block_frac * weighted
        hit = block_delay[:, :, None] == times[None, None, :]
        lower_sum = jnp.sum(jnp.where(hit, lower_weight[:, :, None], 0.0), axis=0)
        upper_sum = jnp.sum(jnp.where(hit, upper_weight[:, :, None], 0.0), axis=0)
        moved = jnp.concatenate(
            [jnp.zeros((width, 1), jnp.float32), upper_sum[:, : samples - 1]], axis=1
        )
        return lower_sum + moved

    stacked = lax.map(one_block, jnp.arange(count_blocks, dtype=jnp.int32))
    return stacked.reshape(observers, samples)


def local(state, surf_index, surf_count, delay, fraction):
    padded_x = padded_2(state, (("ax", 1),), 1, False)
    padded_y = padded_2(state, (("az", 2),), 1, True)
    padded_z = jnp.pad(state, ((0, 0), (0, 0), (0, 0), (1, 1)))
    change = fr_derivative(padded_x, 1, flux_axial, 1.5)
    change = change + fr_derivative(padded_y, 2, flux_azimuthal, 1.0)
    change = change + fr_derivative(padded_z, 3, flux_radial, 1.0)
    updated = state - TIME_STEP * change
    plane_index = 4 * (state.shape[3] // 8)
    plane = (updated[4, :, :, plane_index] + updated[3, :, :, plane_index]).reshape(-1)
    slot_total = surf_index.shape[0]
    live_slots = surf_count[0, 0]
    source = plane[surf_index]
    live = jnp.arange(slot_total, dtype=jnp.int32) < live_slots
    source = jnp.where(live, source, jnp.zeros_like(source))
    partial_sums = accumulate(source, delay, fraction)
    signal = lax.psum_scatter(partial_sums, ("ax", "az"), scatter_dimension=0, tiled=True)
    return signal


def solution(mesh):
    placed = (
        P(None, "ax", "az", None),
        P(("ax", "az")),
        P("ax", "az"),
        P(("ax", "az"), None),
        P(("ax", "az"), None),
    )
    return jax.shard_map(
        local, mesh=mesh, in_specs=placed, out_specs=P(("ax", "az"), None), check_vma=False
    )
```

profile of v0, /device:TPU:0, one launch (start us, length us, event | category | flops | bytes accessed | tf_op | source)
XLA Modules:
  0.0 1064.4 jit_solution(3152604427607072315)
XLA Ops:
  6.5 1.4 fusion.19
  7.9 1.9 collective-permute-start
  9.8 1.3 collective-permute-start.1
  12.7 2.4 collective-permute-start.2
  15.2 4.6 collective-permute-start.3
  21.6 2.9 slice.288
  24.5 2.9 slice.291
  27.3 2.8 slice.294
  30.2 2.9 slice.297
  38.1 1.4 slice_bitcast_fusion.3
  42.5 1.1 copy.111
  43.6 1.3 mul.745
  44.9 1.4 copy.112
  46.3 1.1 copy.113
  47.4 1.3 mul.754
  48.6 1.4 copy.114
  50.1 1.4 copy.94
  51.5 1.4 copy.95
  54.2 1.3 mul.712
  55.4 1.4 copy.107
  56.8 1.3 mul.720
  58.1 1.4 copy.108
  59.5 1.3 mul.728
  60.8 1.4 copy.109
  62.5 1.4 copy.110
  78.8 2.4 gather_fusion
  81.2 333.4 %while.11 = (s32[]{:T(128)}, f32[16,128,512]{2,1,0:T(8,128)}, s32[16]{0:T(128)S(1)}, s32[272,2048]{1,0:T(8,128)}, f32[272,2048]{1,0:T(8,128)}, /*index=5*/f32[27...) while((s32[]{:T(128)}, f32[16,128,512]{2,1,0:T(8,128)}, s32[16]{0:T(128)S(1)}, ...), condition=%wide.region_3.4_spmd.clone, body=%wide.region_0.3_spmd.clone.sunk | while | flops 89307144 | bytes 2565351 | solution.py:125
  82.5 1.1 subtract_multiply_fusion.2
  84.5 16.7 %fusion.27 = (f32[128,512]{1,0:T(8,128)S(1)}, f32[128,512]{1,0:T(8,128)S(1)}) fusion(f32[272,128]{1,0:T(8,128)S(1)} %get-tuple-element.170, s32[272,128]{1,0:T(8,128)S(1)} %constant_dynamic-slice_fusion.2, f32[272,128]{1,0:T(8,128)S(1)} %get-tuple-element.171), kind=kLoop, calls=%fused_computation.6.clone.1 | loop fusion | flops 88997888 | bytes 942080 | tf_op jit(solution)/shard_map/while/body/eval_jaxpr/reduce_sum | solution.py:119
  103.3 1.1 subtract_multiply_fusion.2
  105.3 16.7 %fusion.27 = (f32[128,512]{1,0:T(8,128)S(1)}, f32[128,512]{1,0:T(8,128)S(1)}) fusion(f32[272,128]{1,0:T(8,128)S(1)} %get-tuple-element.170, s32[272,128]{1,0:T(8,128)S(1)} %constant_dynamic-slice_fusion.2, f32[272,128]{1,0:T(8,128)S(1)} %get-tuple-element.171), kind=kLoop, calls=%fused_computation.6.clone.1 | loop fusion | flops 88997888 | bytes 942080 | tf_op jit(solution)/shard_map/while/body/eval_jaxpr/reduce_sum | solution.py:119
  124.2 1.1 subtract_multiply_fusion.2
  126.2 16.7 %fusion.27 = (f32[128,512]{1,0:T(8,128)S(1)}, f32[128,512]{1,0:T(8,128)S(1)}) fusion(f32[272,128]{1,0:T(8,128)S(1)} %get-tuple-element.170, s32[272,128]{1,0:T(8,128)S(1)} %constant_dynamic-slice_fusion.2, f32[272,128]{1,0:T(8,128)S(1)} %get-tuple-element.171), kind=kLoop, calls=%fused_computation.6.clone.1 | loop fusion | flops 88997888 | bytes 942080 | tf_op jit(solution)/shard_map/while/body/eval_jaxpr/reduce_sum | solution.py:119
  145.0 1.1 subtract_multiply_fusion.2
  147.0 16.7 %fusion.27 = (f32[128,512]{1,0:T(8,128)S(1)}, f32[128,512]{1,0:T(8,128)S(1)}) fusion(f32[272,128]{1,0:T(8,128)S(1)} %get-tuple-element.170, s32[272,128]{1,0:T(8,128)S(1)} %constant_dynamic-slice_fusion.2, f32[272,128]{1,0:T(8,128)S(1)} %get-tuple-element.171), kind=kLoop, calls=%fused_computation.6.clone.1 | loop fusion | flops 88997888 | bytes 942080 | tf_op jit(solution)/shard_map/while/body/eval_jaxpr/reduce_sum | solution.py:119
  167.9 16.7 %fusion.27 = (f32[128,512]{1,0:T(8,128)S(1)}, f32[128,512]{1,0:T(8,128)S(1)}) fusion(f32[272,128]{1,0:T(8,128)S(1)} %get-tuple-element.170, s32[272,128]{1,0:T(8,128)S(1)} %constant_dynamic-slice_fusion.2, f32[272,128]{1,0:T(8,128)S(1)} %get-tuple-element.171), kind=kLoop, calls=%fused_computation.6.clone.1 | loop fusion | flops 88997888 | bytes 942080 | tf_op jit(solution)/shard_map/while/body/eval_jaxpr/reduce_sum | solution.py:119
  188.7 16.7 %fusion.27 = (f32[128,512]{1,0:T(8,128)S(1)}, f32[128,512]{1,0:T(8,128)S(1)}) fusion(f32[272,128]{1,0:T(8,128)S(1)} %get-tuple-element.170, s32[272,128]{1,0:T(8,128)S(1)} %constant_dynamic-slice_fusion.2, f32[272,128]{1,0:T(8,128)S(1)} %get-tuple-element.171), kind=kLoop, calls=%fused_computation.6.clone.1 | loop fusion | flops 88997888 | bytes 942080 | tf_op jit(solution)/shard_map/while/body/eval_jaxpr/reduce_sum | solution.py:119
  209.5 16.7 %fusion.27 = (f32[128,512]{1,0:T(8,128)S(1)}, f32[128,512]{1,0:T(8,128)S(1)}) fusion(f32[272,128]{1,0:T(8,128)S(1)} %get-tuple-element.170, s32[272,128]{1,0:T(8,128)S(1)} %constant_dynamic-slice_fusion.2, f32[272,128]{1,0:T(8,128)S(1)} %get-tuple-element.171), kind=kLoop, calls=%fused_computation.6.clone.1 | loop fusion | flops 88997888 | bytes 942080 | tf_op jit(solution)/shard_map/while/body/eval_jaxpr/reduce_sum | solution.py:119
  230.4 16.7 %fusion.27 = (f32[128,512]{1,0:T(8,128)S(1)}, f32[128,512]{1,0:T(8,128)S(1)}) fusion(f32[272,128]{1,0:T(8,128)S(1)} %get-tuple-element.170, s32[272,128]{1,0:T(8,128)S(1)} %constant_dynamic-slice_fusion.2, f32[272,128]{1,0:T(8,128)S(1)} %get-tuple-element.171), kind=kLoop, calls=%fused_computation.6.clone.1 | loop fusion | flops 88997888 | bytes 942080 | tf_op jit(solution)/shard_map/while/body/eval_jaxpr/reduce_sum | solution.py:119
  251.2 16.7 %fusion.27 = (f32[128,512]{1,0:T(8,128)S(1)}, f32[128,512]{1,0:T(8,128)S(1)}) fusion(f32[272,128]{1,0:T(8,128)S(1)} %get-tuple-element.170, s32[272,128]{1,0:T(8,128)S(1)} %constant_dynamic-slice_fusion.2, f32[272,128]{1,0:T(8,128)S(1)} %get-tuple-element.171), kind=kLoop, calls=%fused_computation.6.clone.1 | loop fusion | flops 88997888 | bytes 942080 | tf_op jit(solution)/shard_map/while/body/eval_jaxpr/reduce_sum | solution.py:119
  272.0 16.7 %fusion.27 = (f32[128,512]{1,0:T(8,128)S(1)}, f32[128,512]{1,0:T(8,128)S(1)}) fusion(f32[272,128]{1,0:T(8,128)S(1)} %get-tuple-element.170, s32[272,128]{1,0:T(8,128)S(1)} %constant_dynamic-slice_fusion.2, f32[272,128]{1,0:T(8,128)S(1)} %get-tuple-element.171), kind=kLoop, calls=%fused_computation.6.clone.1 | loop fusion | flops 88997888 | bytes 942080 | tf_op jit(solution)/shard_map/while/body/eval_jaxpr/reduce_sum | solution.py:119
  292.9 16.7 %fusion.27 = (f32[128,512]{1,0:T(8,128)S(1)}, f32[128,512]{1,0:T(8,128)S(1)}) fusion(f32[272,128]{1,0:T(8,128)S(1)} %get-tuple-element.170, s32[272,128]{1,0:T(8,128)S(1)} %constant_dynamic-slice_fusion.2, f32[272,128]{1,0:T(8,128)S(1)} %get-tuple-element.171), kind=kLoop, calls=%fused_computation.6.clone.1 | loop fusion | flops 88997888 | bytes 942080 | tf_op jit(solution)/shard_map/while/body/eval_jaxpr/reduce_sum | solution.py:119
  313.7 16.7 %fusion.27 = (f32[128,512]{1,0:T(8,128)S(1)}, f32[128,512]{1,0:T(8,128)S(1)}) fusion(f32[272,128]{1,0:T(8,128)S(1)} %get-tuple-element.170, s32[272,128]{1,0:T(8,128)S(1)} %constant_dynamic-slice_fusion.2, f32[272,128]{1,0:T(8,128)S(1)} %get-tuple-element.171), kind=kLoop, calls=%fused_computation.6.clone.1 | loop fusion | flops 88997888 | bytes 942080 | tf_op jit(solution)/shard_map/while/body/eval_jaxpr/reduce_sum | solution.py:119
  334.5 16.7 %fusion.27 = (f32[128,512]{1,0:T(8,128)S(1)}, f32[128,512]{1,0:T(8,128)S(1)}) fusion(f32[272,128]{1,0:T(8,128)S(1)} %get-tuple-element.170, s32[272,128]{1,0:T(8,128)S(1)} %constant_dynamic-slice_fusion.2, f32[272,128]{1,0:T(8,128)S(1)} %get-tuple-element.171), kind=kLoop, calls=%fused_computation.6.clone.1 | loop fusion | flops 88997888 | bytes 942080 | tf_op jit(solution)/shard_map/while/body/eval_jaxpr/reduce_sum | solution.py:119
  355.4 16.7 %fusion.27 = (f32[128,512]{1,0:T(8,128)S(1)}, f32[128,512]{1,0:T(8,128)S(1)}) fusion(f32[272,128]{1,0:T(8,128)S(1)} %get-tuple-element.170, s32[272,128]{1,0:T(8,128)S(1)} %constant_dynamic-slice_fusion.2, f32[272,128]{1,0:T(8,128)S(1)} %get-tuple-element.171), kind=kLoop, calls=%fused_computation.6.clone.1 | loop fusion | flops 88997888 | bytes 942080 | tf_op jit(solution)/shard_map/while/body/eval_jaxpr/reduce_sum | solution.py:119
  376.2 16.7 %fusion.27 = (f32[128,512]{1,0:T(8,128)S(1)}, f32[128,512]{1,0:T(8,128)S(1)}) fusion(f32[272,128]{1,0:T(8,128)S(1)} %get-tuple-element.170, s32[272,128]{1,0:T(8,128)S(1)} %constant_dynamic-slice_fusion.2, f32[272,128]{1,0:T(8,128)S(1)} %get-tuple-element.171), kind=kLoop, calls=%fused_computation.6.clone.1 | loop fusion | flops 88997888 | bytes 942080 | tf_op jit(solution)/shard_map/while/body/eval_jaxpr/reduce_sum | solution.py:119
  397.0 16.7 %fusion.27 = (f32[128,512]{1,0:T(8,128)S(1)}, f32[128,512]{1,0:T(8,128)S(1)}) fusion(f32[272,128]{1,0:T(8,128)S(1)} %get-tuple-element.170, s32[272,128]{1,0:T(8,128)S(1)} %constant_dynamic-slice_fusion.2, f32[272,128]{1,0:T(8,128)S(1)} %get-tuple-element.171), kind=kLoop, calls=%fused_computation.6.clone.1 | loop fusion | flops 88997888 | bytes 942080 | tf_op jit(solution)/shard_map/while/body/eval_jaxpr/reduce_sum | solution.py:119
  414.6 642.9 %reduce-scatter.2.cloned.1.call-done = f32[16,512]{1,0:T(8,128)} async-done(((f32[2048,512]{1,0:T(8,128)}), f32[16,512]{1,0:T(8,128)}) %reduce-scatter.2.cloned.1.call-update) | async-done | bytes 32784 | tf_op jit(solution)/shard_map/reduce_scatter | solution.py:145
  (246 shorter events, 77.3 us)
Async XLA Ops:
  6.5 1051.0 %reduce-scatter.2.cloned.1.call-start = ((), (), s32[]{:S(2)}) async-start(), calls=%async_computation.1 | async-start | bytes 4227072 | tf_op jit(solution)/shard_map/reduce_scatter | solution.py:145
  7.9 63.1 %collective-permute-start = (f32[5,1,8,128]{3,2,1,0:T(8,128)}, f32[5,1,8,128]{3,2,1,0:T(8,128)}, u32[]{:S(2)}, u32[]{:S(2)}) collective-permute-start(f32[5,1,8,128]{3,2,1,0:T(8,128)} %get-tuple-element.100), channel_id=1, source_target_pairs={{0,16},{16,32},{32,48},{48,64},{64,80},{80,96},{96,112},{1,17},{17... | collective-permute-start | bytes 61448 | tf_op jit(solution)/shard_map/ppermute | solution.py:22
  9.8 62.0 %collective-permute-start.1 = (f32[5,1,8,128]{3,2,1,0:T(8,128)}, f32[5,1,8,128]{3,2,1,0:T(8,128)}, u32[]{:S(2)}, u32[]{:S(2)}) collective-permute-start(f32[5,1,8,128]{3,2,1,0:T(8,128)} %get-tuple-element.99), channel_id=1, source_target_pairs={{16,0},{32,16},{48,32},{64,48},{80,64},{96,80},{112,96},{17,1},{33... | collective-permute-start | bytes 61448 | tf_op jit(solution)/shard_map/ppermute | solution.py:23
  12.0 8.5 copy-start.12
  12.7 60.0 %collective-permute-start.2 = (f32[5,8,1,128]{3,1,2,0:T(8,128)}, f32[5,8,1,128]{3,1,2,0:T(8,128)}, u32[]{:S(2)}, u32[]{:S(2)}) collective-permute-start(f32[5,8,1,128]{3,1,2,0:T(8,128)} %get-tuple-element.106), channel_id=1, source_target_pairs={{0,1},{1,2},{2,3},{3,4},{4,5},{5,6},{6,7},{7,8},{8,9},{9,10},{10,1... | collective-permute-start | bytes 61448 | tf_op jit(solution)/shard_map/ppermute | solution.py:22
  15.2 59.2 %collective-permute-start.3 = (f32[5,8,1,128]{3,1,2,0:T(8,128)S(1)}, f32[5,8,1,128]{3,1,2,0:T(8,128)}, u32[]{:S(2)}, u32[]{:S(2)}) collective-permute-start(f32[5,8,1,128]{3,1,2,0:T(8,128)S(1)} %get-tuple-element.105), channel_id=1, source_target_pairs={{1,0},{2,1},{3,2},{4,3},{5,4},{6,5},{7,6},{8,7},{9,8},{10,9},{11,1... | collective-permute-start | bytes 61448 | tf_op jit(solution)/shard_map/ppermute | solution.py:23
  33.8 0.9 copy-start.23
  33.9 0.9 copy-start.24
  37.0 2.5 copy-start.25
  37.1 2.5 copy-start.1
  38.1 2.3 copy-start.3
  38.1 2.3 copy-start.4
  38.1 2.3 copy-start.13
  38.1 2.3 copy-start.14
  38.1 3.6 copy-start.2
  42.5 3.8 copy-start.11
  46.3 6.6 copy-start.16
  46.3 7.3 copy-start.15
  60.8 6.2 copy-start.27
  60.8 6.3 copy-start.26
  60.8 11.0 %copy-start = (f32[5,8,8,128]{3,2,1,0:T(8,128)S(1)}, f32[5,8,8,128]{3,2,1,0:T(8,128)}, u32[]{:S(2)}) copy-start(f32[5,8,8,128]{3,2,1,0:T(8,128)} %param.25) | copy-start | bytes 491524
  62.4 15.6 %copy-start.18 = (f32[5,8,2,128]{3,1,2,0:T(8,128)S(1)}, f32[5,8,2,128]{3,1,2,0:T(8,128)}, u32[]{:S(2)}) copy-start(f32[5,8,2,128]{3,1,2,0:T(8,128)} %get-tuple-element.126) | copy-start | bytes 122884
  62.4 15.6 %copy-start.17 = (f32[5,8,2,128]{3,1,2,0:T(8,128)S(1)}, f32[5,8,2,128]{3,1,2,0:T(8,128)}, u32[]{:S(2)}) copy-start(f32[5,8,2,128]{3,1,2,0:T(8,128)} %get-tuple-element.125) | copy-start | bytes 122884
  62.4 15.7 %copy-start.5 = (f32[5,8,8,128]{3,1,2,0:T(8,128)S(1)}, f32[5,8,8,128]{3,1,2,0:T(8,128)}, u32[]{:S(2)}) copy-start(f32[5,8,8,128]{3,1,2,0:T(8,128)} %copy.112) | copy-start | bytes 491524
  62.4 15.7 %copy-start.6 = (f32[5,8,8,128]{3,1,2,0:T(8,128)S(1)}, f32[5,8,8,128]{3,1,2,0:T(8,128)}, u32[]{:S(2)}) copy-start(f32[5,8,8,128]{3,1,2,0:T(8,128)} %copy.114) | copy-start | bytes 491524
  62.4 15.7 %copy-start.7 = (f32[5,8,8,128]{3,1,2,0:T(8,128)S(1)}, f32[5,8,8,128]{3,1,2,0:T(8,128)}, u32[]{:S(2)}) copy-start(f32[5,8,8,128]{3,1,2,0:T(8,128)} %copy.107) | copy-start | bytes 491524
  62.5 15.7 %copy-start.8 = (f32[5,8,8,128]{3,1,2,0:T(8,128)S(1)}, f32[5,8,8,128]{3,1,2,0:T(8,128)}, u32[]{:S(2)}) copy-start(f32[5,8,8,128]{3,1,2,0:T(8,128)} %copy.108) | copy-start | bytes 491524
  63.9 14.0 %copy-start.21 = (f32[5,2,8,128]{3,1,2,0:T(2,128)S(1)}, f32[5,2,8,128]{3,1,2,0:T(2,128)}, u32[]{:S(2)}) copy-start(f32[5,2,8,128]{3,1,2,0:T(2,128)} %copy.92) | copy-start | bytes 122884
  63.9 14.0 %copy-start.22 = (f32[5,2,8,128]{3,1,2,0:T(2,128)S(1)}, f32[5,2,8,128]{3,1,2,0:T(2,128)}, u32[]{:S(2)}) copy-start(f32[5,2,8,128]{3,1,2,0:T(2,128)} %copy.93) | copy-start | bytes 122884
  63.9 14.2 %copy-start.20 = (f32[5,8,2,128]{3,1,2,0:T(8,128)S(1)}, f32[5,8,2,128]{3,1,2,0:T(8,128)}, u32[]{:S(2)}) copy-start(f32[5,8,2,128]{3,1,2,0:T(8,128)} %get-tuple-element.124) | copy-start | bytes 122884
  63.9 14.2 %copy-start.19 = (f32[5,8,2,128]{3,1,2,0:T(8,128)S(1)}, f32[5,8,2,128]{3,1,2,0:T(8,128)}, u32[]{:S(2)}) copy-start(f32[5,8,2,128]{3,1,2,0:T(8,128)} %get-tuple-element.123) | copy-start | bytes 122884
  63.9 14.2 %copy-start.9 = (f32[5,8,8,128]{3,1,2,0:T(8,128)S(1)}, f32[5,8,8,128]{3,1,2,0:T(8,128)}, u32[]{:S(2)}) copy-start(f32[5,8,8,128]{3,1,2,0:T(8,128)} %copy.109) | copy-start | bytes 491524
  63.9 14.2 %copy-start.10 = (f32[5,8,8,128]{3,1,2,0:T(8,128)S(1)}, f32[5,8,8,128]{3,1,2,0:T(8,128)}, u32[]{:S(2)}) copy-start(f32[5,8,8,128]{3,1,2,0:T(8,128)} %copy.110) | copy-start | bytes 491524
Sparse Core Ops, SparseCore 0:
  414.8 642.7 reduce-scatter.1
where the time goes:
time: 1070 us; the launch traced here: 1060 us
  waiting for transfers between devices  643 us (60%)
  other arithmetic  302 us (28%)
  local copies, waits for them, and re-layouts  83 us (8%)
  between operations  15 us (1%)
  loops' own time  10.8 us (1%)
    reduce_scatter x1, waiting for transfers between devices, local(): lax.psum_scatter(partial_sums, ('ax', 'az'), scatter_dimension=0, tiled=T...  643 us
    reduce_sum x16, other arithmetic, one_block(): upper_sum = jnp.sum(jnp.where(hit, upper_weight[:, :, None], 0.0), axis=0)  267 us
    mul x40, local copies, waits for them, and re-layouts, fr_derivative(): jnp.asarray(table[:, j].reshape(bshape), jnp.float32) * column  24.9 us
  transfers between devices with their start and end apart: 5, of which 1 were waited for; matrix products, arithmetic and copies ran while one was open for 5% of the time, Pallas kernels for 0%

commit v1 on v0

v1 whole, which is shorter than its diff:
```python
import jax
import jax.numpy as jnp
import numpy as np
from jax import lax
from jax.experimental import pallas as pl
from jax.experimental.pallas import tpu as pltpu
from jax.sharding import Mesh
from jax.sharding import PartitionSpec as P

SLOTS = 272
LANES = 640
RADIX = 15
ROWS = 36
BLOCK = 128
SAMPLES = 512
CHIP = ("x", "y", "z")


def lobatto_matrix():
    points = np.array([-1.0, -1.0 / np.sqrt(5.0), 1.0 / np.sqrt(5.0), 1.0])
    table = np.zeros((4, 4))
    for i in range(4):
        for j in range(4):
            if i == j:
                table[i, j] = sum((1.0 / (points[i] - points[m]) for m in range(4) if m != i))
            else:
                a = np.prod([points[i] - points[m] for m in range(4) if m != i])
                b = np.prod([points[j] - points[m] for m in range(4) if m != j])
                table[i, j] = a / (b * (points[i] - points[j]))
    return table


def line_derivative(flux, value, speed):
    table = lobatto_matrix()
    out = []
    for start in (1, 5):
        def common(low):
            return 0.5 * (flux[low] + flux[low + 1]) - 0.5 * speed * (value[low + 1] - value[low])
        rows = [
            sum(np.float32(table[i, j]) * flux[start + j] for j in range(4)) for i in range(4)
        ]
        rows[3] = rows[3] + 6.0 * (common(start + 3) - flux[start + 3])
        rows[0] = rows[0] - 6.0 * (common(start - 1) - flux[start])
        out += rows
    return jnp.stack(out)


def surface_plane(state):
    at = 4 * (state.shape[3] // 8)
    near = state[3, :, :, at - 1 : at + 4] + state[4, :, :, at - 1 : at + 4]
    value = near[:, :, 1]
    along = 0.5 * value + state[1, :, :, at]
    across = state[2, :, :, at]

    def ends(flux, axes, size, wrap):
        up = [(i, (i + 1) % size) for i in range(size if wrap else size - 1)]
        down = [(j, i) for i, j in up]
        both = jnp.stack([flux, value], axis=0)
        before = lax.ppermute(both[:, 7], axes, up)
        after = lax.ppermute(both[:, 0], axes, down)
        return jnp.concatenate([before[:, None], both, after[:, None]], axis=1)

    both = ends(along, ("x", "core"), lax.axis_size("x") * lax.axis_size("core"), False)
    change = line_derivative(both[0], both[1], 1.5)
    value_t = value
    value = value.T
    both = ends(across.T, ("y", "z"), lax.axis_size("y") * lax.axis_size("z"), True)
    change = change + line_derivative(both[0], both[1], 1.0).T
    value = value_t
    table = lobatto_matrix()
    radial = sum(np.float32(table[0, j]) * near[:, :, 1 + j] for j in range(4))
    common = 0.5 * (near[:, :, 0] + value) - 0.5 * (value - near[:, :, 0])
    change = change + (radial - 6.0 * (common - value))
    return value - 0.05 * change


def slot_source(state, surf_index, surf_count):
    plane = surface_plane(state).reshape(-1)
    points = jnp.arange(64, dtype=jnp.int32)
    source = jnp.sum(jnp.where(surf_index[None, :] == points[:, None], plane[:, None], 0.0), axis=0)
    live = jnp.arange(SLOTS, dtype=jnp.int32) < surf_count[0, 0]
    return jnp.where(live, source, 0.0)


def bins_kernel(core_ref, src_ref, da_ref, fa_ref, db_ref, fb_ref, out_ref, d_t, f_t, hi_s, *, unroll=2):
    def flip(a_ref, b_ref, dst, cast):
        for n, (r, base) in enumerate(((a_ref, 0), (a_ref, 128), (b_ref, 0), (b_ref, 128))):
            dst[:, n * 128:(n + 1) * 128] = cast(r[base:base + 128, :]).T
        rest = jnp.concatenate([cast(a_ref[256:272, :]), cast(b_ref[256:272, :]), jnp.zeros((96, 128), jnp.float32)], axis=0)
        dst[:, 512:640] = rest.T
    flip(da_ref, db_ref, d_t, lambda v: v.astype(jnp.float32))
    flip(fa_ref, fb_ref, f_t, lambda v: v)
    src = src_ref[...]
    row16 = lax.broadcasted_iota(jnp.int32, (16, LANES), 0)
    half = (row16 >= 8).astype(jnp.float32)
    count_lo = row16.astype(jnp.float32).astype(jnp.bfloat16)
    count_up = (row16 + 16).astype(jnp.float32).astype(jnp.bfloat16)
    one = jnp.ones((16, LANES), jnp.bfloat16)
    zero = jnp.zeros((16, LANES), jnp.bfloat16)
    lane = lax.broadcasted_iota(jnp.int32, (32, 128), 1) & 7
    lane8 = lax.broadcasted_iota(jnp.int32, (8, 128), 1) & 7
    diag8 = lane8 == lax.broadcasted_iota(jnp.int32, (8, 128), 0)

    def group(g, slot):
        rows = pl.ds(pl.multiple_of(g * 8, 8), 8)
        k = d_t[rows, :]
        f = f_t[rows, :]
        c = src * (25.6 / (512.0 + k))
        up = f * c
        low = c - up
        hi = jnp.floor((k + 0.5) * (1.0 / 15.0))
        lo = k - 15.0 * hi
        hi_s[slot] = hi
        twice = lambda v: jnp.concatenate([v, v], axis=0)
        lo2 = (twice(lo) - half).astype(jnp.bfloat16)
        hi2 = (twice(hi) - half).astype(jnp.bfloat16)
        def parts(v):
            top = v.astype(jnp.bfloat16)
            rest = (v - top.astype(jnp.float32))
            return twice(v).astype(jnp.bfloat16), twice(rest).astype(jnp.bfloat16)
        low_a, low_b = parts(low)
        up_a, up_b = parts(up)
        wa, wb = [], []
        for j in range(0, 16, 2):
            at = lo2 == jnp.bfloat16(j)
            before = lo2 == jnp.bfloat16(j - 1)
            wa.append(jnp.where(at, low_a, jnp.where(before, up_a, zero)))
            wb.append(jnp.where(at, low_b, jnp.where(before, up_b, zero)))
        w = jnp.concatenate(wa + wb, axis=0)
        h = []
        for o in range(8):
            row = jnp.broadcast_to(hi_s[slot, o:o + 1, :], (16, LANES)).astype(jnp.bfloat16)
            h.append(jnp.where(row == count_lo, one, zero))
            h.append(jnp.where(row == count_up, one, zero))
        h.append(jnp.where(hi2 == jnp.bfloat16(32), one, zero))
        h.append(jnp.where(hi2 == jnp.bfloat16(34), one, zero))
        h = jnp.concatenate(h, axis=0)
        r = lax.dot_general(h, w, (((1,), (1,)), ((), ())), preferred_element_type=jnp.float32)
        r = r[:, :128] + r[:, 128:]
        main = r[0:32]
        for o in range(1, 8):
            main = jnp.where(lane == o, r[32 * o:32 * o + 32], main)
        extra = [jnp.sum(jnp.where(diag8, r[256 + 8 * e:264 + 8 * e], 0.0), axis=0, keepdims=True) for e in range(4)]
        return jnp.concatenate([main] + extra, axis=0)

    def pair(p, _):
        two = [group(2 * p + t, t) for t in range(2)]
        out_ref[p] = jnp.concatenate(two, axis=0)
        return 0
    lax.fori_loop(0, BLOCK // 16, pair, 0, unroll=False)

def bins(core, src, delay, frac, delay_b, frac_b, first, blocks):
    own = lambda n, c: (0, ((n + first) // 2) * 4 + c[0] * 2 + (n + first) % 2)
    sib = lambda n, c: (0, n + first)
    spec = pl.BlockSpec((SLOTS, BLOCK), own)
    spec_b = pl.BlockSpec((SLOTS, BLOCK), sib)
    return pl.pallas_call(
        bins_kernel,
        grid_spec=pltpu.PrefetchScalarGridSpec(
            num_scalar_prefetch=1, grid=(blocks,),
            in_specs=[pl.BlockSpec((1, LANES), lambda n, c: (0, 0)), spec, spec, spec_b, spec_b],
            out_specs=pl.BlockSpec((8, 2 * ROWS, 128), lambda n, c: (n, 0, 0)),
            scratch_shapes=[pltpu.VMEM((BLOCK, LANES), jnp.float32), pltpu.VMEM((BLOCK, LANES), jnp.float32), pltpu.VMEM((2, 8, LANES), jnp.float32)],
        ),
        out_shape=jax.ShapeDtypeStruct((8 * blocks, 2 * ROWS, 128), jnp.float32),
        compiler_params=pltpu.CompilerParams(vmem_limit_bytes=48 * 1024 * 1024),
        name="bins",
    )(core, src, delay, frac, delay_b, frac_b)


def local(state, surf_index, surf_count, delay, fraction):
    core = lax.axis_index("core")
    swap = [(0, 1), (1, 0)]

    def other_half(rows):
        halves = rows.reshape(SLOTS, 4, 2, 256)
        return lax.dynamic_index_in_dim(halves, 1 - core, 2, keepdims=False).reshape(SLOTS, 1024)

    delay_b = lax.ppermute(other_half(delay), "core", swap)
    fraction_b = lax.ppermute(other_half(fraction), "core", swap)
    source = slot_source(state, surf_index, surf_count)
    source_b = lax.ppermute(source, "core", swap)
    source = jnp.concatenate(
        [source[:256], source_b[:256], source[256:], source_b[256:], jnp.zeros((96,), jnp.float32)]
    )
    sums = bins(core.reshape(1), source[None, :], delay, fraction, delay_b, fraction_b, 0, 8)
    parts = lax.all_to_all(sums, CHIP, 0, 0, tiled=True)
    total = jnp.sum(parts, axis=0)
    total = total.reshape(2, ROWS, 16, 8).transpose(0, 3, 1, 2).reshape(16, ROWS, 16)
    carry = jnp.pad(total[:, :34, 15:], ((0, 0), (1, 0), (0, 14)))
    return (total[:, :35, :RADIX] + carry).reshape(16, 35 * RADIX)[:, :SAMPLES]


def solution(mesh):
    fine = Mesh(mesh.devices.reshape(4, 2, 4, 4), ("x", "core", "y", "z"))
    ax, az = ("x", "core"), ("y", "z")
    placed = (
        P(None, ax, az, None),
        P(ax + az),
        P(ax, az),
        P(ax + az, None),
        P(ax + az, None),
    )
    return jax.shard_map(
        local, mesh=fine, in_specs=placed, out_specs=P(ax + az, None), check_vma=False
    )
```

time: 1070 us -> 130 us (0.12)
  waiting for transfers between devices: 643 us -> 0.89 us
  other arithmetic: 302 us -> 2.05 us
  local copies, waits for them, and re-layouts: 83 us -> 36.1 us
  blocking collectives: 0 us -> 43.2 us
  Pallas kernels: 0 us -> 33.9 us
  between operations: 15 us -> 0.92 us
  loops' own time: 10.8 us -> 0 us
    reduce_scatter x1 -> x0, waiting for transfers between devices: 643 us -> none  [local(): lax.psum_scatter(partial_sums, ('ax', 'az'), scatter_dimension=0, tiled=T...]
    reduce_sum x16 -> x2, other arithmetic: 267 us -> 0.93 us  [the longest x1 0.78 us: slot_source(): jnp.sum(jnp.where(surf_index[None, :] == points[:, None], plane[:, None],...]
    all_to_all x0 -> x1, blocking collectives: none -> 43.2 us  [local(): parts = lax.all_to_all(sums, CHIP, 0, 0, tiled=True)]
    pallas_call x0 -> x1, Pallas kernels: none -> 33.9 us  [bins(): pl.pallas_call(bins_kernel, grid_spec=pltpu.PrefetchScalarGridSpec(num_sc...]
    mul x56 -> x34, local copies, waits for them, and re-layouts: 30.7 us -> 10.7 us  [the longest x32 10.5 us: line_derivative(): np.float32(table[i, j]) * flux[start + j]]
    mul x16 -> x2, other arithmetic: 17.4 us -> 0.63 us  [line_derivative(): np.float32(table[i, j]) * flux[start + j]]
    dynamic_slice x32 -> x2, local copies, waits for them, and re-layouts: 24.1 us -> 8.55 us  [other_half(): lax.dynamic_index_in_dim(halves, 1 - core, 2, keepdims=False)]
    dynamic_update_slice x16 -> x0, other arithmetic: 13.7 us -> none  [accumulate(): stacked = lax.map(one_block, jnp.arange(count_blocks, dtype=jnp.int32))]
  transfers between devices with their start and end apart: 5 -> 7, of which waited for: 1 -> 2; matrix products, arithmetic and copies ran while one was open for 5% -> 26% of each run, Pallas kernels for 0% -> 0%
where the time goes in v1:
time: 130 us; the launch traced here: 129 us
  blocking collectives  43.2 us (33%)
  local copies, waits for them, and re-layouts  36.1 us (28%)
  Pallas kernels  33.9 us (26%)
  starting transfers between devices  12.3 us (9%)
  other arithmetic  2.05 us (2%)
    all_to_all x1, blocking collectives, local(): parts = lax.all_to_all(sums, CHIP, 0, 0, tiled=True)  43.2 us
    pallas_call x1, Pallas kernels, bins(): pl.pallas_call(bins_kernel, grid_spec=pltpu.PrefetchScalarGridSpec(num_sc...  33.9 us
    mul x32, local copies, waits for them, and re-layouts, line_derivative(): np.float32(table[i, j]) * flux[start + j]  10.5 us
    dynamic_slice x2, local copies, waits for them, and re-layouts, other_half(): lax.dynamic_index_in_dim(halves, 1 - core, 2, keepdims=False)  8.55 us
    ppermute x2, starting transfers between devices, ends(): after = lax.ppermute(both[:, 0], axes, down)  7.85 us
    reshape x2, local copies, waits for them, and re-layouts, other_half(): halves = rows.reshape(SLOTS, 4, 2, 256)  6.1 us
    ppermute x2, starting transfers between devices, ends(): before = lax.ppermute(both[:, 7], axes, up)  3.02 us
    unnamed x25, local copies, waits for them, and re-layouts  2.85 us
  transfers between devices with their start and end apart: 7, of which 2 were waited for; matrix products, arithmetic and copies ran while one was open for 26% of the time, Pallas kernels for 0%

profile of v1, /device:TPU:0, one launch (start us, length us, event | category | flops | bytes accessed | tf_op | source)
XLA Modules:
  0.0 129.3 jit_solution(4308035096831146803)
XLA Ops:
  0.0 0.8 fusion.16
  0.9 0.9 fusion.15
  1.7 0.1 copy.510
  1.8 0.1 copy.509
  2.0 0.1 copy.511
  2.1 0.7 copy.451
  2.8 1.3 collective-permute-start.1
  4.1 0.1 copy.414
  4.2 3.0 %collective-permute-start = (f32[2,8]{0,1:T(8,128)S(1)}, f32[2,8]{0,1:T(8,128)S(1)}, u32[]{:S(2)}, u32[]{:S(2)}) collective-permute-start(f32[2,8]{0,1:T(8,128)S(1)} %copy.414), channel_id=1, source_target_pairs={{0,16},{16,32},{32,48},{48,64},{64,80},{80,96},{96,112},{1,17},{17... | collective-permute-start | bytes 200 | tf_op jit(solution)/shard_map/ppermute | solution.py:59
  7.3 0.1 copy.515
  7.4 0.7 copy.499
  8.1 6.6 %collective-permute-start.3 = (f32[2,8]{0,1:T(8,128)}, f32[2,8]{0,1:T(8,128)S(1)}, u32[]{:S(2)}, u32[]{:S(2)}) collective-permute-start(f32[2,8]{0,1:T(8,128)} %copy.499), channel_id=1, source_target_pairs={{1,0},{2,1},{3,2},{4,3},{5,4},{6,5},{7,6},{8,7},{9,8},{10,9},{11,1... | collective-permute-start | bytes 200 | tf_op jit(solution)/shard_map/ppermute | solution.py:60
  14.7 0.7 copy.462
  15.3 3.2 %reshape.1176 = s32[272,4,2,256]{3,2,1,0:T(2,128)S(1)} reshape(s32[272,2048]{1,0:T(8,128)} %da_ref.1) | data formatting | bytes 4456448 | tf_op jit(solution)/shard_map/reshape | solution.py:176
  18.5 3.4 %dynamic-slice_reduce_fusion.1 = s32[272,4,256]{2,1,0:T(4,128)S(1)} fusion(s32[272,4,2,256]{3,2,1,0:T(2,128)S(1)} %reshape.1176, s32[]{:T(128)S(6)} %select_n.16), kind=kLoop, calls=%fused_computation.1 | loop fusion | bytes 2228228 | tf_op jit(solution)/shard_map/jit(dynamic_index_in_dim)/dynamic_slice | solution.py:177
  22.0 1.2 copy.516
  23.2 0.8 collective-permute-start.5
  24.1 0.6 multiply_bitcast_fusion.18
  26.0 0.7 copy.448
  26.7 0.7 copy.437
  27.7 0.7 copy.427
  28.4 1.3 %copy.420 = f32[1,8]{0,1:T(8,128)} copy(f32[1,8]{1,0:T(1,128)} %get-tuple-element.57) | data formatting | bytes 64 | tf_op jit(solution)/shard_map/mul | solution.py:40
  29.7 1.3 %copy.424 = f32[1,8]{0,1:T(8,128)} copy(f32[1,8]{1,0:T(1,128)} %get-tuple-element.58) | data formatting | bytes 64 | tf_op jit(solution)/shard_map/mul | solution.py:40
  31.1 0.7 copy.428
  32.1 0.7 copy.449
  32.8 1.2 copy.436
  34.1 0.7 copy.435
  34.7 0.7 copy.413
  35.4 0.7 copy.412
  36.1 0.7 copy.411
  38.3 2.9 %reshape.1178 = f32[272,4,2,256]{3,2,1,0:T(2,128)} reshape(f32[272,2048]{1,0:T(8,128)S(1)} %copy-done.1) | data formatting | bytes 4456448 | tf_op jit(solution)/shard_map/reshape | solution.py:176
  41.2 5.1 %dynamic-slice_reduce_fusion = f32[272,4,256]{2,1,0:T(4,128)S(1)} fusion(f32[272,4,2,256]{3,2,1,0:T(2,128)} %reshape.1178, s32[]{:T(128)S(6)} %select_n.16), kind=kLoop, calls=%fused_computation | loop fusion | bytes 2228228 | tf_op jit(solution)/shard_map/jit(dynamic_index_in_dim)/dynamic_slice | solution.py:177
  46.3 1.2 copy.517
  47.6 0.1 multiply_subtract_fusion.3
  47.9 0.1 multiply_add_fusion
  48.1 0.1 multiply_subtract_fusion
  48.3 0.8 select_reduce_fusion
  49.1 0.6 collective-permute-start.4
  49.7 0.8 collective-permute-done.4
  50.7 33.9 %bins.1 = f32[64,72,128]{2,1,0:T(8,128)} custom-call(s32[1]{0:T(128)} %bitcast.core_ref, f32[1,640]{1,0:T(1,128)S(1)} %broadcast_in_dim.35.src_ref, s32[272,2048]{1,0:T(8,128)S(1)} %copy-done, f32[272,2048]{1,0:T(8,128)} %fa_ref.1, s32[272,1024]{1,0:T(8,128)S(1)} %collective-permute-done.5.db_ref, f32[272,1024]{1,0:T(8,128)} %collective-permute-done.6.fb_ref), custom_call_target="tpu_custom_call" | custom-call | tf_op jit(solution)/shard_map/bins/pallas_call | solution.py:157
  84.6 43.2 %all_to_all.5 = f32[64,72,128]{2,1,0:T(8,128)S(1)} all-to-all(f32[64,72,128]{2,1,0:T(8,128)} %bins.1), channel_id=1, replica_groups=mesh['x'=4,'core'=2,'y'=4,'z'=4] {'x','y','z'}, dimensions={0} | all-to-all | bytes 4718592 | tf_op jit(solution)/shard_map/all_to_all | solution.py:187
  127.7 0.1 reduce_sum.19
  127.9 0.1 copy.506
  128.0 0.1 reshape.1180
  128.2 0.1 slice_add_fusion
  128.3 0.2 copy.508
  128.5 0.1 reshape.1182
  128.6 0.6 slice.421
  (89 shorter events, 3.6 us)
Async XLA Ops:
  2.8 44.9 %collective-permute-start.1 = (f32[2,8]{0,1:T(8,128)}, f32[2,8]{0,1:T(8,128)S(1)}, u32[]{:S(2)}, u32[]{:S(2)}) collective-permute-start(f32[2,8]{0,1:T(8,128)} %copy.451), channel_id=1, source_target_pairs={{16,0},{32,16},{48,32},{64,48},{80,64},{96,80},{112,96},{17,1},{33... | collective-permute-start | bytes 200 | tf_op jit(solution)/shard_map/ppermute | solution.py:60
  4.2 43.4 %collective-permute-start = (f32[2,8]{0,1:T(8,128)S(1)}, f32[2,8]{0,1:T(8,128)S(1)}, u32[]{:S(2)}, u32[]{:S(2)}) collective-permute-start(f32[2,8]{0,1:T(8,128)S(1)} %copy.414), channel_id=1, source_target_pairs={{0,16},{16,32},{32,48},{48,64},{64,80},{80,96},{96,112},{1,17},{17... | collective-permute-start | bytes 200 | tf_op jit(solution)/shard_map/ppermute | solution.py:59
  8.1 39.8 %collective-permute-start.3 = (f32[2,8]{0,1:T(8,128)}, f32[2,8]{0,1:T(8,128)S(1)}, u32[]{:S(2)}, u32[]{:S(2)}) collective-permute-start(f32[2,8]{0,1:T(8,128)} %copy.499), channel_id=1, source_target_pairs={{1,0},{2,1},{3,2},{4,3},{5,4},{6,5},{7,6},{8,7},{9,8},{10,9},{11,1... | collective-permute-start | bytes 200 | tf_op jit(solution)/shard_map/ppermute | solution.py:60
  15.3 32.7 %collective-permute-start.2 = (f32[2,8]{0,1:T(8,128)}, f32[2,8]{0,1:T(8,128)S(1)}, u32[]{:S(2)}, u32[]{:S(2)}) collective-permute-start(f32[2,8]{0,1:T(8,128)} %copy.462), channel_id=1, source_target_pairs={{0,1},{1,2},{2,3},{3,4},{4,5},{5,6},{6,7},{7,8},{8,9},{9,10},{10,1... | collective-permute-start | bytes 200 | tf_op jit(solution)/shard_map/ppermute | solution.py:59
  22.0 16.3 %copy-start.1 = (f32[272,2048]{1,0:T(8,128)S(1)}, f32[272,2048]{1,0:T(8,128)}, u32[]{:S(2)}) copy-start(f32[272,2048]{1,0:T(8,128)} %fa_ref.1) | copy-start | bytes 6684676
  23.2 27.4 %collective-permute-start.5 = (s32[272,1024]{1,0:T(8,128)}, s32[272,1024]{1,0:T(8,128)S(1)}, u32[]{:S(2)}, u32[]{:S(2)}) collective-permute-start(s32[272,1024]{1,0:T(8,128)} %bitcast.73), channel_id=1, source_target_pairs={{0,16},{16,0},{1,17},{17,1},{2,18},{18,2},{3,19},{19,3},{4,20},{20... | collective-permute-start | bytes 3342344 | tf_op jit(solution)/shard_map/ppermute | solution.py:179
  41.2 6.4 %copy-start.2 = (f32[1,8]{0,1:T(8,128)S(1)}, f32[1,8]{0,1:T(8,128)}, u32[]{:S(2)}) copy-start(f32[1,8]{0,1:T(8,128)} %copy.420) | copy-start | bytes 100
  41.2 6.4 %copy-start.3 = (f32[1,8]{0,1:T(8,128)S(1)}, f32[1,8]{0,1:T(8,128)}, u32[]{:S(2)}) copy-start(f32[1,8]{0,1:T(8,128)} %copy.424) | copy-start | bytes 100
  41.2 6.4 %copy-start.4 = (f32[1,8]{0,1:T(8,128)S(1)}, f32[1,8]{0,1:T(8,128)}, u32[]{:S(2)}) copy-start(f32[1,8]{0,1:T(8,128)} %copy.428) | copy-start | bytes 100
  41.2 6.4 %copy-start.5 = (f32[1,8]{0,1:T(8,128)S(1)}, f32[1,8]{0,1:T(8,128)}, u32[]{:S(2)}) copy-start(f32[1,8]{0,1:T(8,128)} %copy.436) | copy-start | bytes 100
  41.2 6.4 %copy-start.6 = (f32[1,8]{0,1:T(8,128)S(1)}, f32[1,8]{0,1:T(8,128)}, u32[]{:S(2)}) copy-start(f32[1,8]{0,1:T(8,128)} %copy.435) | copy-start | bytes 100
  41.2 6.4 %copy-start.7 = (f32[1,8]{0,1:T(8,128)S(1)}, f32[1,8]{0,1:T(8,128)}, u32[]{:S(2)}) copy-start(f32[1,8]{0,1:T(8,128)} %copy.413) | copy-start | bytes 100
  41.2 6.4 %copy-start.8 = (f32[1,8]{0,1:T(8,128)S(1)}, f32[1,8]{0,1:T(8,128)}, u32[]{:S(2)}) copy-start(f32[1,8]{0,1:T(8,128)} %copy.412) | copy-start | bytes 100
  41.2 6.4 %copy-start.9 = (f32[1,8]{0,1:T(8,128)S(1)}, f32[1,8]{0,1:T(8,128)}, u32[]{:S(2)}) copy-start(f32[1,8]{0,1:T(8,128)} %copy.411) | copy-start | bytes 100
  46.3 4.3 %copy-start = (s32[272,2048]{1,0:T(8,128)S(1)}, s32[272,2048]{1,0:T(8,128)}, u32[]{:S(2)}) copy-start(s32[272,2048]{1,0:T(8,128)} %da_ref.1) | copy-start | bytes 6684676
  47.6 3.1 %collective-permute-start.6 = (f32[272,1024]{1,0:T(8,128)}, f32[272,1024]{1,0:T(8,128)}, u32[]{:S(2)}, u32[]{:S(2)}) collective-permute-start(f32[272,1024]{1,0:T(8,128)} %bitcast.75), channel_id=1, source_target_pairs={{0,16},{16,0},{1,17},{17,1},{2,18},{18,2},{3,19},{19,3},{4,20},{20... | collective-permute-start | bytes 3342344 | tf_op jit(solution)/shard_map/ppermute | solution.py:180
  49.1 1.4 %collective-permute-start.4 = (f32[272]{0:T(512)S(1)}, f32[272]{0:T(512)S(1)}, u32[]{:S(2)}, u32[]{:S(2)}) collective-permute-start(f32[272]{0:T(512)S(1)} %fusion.14), channel_id=1, source_target_pairs={{0,16},{16,0},{1,17},{17,1},{2,18},{18,2},{3,19},{19,3},{4,20},{20... | collective-permute-start | bytes 3272 | tf_op jit(solution)/shard_map/ppermute | solution.py:182

commit v2 on v1

--- a/solution.py
+++ b/solution.py
@@ -14,6 +14,10 @@
 BLOCK = 128
 SAMPLES = 512
 CHIP = ("x", "y", "z")
+AXIAL = ("x", "core")
+AZIMUTHAL = ("y", "z")
+MEAN_FLOW = 0.5
+TIME_STEP = 0.05
 
 
 def lobatto_matrix():
@@ -30,59 +34,143 @@
     return table
 
 
-def line_derivative(flux, value, speed):
+def line_operators():
     table = lobatto_matrix()
-    out = []
-    for start in (1, 5):
-        def common(low):
-            return 0.5 * (flux[low] + flux[low + 1]) - 0.5 * speed * (value[low + 1] - value[low])
-        rows = [
-            sum(np.float32(table[i, j]) * flux[start + j] for j in range(4)) for i in range(4)
-        ]
-        rows[3] = rows[3] + 6.0 * (common(start + 3) - flux[start + 3])
-        rows[0] = rows[0] - 6.0 * (common(start - 1) - flux[start])
-        out += rows
-    return jnp.stack(out)
-
-
-def surface_plane(state):
-    at = 4 * (state.shape[3] // 8)
-    near = state[3, :, :, at - 1 : at + 4] + state[4, :, :, at - 1 : at + 4]
-    value = near[:, :, 1]
-    along = 0.5 * value + state[1, :, :, at]
-    across = state[2, :, :, at]
-
-    def ends(flux, axes, size, wrap):
+
+    def derivative(flux, value, speed):
+        out = np.zeros((8,) + flux.shape[1:])
+        for start in (1, 5):
+            def common(low):
+                mean = 0.5 * (flux[low] + flux[low + 1])
+                return mean - 0.5 * speed * (value[low + 1] - value[low])
+            for i in range(4):
+                out[start - 1 + i] = sum(table[i, j] * flux[start + j] for j in range(4))
+            out[start + 2] += 6.0 * (common(start + 3) - flux[start + 3])
+            out[start - 1] -= 6.0 * (common(start - 1) - flux[start])
+        return out
+
+    def maps(along_axial):
+        result = []
+        for place in range(3):
+            unit = np.zeros((24, 8, 128))
+            for point in range(64):
+                line, other = (point // 8, point % 8) if along_axial else (point % 8, point // 8)
+                unit[place * 8 + line, other, point] = 1.0
+            value = unit[7:17]
+            speed_of = np.zeros((24, 8, 128))
+            for point in range(64):
+                line, other = (point // 8, point % 8) if along_axial else (point % 8, point // 8)
+                speed_of[place * 8 + line, other, 64 + point] = 1.0
+            velocity = speed_of[7:17]
+            if along_axial:
+                change = derivative(MEAN_FLOW * value + velocity, value, 1.5)
+            else:
+                change = np.swapaxes(derivative(velocity, value, 1.0), 0, 1)
+            result.append(-TIME_STEP * change.reshape(64, 128).T)
+        return result
+
+    before_x, own_x, after_x = maps(True)
+    before_y, own_y, after_y = maps(False)
+    eye = np.eye(64)
+    own_x[:64] += eye
+    own_x[:64] -= TIME_STEP * (table[0, 0] - 6.0 * (0.5 - 0.5 - 1.0)) * eye
+    low = -TIME_STEP * -6.0 * (0.5 + 0.5) * eye
+    near_a = np.concatenate([low, -TIME_STEP * table[0, 1] * eye])
+    near_b = np.concatenate([-TIME_STEP * table[0, 2] * eye, -TIME_STEP * table[0, 3] * eye])
+    every = [own_x, own_y, near_a, near_b, before_x, after_x, before_y, after_y]
+    return np.concatenate(every).astype(np.float32)
+
+
+def tile_kernel(state_ref, tile_ref):
+    at = 4 * (state_ref.shape[2] // 8)
+    pick = lax.broadcasted_iota(jnp.int32, (8, 128), 1) == (
+        lax.broadcasted_iota(jnp.int32, (8, 128), 0) + (at - 1)
+    )
+    pick = pick.astype(jnp.float32)
+
+    def points(field):
+        return lax.dot_general(
+            pick, field, (((1,), (1,)), ((), ())),
+            precision=lax.Precision.HIGHEST, preferred_element_type=jnp.float32,
+        )
+
+    value = points(state_ref[3] + state_ref[4])
+    axial = points(state_ref[1])
+    azimuthal = points(state_ref[2])
+    rows = [
+        jnp.concatenate([value[1:2], axial[1:2]], axis=1),
+        jnp.concatenate([value[1:2], azimuthal[1:2]], axis=1),
+        jnp.concatenate([value[0:1], value[2:3]], axis=1),
+        jnp.concatenate([value[3:4], value[4:5]], axis=1),
+        jnp.zeros((4, 128), jnp.float32),
+    ]
+    tile_ref[...] = jnp.concatenate(rows, axis=0)
+
+
+def source_kernel(map_ref, own_ref, bx_ref, ax_ref, by_ref, ay_ref, index_ref, count_ref, source_ref):
+    rows = [own_ref[0:1], own_ref[1:2], own_ref[2:3], own_ref[3:4],
+            bx_ref[0:1], ax_ref[0:1], by_ref[1:2], ay_ref[1:2]]
+    exact = dict(precision=lax.Precision.HIGHEST, preferred_element_type=jnp.float32)
+    plane = jnp.dot(jnp.concatenate(rows, axis=1), map_ref[...], **exact)
+    points = lax.broadcasted_iota(jnp.int32, (64, SLOTS), 0)
+    hit = (index_ref[...] == points).astype(jnp.float32)
+    source = jnp.dot(plane, hit, **exact)
+    live = lax.broadcasted_iota(jnp.int32, (1, SLOTS), 1) < count_ref[0, 0]
+    source_ref[...] = jnp.where(live, source, 0.0)
+
+
+def slot_source(state, surf_index, surf_count):
+    vmem = pl.BlockSpec(memory_space=pltpu.VMEM)
+    tile = pl.pallas_call(
+        tile_kernel,
+        in_specs=[vmem],
+        out_specs=vmem,
+        out_shape=jax.ShapeDtypeStruct((8, 128), jnp.float32),
+        name="tile",
+    )(state.reshape(5, 64, state.shape[3]))
+
+    def around(axes, size, wrap):
         up = [(i, (i + 1) % size) for i in range(size if wrap else size - 1)]
         down = [(j, i) for i, j in up]
-        both = jnp.stack([flux, value], axis=0)
-        before = lax.ppermute(both[:, 7], axes, up)
-        after = lax.ppermute(both[:, 0], axes, down)
-        return jnp.concatenate([before[:, None], both, after[:, None]], axis=1)
-
-    both = ends(along, ("x", "core"), lax.axis_size("x") * lax.axis_size("core"), False)
-    change = line_derivative(both[0], both[1], 1.5)
-    value_t = value
-    value = value.T
-    both = ends(across.T, ("y", "z"), lax.axis_size("y") * lax.axis_size("z"), True)
-    change = change + line_derivative(both[0], both[1], 1.0).T
-    value = value_t
-    table = lobatto_matrix()
-    radial = sum(np.float32(table[0, j]) * near[:, :, 1 + j] for j in range(4))
-    common = 0.5 * (near[:, :, 0] + value) - 0.5 * (value - near[:, :, 0])
-    change = change + (radial - 6.0 * (common - value))
-    return value - 0.05 * change
-
-
-def slot_source(state, surf_index, surf_count):
-    plane = surface_plane(state).reshape(-1)
-    points = jnp.arange(64, dtype=jnp.int32)
-    source = jnp.sum(jnp.where(surf_index[None, :] == points[:, None], plane[:, None], 0.0), axis=0)
-    live = jnp.arange(SLOTS, dtype=jnp.int32) < surf_count[0, 0]
-    return jnp.where(live, source, 0.0)
-
-
-def bins_kernel(core_ref, src_ref, da_ref, fa_ref, db_ref, fb_ref, out_ref, d_t, f_t, hi_s, *, unroll=2):
+        return lax.ppermute(tile, axes, up), lax.ppermute(tile, axes, down)
+
+    before_x, after_x = around(AXIAL, lax.axis_size(AXIAL), False)
+    before_y, after_y = around(AZIMUTHAL, lax.axis_size(AZIMUTHAL), True)
+    return pl.pallas_call(
+        source_kernel,
+        in_specs=[vmem] * 7 + [pl.BlockSpec(memory_space=pltpu.SMEM)],
+        out_specs=vmem,
+        out_shape=jax.ShapeDtypeStruct((1, SLOTS), jnp.float32),
+        name="source",
+    )(
+        jnp.asarray(line_operators()), tile, before_x, after_x, before_y, after_y,
+        surf_index.reshape(1, SLOTS), surf_count,
+    )
+
+
+def half_kernel(core_ref, delay_ref, fraction_ref, delay_out, fraction_out):
+    delay_out[...] = delay_ref[...]
+    fraction_out[...] = fraction_ref[...]
+
+
+def other_half(core, delay, fraction):
+    width = delay.shape[1] // 8
+    taken = pl.BlockSpec((SLOTS, width), lambda n, c: (0, 2 * n + 1 - c[0]))
+    given = pl.BlockSpec((SLOTS, width), lambda n, c: (0, n))
+    return pl.pallas_call(
+        half_kernel,
+        grid_spec=pltpu.PrefetchScalarGridSpec(
+            num_scalar_prefetch=1, grid=(4,), in_specs=[taken] * 2, out_specs=[given] * 2
+        ),
+        out_shape=[
+            jax.ShapeDtypeStruct((SLOTS, 4 * width), jnp.int32),
+            jax.ShapeDtypeStruct((SLOTS, 4 * width), jnp.float32),
+        ],
+        name="other_half",
+    )(core, delay, fraction)
+
+
+def bins_kernel(core_ref, src_ref, src_b_ref, da_ref, fa_ref, db_ref, fb_ref, out_ref, d_t, f_t, hi_s, *, unroll=2):
     def flip(a_ref, b_ref, dst, cast):
         for n, (r, base) in enumerate(((a_ref, 0), (a_ref, 128), (b_ref, 0), (b_ref, 128))):
             dst[:, n * 128:(n + 1) * 128] = cast(r[base:base + 128, :]).T
@@ -90,7 +178,9 @@
         dst[:, 512:640] = rest.T
     flip(da_ref, db_ref, d_t, lambda v: v.astype(jnp.float32))
     flip(fa_ref, fb_ref, f_t, lambda v: v)
-    src = src_ref[...]
+    src = jnp.concatenate(
+        [src_ref[:, :256], src_b_ref[:, :256], src_ref[:, 256:], src_b_ref[:, 256:],
+         jnp.zeros((1, 96), jnp.float32)], axis=1)
     row16 = lax.broadcasted_iota(jnp.int32, (16, LANES), 0)
     half = (row16 >= 8).astype(jnp.float32)
     count_lo = row16.astype(jnp.float32).astype(jnp.bfloat16)
@@ -149,7 +239,7 @@
         return 0
     lax.fori_loop(0, BLOCK // 16, pair, 0, unroll=False)
 
-def bins(core, src, delay, frac, delay_b, frac_b, first, blocks):
+def bins(core, src, src_b, delay, frac, delay_b, frac_b, first, blocks):
     own = lambda n, c: (0, ((n + first) // 2) * 4 + c[0] * 2 + (n + first) % 2)
     sib = lambda n, c: (0, n + first)
     spec = pl.BlockSpec((SLOTS, BLOCK), own)
@@ -158,32 +248,25 @@
         bins_kernel,
         grid_spec=pltpu.PrefetchScalarGridSpec(
             num_scalar_prefetch=1, grid=(blocks,),
-            in_specs=[pl.BlockSpec((1, LANES), lambda n, c: (0, 0)), spec, spec, spec_b, spec_b],
+            in_specs=[pl.BlockSpec((1, SLOTS), lambda n, c: (0, 0))] * 2 + [spec, spec, spec_b, spec_b],
             out_specs=pl.BlockSpec((8, 2 * ROWS, 128), lambda n, c: (n, 0, 0)),
             scratch_shapes=[pltpu.VMEM((BLOCK, LANES), jnp.float32), pltpu.VMEM((BLOCK, LANES), jnp.float32), pltpu.VMEM((2, 8, LANES), jnp.float32)],
         ),
         out_shape=jax.ShapeDtypeStruct((8 * blocks, 2 * ROWS, 128), jnp.float32),
         compiler_params=pltpu.CompilerParams(vmem_limit_bytes=48 * 1024 * 1024),
         name="bins",
-    )(core, src, delay, frac, delay_b, frac_b)
+    )(core, src, src_b, delay, frac, delay_b, frac_b)
 
 
 def local(state, surf_index, surf_count, delay, fraction):
-    core = lax.axis_index("core")
+    core = lax.axis_index("core").reshape(1)
     swap = [(0, 1), (1, 0)]
-
-    def other_half(rows):
-        halves = rows.reshape(SLOTS, 4, 2, 256)
-        return lax.dynamic_index_in_dim(halves, 1 - core, 2, keepdims=False).reshape(SLOTS, 1024)
-
-    delay_b = lax.ppermute(other_half(delay), "core", swap)
-    fraction_b = lax.ppermute(other_half(fraction), "core", swap)
+    delay_b, fraction_b = other_half(core, delay, fraction)
+    delay_b = lax.ppermute(delay_b, "core", swap)
+    fraction_b = lax.ppermute(fraction_b, "core", swap)
     source = slot_source(state, surf_index, surf_count)
     source_b = lax.ppermute(source, "core", swap)
-    source = jnp.concatenate(
-        [source[:256], source_b[:256], source[256:], source_b[256:], jnp.zeros((96,), jnp.float32)]
-    )
-    sums = bins(core.reshape(1), source[None, :], delay, fraction, delay_b, fraction_b, 0, 8)
+    sums = bins(core, source, source_b, delay, fraction, delay_b, fraction_b, 0, 8)
     parts = lax.all_to_all(sums, CHIP, 0, 0, tiled=True)
     total = jnp.sum(parts, axis=0)
     total = total.reshape(2, ROWS, 16, 8).transpose(0, 3, 1, 2).reshape(16, ROWS, 16)

time: 130 us -> 104 us (0.80)
  local copies, waits for them, and re-layouts: 36.1 us -> 3.68 us
  Pallas kernels: 33.9 us -> 42.4 us
  waiting for transfers between devices: 0.89 us -> 3.18 us
  other arithmetic: 2.05 us -> 0.23 us
    mul x34 -> x0, local copies, waits for them, and re-layouts: 10.7 us -> none  [the longest x32 10.5 us: line_derivative(): np.float32(table[i, j]) * flux[start + j]]
    dynamic_slice x2 -> x0, local copies, waits for them, and re-layouts: 8.55 us -> none  [other_half(): lax.dynamic_index_in_dim(halves, 1 - core, 2, keepdims=False)]
    pallas_call x0 -> x3, Pallas kernels: none -> 8.08 us  [the longest x1 4.07 us: other_half(): pl.pallas_call(half_kernel, grid_spec=pltpu.PrefetchScalarGridSpec(num_sc...]
    reshape x2 -> x1, local copies, waits for them, and re-layouts: 6.1 us -> 0.57 us  [slot_source(): surf_index.reshape(1, SLOTS)]
    squeeze x18 -> x0, local copies, waits for them, and re-layouts: 4.32 us -> none  [the longest x8 1.73 us: line_derivative(): flux[start + j]]
    ppermute x6, waiting for transfers between devices: 0.08 us -> 1.82 us  [the longest x4 1.82 us: around(): return (lax.ppermute(tile, axes, up), lax.ppermute(tile, axes, down))]
    slice x6 -> x0, local copies, waits for them, and re-layouts: 1.72 us -> none  [the longest x1 0.86 us: surface_plane(): across = state[2, :, :, at]]
    unnamed x25 -> x14, local copies, waits for them, and re-layouts: 2.85 us -> 1.85 us
  transfers between devices with their start and end apart: 7 -> 7, of which waited for: 2 -> 3; matrix products, arithmetic and copies ran while one was open for 26% -> 1% of each run, Pallas kernels for 0% -> 4%
where the time goes in v2:
time: 104 us
  blocking collectives  42.7 us (41%)
  Pallas kernels  42.4 us (41%)
  starting transfers between devices  11.2 us (11%)
  local copies, waits for them, and re-layouts  3.68 us (4%)
  waiting for transfers between devices  3.18 us (3%)
    all_to_all x1, blocking collectives, local(): parts = lax.all_to_all(sums, CHIP, 0, 0, tiled=True)  42.7 us
    pallas_call x1, Pallas kernels, bins(): pl.pallas_call(bins_kernel, grid_spec=pltpu.PrefetchScalarGridSpec(num_sc...  34.3 us
    ppermute x4, starting transfers between devices, around(): return (lax.ppermute(tile, axes, up), lax.ppermute(tile, axes, down))  10.7 us
    pallas_call x1, Pallas kernels, other_half(): pl.pallas_call(half_kernel, grid_spec=pltpu.PrefetchScalarGridSpec(num_sc...  4.07 us
    pallas_call x1, Pallas kernels, slot_source(): pl.pallas_call(source_kernel, in_specs=[vmem] * 7 + [pl.BlockSpec(memory_...  2.16 us
  transfers between devices with their start and end apart: 7, of which 3 were waited for; matrix products, arithmetic and copies ran while one was open for 1% of the time, Pallas kernels for 4%

profile of v2, /device:TPU:0, one launch (start us, length us, event | category | flops | bytes accessed | tf_op | source)
XLA Modules:
  0.0 104.1 jit_solution(11623804451545952890)
XLA Ops:
  0.0 0.0 copy-start.6
  0.0 0.0 copy-start
  0.0 4.1 %other_half.1 = (s32[272,1024]{1,0:T(8,128)}, f32[272,1024]{1,0:T(8,128)}) custom-call(s32[1]{0:T(128)} %bitcast.core_ref, s32[272,2048]{1,0:T(8,128)} %da_ref.1, f32[272,2048]{1,0:T(8,128)} %fa_ref.1), custom_call_target="tpu_custom_call" | custom-call | tf_op jit(solution)/shard_map/other_half/pallas_call | solution.py:160
  4.1 0.0 collective-permute-start.5
  4.1 0.5 collective-permute-start.6
  4.6 1.8 %tile.1.own_ref = f32[8,128]{1,0:T(8,128)} custom-call(f32[5,64,128]{2,1,0:T(8,128)} %bitcast.9), custom_call_target="tpu_custom_call" | custom-call | tf_op jit(solution)/shard_map/tile/pallas_call | solution.py:124
  6.4 6.6 %collective-permute-start.3 = (f32[8,128]{1,0:T(8,128)}, f32[8,128]{1,0:T(8,128)S(1)}, u32[]{:S(2)}, u32[]{:S(2)}) collective-permute-start(f32[8,128]{1,0:T(8,128)} %tile.1.own_ref), channel_id=1, source_target_pairs={{1,0},{2,1},{3,2},{4,3},{5,4},{6,5},{7,6},{8,7},{9,8},{10,9},{11,1... | collective-permute-start | bytes 12296 | tf_op jit(solution)/shard_map/ppermute | solution.py:135
  13.0 0.0 collective-permute-start.2
  13.0 1.3 %collective-permute-start.1 = (f32[8,128]{1,0:T(8,128)}, f32[8,128]{1,0:T(8,128)S(1)}, u32[]{:S(2)}, u32[]{:S(2)}) collective-permute-start(f32[8,128]{1,0:T(8,128)} %tile.1.own_ref), channel_id=1, source_target_pairs={{16,0},{32,16},{48,32},{64,48},{80,64},{96,80},{112,96},{17,1},{33... | collective-permute-start | bytes 12296 | tf_op jit(solution)/shard_map/ppermute | solution.py:135
  14.3 0.2 collective-permute-done.3.ay_ref
  14.5 0.0 copy-start.2
  14.6 2.8 %collective-permute-start = (f32[8,128]{1,0:T(8,128)}, f32[8,128]{1,0:T(8,128)S(1)}, u32[]{:S(2)}, u32[]{:S(2)}) collective-permute-start(f32[8,128]{1,0:T(8,128)} %tile.1.own_ref), channel_id=1, source_target_pairs={{0,16},{16,32},{32,48},{48,64},{64,80},{80,96},{96,112},{1,17},{17... | collective-permute-start | bytes 12296 | tf_op jit(solution)/shard_map/ppermute | solution.py:135
  18.0 0.0 copy-done.6
  18.0 0.6 reshape.20.index_ref
  18.6 1.6 %collective-permute-done.2.by_ref = f32[8,128]{1,0:T(8,128)S(1)} collective-permute-done((f32[8,128]{1,0:T(8,128)}, f32[8,128]{1,0:T(8,128)S(1)}, u32[]{:S(2)}, u32[]{:S(2)}) %collective-permute-start.2) | collective-permute-done | bytes 4128 | tf_op jit(solution)/shard_map/ppermute | solution.py:135
  20.1 0.0 copy-start.3
  20.1 0.0 collective-permute-done.1.ax_ref
  20.2 0.0 copy-start.4
  20.2 0.0 collective-permute-done.bx_ref
  20.2 0.0 copy-done.2
  20.2 0.6 copy-done.3
  20.7 0.0 copy-done.4
  20.7 0.0 copy-start.5
  20.7 0.6 copy-done.5
  21.3 2.2 %source.1.src_ref = f32[1,272]{1,0:T(1,128)} custom-call(f32[1024,64]{1,0:T(8,128)} %constant.12.clone.map_ref, f32[8,128]{1,0:T(8,128)} %tile.1.own_ref, f32[8,128]{1,0:T(8,128)} %copy-done.5, f32[8,128]{1,0:T(8,128)} %copy-done.4, f32[8,128]{1,0:T(8,128)} %copy-done.3, f32[8,128]{1,0:T(8,128)} %copy-done.2, s32[1,272]{1,0:T(1,128)} %reshape.20.index_ref, ...), custom_call_target="tpu_custom_call" | custom-call | tf_op jit(solution)/shard_map/source/pallas_call | solution.py:139
  23.5 0.0 collective-permute-start.4
  23.5 1.4 %collective-permute-done.4.src_b_ref = f32[1,272]{1,0:T(1,128)S(1)} collective-permute-done((f32[1,272]{1,0:T(1,128)}, f32[1,272]{1,0:T(1,128)S(1)}, u32[]{:S(2)}, u32[]{:S(2)}) %collective-permute-start.4) | collective-permute-done | bytes 1120 | tf_op jit(solution)/shard_map/ppermute | solution.py:268
  24.9 0.0 collective-permute-done.5.db_ref
  24.9 0.0 collective-permute-done.6.fb_ref
  24.9 0.0 copy-done
  24.9 0.0 copy-start.1
  24.9 0.7 copy-done.1
  25.6 34.3 %bins.1 = f32[64,72,128]{2,1,0:T(8,128)} custom-call(s32[1]{0:T(128)} %bitcast.core_ref, f32[1,272]{1,0:T(1,128)S(1)} %copy-done.1, f32[1,272]{1,0:T(1,128)S(1)} %collective-permute-done.4.src_b_ref, s32[272,2048]{1,0:T(8,128)S(1)} %copy-done, f32[272,2048]{1,0:T(8,128)} %fa_ref.1, s32[272,1024]{1,0:T(8,128)S(1)} %collective-permute-done.5.db_ref, ...), custom_call_target="tpu_custom_call" | custom-call | tf_op jit(solution)/shard_map/bins/pallas_call | solution.py:247
  59.9 42.7 %all_to_all.5 = f32[64,72,128]{2,1,0:T(8,128)S(1)} all-to-all(f32[64,72,128]{2,1,0:T(8,128)} %bins.1), channel_id=1, replica_groups=mesh['x'=4,'core'=2,'y'=4,'z'=4] {'x','y','z'}, dimensions={0} | all-to-all | bytes 4718592 | tf_op jit(solution)/shard_map/all_to_all | solution.py:270
  102.5 0.1 reduce_sum.9
  102.7 0.1 copy.9
  102.8 0.1 reshape.21
  103.0 0.1 slice_add_fusion
  103.1 0.2 copy.11
  103.3 0.1 reshape.23
  103.4 0.6 slice.14
  (2 shorter events, 0.1 us)
Async XLA Ops:
  0.0 18.0 %copy-start.6 = (s32[272]{0:T(512)S(1)}, s32[272]{0:T(512)}, u32[]{:S(2)}) copy-start(s32[272]{0:T(512)} %param.7) | copy-start | bytes 3268
  0.0 24.9 %copy-start = (s32[272,2048]{1,0:T(8,128)S(1)}, s32[272,2048]{1,0:T(8,128)}, u32[]{:S(2)}) copy-start(s32[272,2048]{1,0:T(8,128)} %da_ref.1) | copy-start | bytes 6684676
  4.1 20.8 %collective-permute-start.5 = (s32[272,1024]{1,0:T(8,128)}, s32[272,1024]{1,0:T(8,128)S(1)}, u32[]{:S(2)}, u32[]{:S(2)}) collective-permute-start(s32[272,1024]{1,0:T(8,128)} %get-tuple-element.7), channel_id=1, source_target_pairs={{0,16},{16,0},{1,17},{17,1},{2,18},{18,2},{3,19},{19,3},{4,20},{20... | collective-permute-start | bytes 3342344 | tf_op jit(solution)/shard_map/ppermute | solution.py:265
  4.1 20.8 %collective-permute-start.6 = (f32[272,1024]{1,0:T(8,128)}, f32[272,1024]{1,0:T(8,128)}, u32[]{:S(2)}, u32[]{:S(2)}) collective-permute-start(f32[272,1024]{1,0:T(8,128)} %get-tuple-element.8), channel_id=1, source_target_pairs={{0,16},{16,0},{1,17},{17,1},{2,18},{18,2},{3,19},{19,3},{4,20},{20... | collective-permute-start | bytes 3342344 | tf_op jit(solution)/shard_map/ppermute | solution.py:266
  6.4 8.1 %collective-permute-start.3 = (f32[8,128]{1,0:T(8,128)}, f32[8,128]{1,0:T(8,128)S(1)}, u32[]{:S(2)}, u32[]{:S(2)}) collective-permute-start(f32[8,128]{1,0:T(8,128)} %tile.1.own_ref), channel_id=1, source_target_pairs={{1,0},{2,1},{3,2},{4,3},{5,4},{6,5},{7,6},{8,7},{9,8},{10,9},{11,1... | collective-permute-start | bytes 12296 | tf_op jit(solution)/shard_map/ppermute | solution.py:135
  13.0 7.1 %collective-permute-start.2 = (f32[8,128]{1,0:T(8,128)}, f32[8,128]{1,0:T(8,128)S(1)}, u32[]{:S(2)}, u32[]{:S(2)}) collective-permute-start(f32[8,128]{1,0:T(8,128)} %tile.1.own_ref), channel_id=1, source_target_pairs={{0,1},{1,2},{2,3},{3,4},{4,5},{5,6},{6,7},{7,8},{8,9},{9,10},{10,1... | collective-permute-start | bytes 12296 | tf_op jit(solution)/shard_map/ppermute | solution.py:135
  13.0 7.1 %collective-permute-start.1 = (f32[8,128]{1,0:T(8,128)}, f32[8,128]{1,0:T(8,128)S(1)}, u32[]{:S(2)}, u32[]{:S(2)}) collective-permute-start(f32[8,128]{1,0:T(8,128)} %tile.1.own_ref), channel_id=1, source_target_pairs={{16,0},{32,16},{48,32},{64,48},{80,64},{96,80},{112,96},{17,1},{33... | collective-permute-start | bytes 12296 | tf_op jit(solution)/shard_map/ppermute | solution.py:135
  14.5 5.6 %copy-start.2 = (f32[8,128]{1,0:T(8,128)}, f32[8,128]{1,0:T(8,128)S(1)}, u32[]{:S(2)}) copy-start(f32[8,128]{1,0:T(8,128)S(1)} %collective-permute-done.3.ay_ref) | copy-start | bytes 12292
  14.6 5.6 %collective-permute-start = (f32[8,128]{1,0:T(8,128)}, f32[8,128]{1,0:T(8,128)S(1)}, u32[]{:S(2)}, u32[]{:S(2)}) collective-permute-start(f32[8,128]{1,0:T(8,128)} %tile.1.own_ref), channel_id=1, source_target_pairs={{0,16},{16,32},{32,48},{48,64},{64,80},{80,96},{96,112},{1,17},{17... | collective-permute-start | bytes 12296 | tf_op jit(solution)/shard_map/ppermute | solution.py:135
  20.1 0.6 copy-start.3
  20.2 0.6 copy-start.4
  20.7 0.6 copy-start.5
  23.5 1.4 %collective-permute-start.4 = (f32[1,272]{1,0:T(1,128)}, f32[1,272]{1,0:T(1,128)S(1)}, u32[]{:S(2)}, u32[]{:S(2)}) collective-permute-start(f32[1,272]{1,0:T(1,128)} %source.1.src_ref), channel_id=1, source_target_pairs={{0,16},{16,0},{1,17},{17,1},{2,18},{18,2},{3,19},{19,3},{4,20},{20... | collective-permute-start | bytes 3272 | tf_op jit(solution)/shard_map/ppermute | solution.py:268
  24.9 0.7 copy-start.1

commit v3 on v2

--- a/solution.py
+++ b/solution.py
@@ -239,23 +239,42 @@
         return 0
     lax.fori_loop(0, BLOCK // 16, pair, 0, unroll=False)
 
-def bins(core, src, src_b, delay, frac, delay_b, frac_b, first, blocks):
-    own = lambda n, c: (0, ((n + first) // 2) * 4 + c[0] * 2 + (n + first) % 2)
-    sib = lambda n, c: (0, n + first)
-    spec = pl.BlockSpec((SLOTS, BLOCK), own)
-    spec_b = pl.BlockSpec((SLOTS, BLOCK), sib)
+def bins(place, src, src_b, delay, frac, delay_b, frac_b):
+    mine = pl.BlockSpec((SLOTS, BLOCK), lambda n, c: (0, c[1] * 4 + c[0] * 2 + n))
+    other = pl.BlockSpec((SLOTS, BLOCK), lambda n, c: (0, c[1] * 2 + n))
+    row = pl.BlockSpec((1, SLOTS), lambda n, c: (0, 0))
+    owners = 256 // 16
     return pl.pallas_call(
         bins_kernel,
         grid_spec=pltpu.PrefetchScalarGridSpec(
-            num_scalar_prefetch=1, grid=(blocks,),
-            in_specs=[pl.BlockSpec((1, SLOTS), lambda n, c: (0, 0))] * 2 + [spec, spec, spec_b, spec_b],
-            out_specs=pl.BlockSpec((8, 2 * ROWS, 128), lambda n, c: (n, 0, 0)),
-            scratch_shapes=[pltpu.VMEM((BLOCK, LANES), jnp.float32), pltpu.VMEM((BLOCK, LANES), jnp.float32), pltpu.VMEM((2, 8, LANES), jnp.float32)],
+            num_scalar_prefetch=1,
+            grid=(256 // BLOCK,),
+            in_specs=[row, row, mine, mine, other, other],
+            out_specs=pl.BlockSpec((BLOCK // 16, 2 * ROWS, 128), lambda n, c: (n, 0, 0)),
+            scratch_shapes=[
+                pltpu.VMEM((BLOCK, LANES), jnp.float32),
+                pltpu.VMEM((BLOCK, LANES), jnp.float32),
+                pltpu.VMEM((2, 8, LANES), jnp.float32),
+            ],
         ),
-        out_shape=jax.ShapeDtypeStruct((8 * blocks, 2 * ROWS, 128), jnp.float32),
-        compiler_params=pltpu.CompilerParams(vmem_limit_bytes=48 * 1024 * 1024),
+        out_shape=jax.ShapeDtypeStruct((owners, 2 * ROWS, 128), jnp.float32),
+        compiler_params=pltpu.CompilerParams(vmem_limit_bytes=32 * 1024 * 1024),
+        cost_estimate=pl.CostEstimate(
+            flops=32 * 2 * 288 * 256 * LANES, bytes_accessed=8 * 2 * SLOTS * 256, transcendentals=0
+        ),
         name="bins",
-    )(core, src, src_b, delay, frac, delay_b, frac_b)
+    )(place, src, src_b, delay, frac, delay_b, frac_b)
+
+
+def shifted(array, axis, step):
+    return lax.ppermute(array, axis, [(i, (i + step) % 4) for i in range(4)])
+
+
+def scattered(total, axis):
+    here = lax.axis_index(axis)
+    block = lambda d: lax.dynamic_index_in_dim(total, (here + d) % 4, 0, keepdims=False)
+    got = [shifted(block(d), axis, d) for d in (2, 1, 3)]
+    return block(0) + got[0] + got[1] + got[2]
 
 
 def local(state, surf_index, surf_count, delay, fraction):
@@ -266,9 +285,14 @@
     fraction_b = lax.ppermute(fraction_b, "core", swap)
     source = slot_source(state, surf_index, surf_count)
     source_b = lax.ppermute(source, "core", swap)
-    sums = bins(core, source, source_b, delay, fraction, delay_b, fraction_b, 0, 8)
-    parts = lax.all_to_all(sums, CHIP, 0, 0, tiled=True)
-    total = jnp.sum(parts, axis=0)
+    here = lax.axis_index("x")
+    got = []
+    for d in (2, 1, 3, 0):
+        place = jnp.stack([core[0], (here + d) % 4])
+        sums = bins(place, source, source_b, delay, fraction, delay_b, fraction_b)
+        got.append(shifted(sums, "x", d) if d else sums)
+    total = (got[0] + got[1] + got[2] + got[3]).reshape(4, 4, 2 * ROWS, 128)
+    total = scattered(scattered(total, "y"), "z")
     total = total.reshape(2, ROWS, 16, 8).transpose(0, 3, 1, 2).reshape(16, ROWS, 16)
     carry = jnp.pad(total[:, :34, 15:], ((0, 0), (1, 0), (0, 14)))
     return (total[:, :35, :RADIX] + carry).reshape(16, 35 * RADIX)[:, :SAMPLES]

time: 104 us -> 98.5 us (0.947); the launches traced: 104 us -> 97.2 us
  blocking collectives: 42.7 us -> 0 us
  waiting for transfers between devices: 3.18 us -> 15.6 us
  starting transfers between devices: 11.2 us -> 23.3 us
  Pallas kernels: 42.4 us -> 48.5 us
  local copies, waits for them, and re-layouts: 3.68 us -> 7 us
  other arithmetic: 0.23 us -> 1.95 us
    all_to_all x1 -> x0, blocking collectives: 42.7 us -> none  [local(): parts = lax.all_to_all(sums, CHIP, 0, 0, tiled=True)]
    ppermute x0 -> x9, waiting for transfers between devices: none -> 12.8 us  [shifted(): return lax.ppermute(array, axis, [(i, (i + step) % 4) for i in range(4)])]
    ppermute x0 -> x9, starting transfers between devices: none -> 12.1 us  [shifted(): return lax.ppermute(array, axis, [(i, (i + step) % 4) for i in range(4)])]
    pallas_call x1 -> x4, Pallas kernels: 34.3 us -> 40.4 us  [bins(): pl.pallas_call(bins_kernel, grid_spec=pltpu.PrefetchScalarGridSpec(num_sc...]
    unnamed x14 -> x20, local copies, waits for them, and re-layouts: 1.85 us -> 5.1 us
    add x0 -> x3, other arithmetic: none -> 1.57 us  [the longest x1 1.52 us: local(): total = (got[0] + got[1] + got[2] + got[3]).reshape(4, 4, 2 * ROWS, 128)]
  transfers between devices with their start and end apart: 7 -> 16, of which waited for: 3 -> 9; matrix products, arithmetic and copies ran while one was open for 1% -> 1% of each run, Pallas kernels for 4% -> 35%
where the time goes in v3:
time: 98.5 us; the launch traced here: 97.2 us
  Pallas kernels  48.5 us (49%)
  starting transfers between devices  23.3 us (24%)
  waiting for transfers between devices  15.6 us (16%)
  local copies, waits for them, and re-layouts  7 us (7%)
  other arithmetic  1.95 us (2%)
    pallas_call x4, Pallas kernels, bins(): pl.pallas_call(bins_kernel, grid_spec=pltpu.PrefetchScalarGridSpec(num_sc...  40.4 us
    ppermute x9, waiting for transfers between devices, shifted(): return lax.ppermute(array, axis, [(i, (i + step) % 4) for i in range(4)])  12.8 us
    ppermute x9, starting transfers between devices, shifted(): return lax.ppermute(array, axis, [(i, (i + step) % 4) for i in range(4)])  12.1 us
    ppermute x4, starting transfers between devices, around(): return (lax.ppermute(tile, axes, up), lax.ppermute(tile, axes, down))  10.7 us
    unnamed x20, local copies, waits for them, and re-layouts  5.1 us
    pallas_call x1, Pallas kernels, other_half(): pl.pallas_call(half_kernel, grid_spec=pltpu.PrefetchScalarGridSpec(num_sc...  4.05 us
    pallas_call x1, Pallas kernels, slot_source(): pl.pallas_call(source_kernel, in_specs=[vmem] * 7 + [pl.BlockSpec(memory_...  2.15 us
  transfers between devices with their start and end apart: 16, of which 9 were waited for; matrix products, arithmetic and copies ran while one was open for 1% of the time, Pallas kernels for 35%

profile of v3, /device:TPU:0, one launch (start us, length us, event | category | flops | bytes accessed | tf_op | source)
XLA Modules:
  0.0 97.2 jit_solution(16733193293225701665)
XLA Ops:
  0.0 4.0 %other_half.1 = (s32[272,1024]{1,0:T(8,128)}, f32[272,1024]{1,0:T(8,128)}) custom-call(s32[1]{0:T(128)} %bitcast.core_ref, s32[272,2048]{1,0:T(8,128)} %da_ref.7, f32[272,2048]{1,0:T(8,128)} %fa_ref.7), custom_call_target="tpu_custom_call" | custom-call | tf_op jit(solution)/shard_map/other_half/pallas_call | solution.py:160
  4.1 0.5 collective-permute-start.6
  4.6 1.8 %tile.1.own_ref = f32[8,128]{1,0:T(8,128)} custom-call(f32[5,64,128]{2,1,0:T(8,128)} %bitcast.40), custom_call_target="tpu_custom_call" | custom-call | tf_op jit(solution)/shard_map/tile/pallas_call | solution.py:124
  6.4 6.6 %collective-permute-start.3 = (f32[8,128]{1,0:T(8,128)}, f32[8,128]{1,0:T(8,128)S(1)}, u32[]{:S(2)}, u32[]{:S(2)}) collective-permute-start(f32[8,128]{1,0:T(8,128)} %tile.1.own_ref), channel_id=1, source_target_pairs={{1,0},{2,1},{3,2},{4,3},{5,4},{6,5},{7,6},{8,7},{9,8},{10,9},{11,1... | collective-permute-start | bytes 12296 | tf_op jit(solution)/shard_map/ppermute | solution.py:135
  13.0 0.0 collective-permute-start.2
  13.0 1.3 %collective-permute-start.1 = (f32[8,128]{1,0:T(8,128)}, f32[8,128]{1,0:T(8,128)S(1)}, u32[]{:S(2)}, u32[]{:S(2)}) collective-permute-start(f32[8,128]{1,0:T(8,128)} %tile.1.own_ref), channel_id=1, source_target_pairs={{16,0},{32,16},{48,32},{64,48},{80,64},{96,80},{112,96},{17,1},{33... | collective-permute-start | bytes 12296 | tf_op jit(solution)/shard_map/ppermute | solution.py:135
  14.3 0.1 pad_add_fusion.1.core_ref
  14.4 0.2 collective-permute-done.3.ay_ref
  14.5 2.9 %collective-permute-start = (f32[8,128]{1,0:T(8,128)}, f32[8,128]{1,0:T(8,128)S(1)}, u32[]{:S(2)}, u32[]{:S(2)}) collective-permute-start(f32[8,128]{1,0:T(8,128)} %tile.1.own_ref), channel_id=1, source_target_pairs={{0,16},{16,32},{32,48},{48,64},{64,80},{80,96},{96,112},{1,17},{17... | collective-permute-start | bytes 12296 | tf_op jit(solution)/shard_map/ppermute | solution.py:135
  17.4 0.1 pad_add_fusion.2.core_ref
  18.1 0.6 reshape.20.index_ref
  18.7 1.4 %collective-permute-done.2.by_ref = f32[8,128]{1,0:T(8,128)S(1)} collective-permute-done((f32[8,128]{1,0:T(8,128)}, f32[8,128]{1,0:T(8,128)S(1)}, u32[]{:S(2)}, u32[]{:S(2)}) %collective-permute-start.2) | collective-permute-done | bytes 4128 | tf_op jit(solution)/shard_map/ppermute | solution.py:135
  20.1 0.6 copy-done.6
  20.7 0.6 copy-done.8
  21.3 2.1 %source.1.src_ref = f32[1,272]{1,0:T(1,128)} custom-call(f32[1024,64]{1,0:T(8,128)} %constant.104.clone.map_ref, f32[8,128]{1,0:T(8,128)} %tile.1.own_ref, f32[8,128]{1,0:T(8,128)} %copy-done.8, f32[8,128]{1,0:T(8,128)} %copy-done.7, f32[8,128]{1,0:T(8,128)} %copy-done.6, f32[8,128]{1,0:T(8,128)} %copy-done.5, s32[1,272]{1,0:T(1,128)} %reshape.20.index_ref, ...), custom_call_target="tpu_custom_call" | custom-call | tf_op jit(solution)/shard_map/source/pallas_call | solution.py:139
  23.5 0.1 pad_add_fusion.core_ref
  23.5 1.3 %collective-permute-done.4.src_b_ref = f32[1,272]{1,0:T(1,128)S(1)} collective-permute-done((f32[1,272]{1,0:T(1,128)}, f32[1,272]{1,0:T(1,128)S(1)}, u32[]{:S(2)}, u32[]{:S(2)}) %collective-permute-start.4) | collective-permute-done | bytes 1120 | tf_op jit(solution)/shard_map/ppermute | solution.py:287
  24.8 0.0 copy-start.1
  24.8 1.6 %copy-done.1 = f32[272,2048]{1,0:T(8,128)S(1)} copy-done((f32[272,2048]{1,0:T(8,128)S(1)}, f32[272,2048]{1,0:T(8,128)}, u32[]{:S(2)}) %copy-start.1) | copy-done | bytes 2228248
  26.5 0.7 copy-done.3
  27.1 10.3 %bins.4 = f32[16,72,128]{2,1,0:T(8,128)} custom-call(s32[2]{0:T(128)S(1)} %pad_add_fusion.core_ref, f32[1,272]{1,0:T(1,128)S(1)} %copy-done.3, f32[1,272]{1,0:T(1,128)S(1)} %collective-permute-done.4.src_b_ref, s32[272,2048]{1,0:T(8,128)S(1)} %copy-done, f32[272,2048]{1,0:T(8,128)S(1)} %copy-done.1, s32[272,1024]{1,0:T(8,128)S(1)} %collective-permute-done.5.db_ref, ...), custom_call_target="tpu_custom_call" | custom-call | flops 3019898880 | bytes 1114112 | tf_op jit(solution)/shard_map/bins/pallas_call | solution.py:247
  37.4 3.0 %collective-permute-start.7 = (f32[16,72,128]{2,1,0:T(8,128)}, f32[16,72,128]{2,1,0:T(8,128)}, u32[]{:S(2)}, u32[]{:S(2)}) collective-permute-start(f32[16,72,128]{2,1,0:T(8,128)} %bins.4), channel_id=1, source_target_pairs={{0,64},{32,96},{64,0},{96,32},{1,65},{33,97},{65,1},{97,33},{2,66}... | collective-permute-start | bytes 1769480 | tf_op jit(solution)/shard_map/ppermute | solution.py:270
  40.5 10.3 %bins.5 = f32[16,72,128]{2,1,0:T(8,128)} custom-call(s32[2]{0:T(128)S(1)} %pad_add_fusion.1.core_ref, f32[1,272]{1,0:T(1,128)S(1)} %copy-done.3, f32[1,272]{1,0:T(1,128)S(1)} %collective-permute-done.4.src_b_ref, s32[272,2048]{1,0:T(8,128)S(1)} %copy-done, f32[272,2048]{1,0:T(8,128)S(1)} %copy-done.1, s32[272,1024]{1,0:T(8,128)S(1)} %collective-permute-done.5.db_ref, ...), custom_call_target="tpu_custom_call" | custom-call | flops 3019898880 | bytes 1114112 | tf_op jit(solution)/shard_map/bins/pallas_call | solution.py:247
  50.7 0.6 collective-permute-start.8
  51.3 10.3 %bins.6 = f32[16,72,128]{2,1,0:T(8,128)} custom-call(s32[2]{0:T(128)S(1)} %pad_add_fusion.2.core_ref, f32[1,272]{1,0:T(1,128)S(1)} %copy-done.3, f32[1,272]{1,0:T(1,128)S(1)} %collective-permute-done.4.src_b_ref, s32[272,2048]{1,0:T(8,128)S(1)} %copy-done, f32[272,2048]{1,0:T(8,128)S(1)} %copy-done.1, s32[272,1024]{1,0:T(8,128)S(1)} %collective-permute-done.5.db_ref, ...), custom_call_target="tpu_custom_call" | custom-call | flops 3019898880 | bytes 1114112 | tf_op jit(solution)/shard_map/bins/pallas_call | solution.py:247
  61.6 2.7 %collective-permute-start.9 = (f32[16,72,128]{2,1,0:T(8,128)}, f32[16,72,128]{2,1,0:T(8,128)}, u32[]{:S(2)}, u32[]{:S(2)}) collective-permute-start(f32[16,72,128]{2,1,0:T(8,128)} %bins.6), channel_id=1, source_target_pairs={{0,96},{32,0},{64,32},{96,64},{1,97},{33,1},{65,33},{97,65},{2,98}... | collective-permute-start | bytes 1769480 | tf_op jit(solution)/shard_map/ppermute | solution.py:270
  64.3 0.1 pad_add_fusion.3.core_ref
  64.3 1.6 %copy-done.2 = f32[272,2048]{1,0:T(8,128)S(1)} copy-done((f32[272,2048]{1,0:T(8,128)S(1)}, f32[272,2048]{1,0:T(8,128)}, u32[]{:S(2)}) %copy-start.2) | copy-done | bytes 2228248
  66.0 9.6 %bins.7 = f32[16,72,128]{2,1,0:T(8,128)S(1)} custom-call(s32[2]{0:T(128)S(1)} %pad_add_fusion.3.core_ref, f32[1,272]{1,0:T(1,128)S(1)} %copy-done.4, f32[1,272]{1,0:T(1,128)S(1)} %collective-permute-done.4.src_b_ref, s32[272,2048]{1,0:T(8,128)S(1)} %copy-done, f32[272,2048]{1,0:T(8,128)S(1)} %copy-done.2, s32[272,1024]{1,0:T(8,128)S(1)} %collective-permute-done.5.db_ref, ...), custom_call_target="tpu_custom_call" | custom-call | flops 3019898880 | bytes 1114112 | tf_op jit(solution)/shard_map/bins/pallas_call | solution.py:247
  75.6 1.4 %collective-permute-done.9 = f32[16,72,128]{2,1,0:T(8,128)} collective-permute-done((f32[16,72,128]{2,1,0:T(8,128)}, f32[16,72,128]{2,1,0:T(8,128)}, u32[]{:S(2)}, u32[]{:S(2)}) %collective-permute-start.9) | collective-permute-done | bytes 589856 | tf_op jit(solution)/shard_map/ppermute | solution.py:270
  77.0 1.5 %add_add_fusion = f32[16,72,128]{2,1,0:T(8,128)S(1)} fusion(f32[16,72,128]{2,1,0:T(8,128)S(1)} %bins.7, f32[16,72,128]{2,1,0:T(8,128)} %collective-permute-done.9, f32[16,72,128]{2,1,0:T(8,128)} %collective-permute-done.7, f32[16,72,128]{2,1,0:T(8,128)} %collective-permute-done.8), kind=kLoop, calls=%fused_computation | loop fusion | flops 442368 | bytes 2949120 | tf_op jit(solution)/shard_map/add | solution.py:294
  78.5 0.1 collective-permute-start.10
  78.7 1.1 %collective-permute-start.12 = (f32[4,72,128]{2,1,0:T(8,128)S(1)}, f32[4,72,128]{2,1,0:T(8,128)S(1)}, u32[]{:S(2)}, u32[]{:S(2)}) collective-permute-start(f32[4,72,128]{2,1,0:T(8,128)S(1)} %get-tuple-element.10), channel_id=1, source_target_pairs={{0,12},{4,0},{8,4},{12,8},{1,13},{5,1},{9,5},{13,9},{2,14},{6,2},{... | collective-permute-start | bytes 442376 | tf_op jit(solution)/shard_map/ppermute | solution.py:270
  79.7 1.0 %collective-permute-start.11 = (f32[4,72,128]{2,1,0:T(8,128)S(1)}, f32[4,72,128]{2,1,0:T(8,128)S(1)}, u32[]{:S(2)}, u32[]{:S(2)}) collective-permute-start(f32[4,72,128]{2,1,0:T(8,128)S(1)} %get-tuple-element.11), channel_id=1, source_target_pairs={{0,4},{4,8},{8,12},{12,0},{1,5},{5,9},{9,13},{13,1},{2,6},{6,10},{... | collective-permute-start | bytes 442376 | tf_op jit(solution)/shard_map/ppermute | solution.py:270
  80.7 5.5 %collective-permute-done.10 = f32[4,72,128]{2,1,0:T(8,128)S(1)} collective-permute-done((f32[4,72,128]{2,1,0:T(8,128)S(1)}, f32[4,72,128]{2,1,0:T(8,128)S(1)}, u32[]{:S(2)}, u32[]{:S(2)}) %collective-permute-start.10) | collective-permute-done | bytes 147488 | tf_op jit(solution)/shard_map/ppermute | solution.py:270
  86.2 1.5 %collective-permute-done.11 = f32[4,72,128]{2,1,0:T(8,128)S(1)} collective-permute-done((f32[4,72,128]{2,1,0:T(8,128)S(1)}, f32[4,72,128]{2,1,0:T(8,128)S(1)}, u32[]{:S(2)}, u32[]{:S(2)}) %collective-permute-start.11) | collective-permute-done | bytes 147488 | tf_op jit(solution)/shard_map/ppermute | solution.py:270
  87.8 0.4 collective-permute-start.13
  88.2 2.5 %collective-permute-start.15 = (f32[72,128]{1,0:T(8,128)S(1)}, f32[72,128]{1,0:T(8,128)S(1)}, u32[]{:S(2)}, u32[]{:S(2)}) collective-permute-start(f32[72,128]{1,0:T(8,128)S(1)} %get-tuple-element.13), channel_id=1, source_target_pairs={{0,3},{1,0},{2,1},{3,2},{4,7},{5,4},{6,5},{7,6},{8,11},{9,8},{10,9... | collective-permute-start | bytes 110600 | tf_op jit(solution)/shard_map/ppermute | solution.py:270
  90.7 0.8 collective-permute-start.14
  91.4 1.9 %collective-permute-done.13 = f32[72,128]{1,0:T(8,128)S(1)} collective-permute-done((f32[72,128]{1,0:T(8,128)S(1)}, f32[72,128]{1,0:T(8,128)S(1)}, u32[]{:S(2)}, u32[]{:S(2)}) %collective-permute-start.13) | collective-permute-done | bytes 36896 | tf_op jit(solution)/shard_map/ppermute | solution.py:270
  93.3 0.4 collective-permute-done.15
  93.8 2.1 %collective-permute-done.14 = f32[72,128]{1,0:T(8,128)S(1)} collective-permute-done((f32[72,128]{1,0:T(8,128)S(1)}, f32[72,128]{1,0:T(8,128)S(1)}, u32[]{:S(2)}, u32[]{:S(2)}) %collective-permute-start.14) | collective-permute-done | bytes 36896 | tf_op jit(solution)/shard_map/ppermute | solution.py:270
  95.8 0.1 copy.9
  95.9 0.1 reshape.22
  96.2 0.1 slice_add_fusion
  96.2 0.2 copy.11
  96.5 0.1 reshape.24
  96.6 0.6 slice.14
  (29 shorter events, 0.2 us)
Async XLA Ops:
  0.0 18.1 %copy-start.9 = (s32[272]{0:T(512)S(1)}, s32[272]{0:T(512)}, u32[]{:S(2)}) copy-start(s32[272]{0:T(512)} %param.7) | copy-start | bytes 3268
  0.0 24.8 %copy-start = (s32[272,2048]{1,0:T(8,128)S(1)}, s32[272,2048]{1,0:T(8,128)}, u32[]{:S(2)}) copy-start(s32[272,2048]{1,0:T(8,128)} %da_ref.7) | copy-start | bytes 6684676
  4.1 20.8 %collective-permute-start.5 = (s32[272,1024]{1,0:T(8,128)}, s32[272,1024]{1,0:T(8,128)S(1)}, u32[]{:S(2)}, u32[]{:S(2)}) collective-permute-start(s32[272,1024]{1,0:T(8,128)} %get-tuple-element.7), channel_id=1, source_target_pairs={{0,16},{16,0},{1,17},{17,1},{2,18},{18,2},{3,19},{19,3},{4,20},{20... | collective-permute-start | bytes 3342344 | tf_op jit(solution)/shard_map/ppermute | solution.py:284
  4.1 20.8 %collective-permute-start.6 = (f32[272,1024]{1,0:T(8,128)}, f32[272,1024]{1,0:T(8,128)}, u32[]{:S(2)}, u32[]{:S(2)}) collective-permute-start(f32[272,1024]{1,0:T(8,128)} %get-tuple-element.8), channel_id=1, source_target_pairs={{0,16},{16,0},{1,17},{17,1},{2,18},{18,2},{3,19},{19,3},{4,20},{20... | collective-permute-start | bytes 3342344 | tf_op jit(solution)/shard_map/ppermute | solution.py:285
  6.4 8.1 %collective-permute-start.3 = (f32[8,128]{1,0:T(8,128)}, f32[8,128]{1,0:T(8,128)S(1)}, u32[]{:S(2)}, u32[]{:S(2)}) collective-permute-start(f32[8,128]{1,0:T(8,128)} %tile.1.own_ref), channel_id=1, source_target_pairs={{1,0},{2,1},{3,2},{4,3},{5,4},{6,5},{7,6},{8,7},{9,8},{10,9},{11,1... | collective-permute-start | bytes 12296 | tf_op jit(solution)/shard_map/ppermute | solution.py:135
  13.0 7.1 %collective-permute-start.2 = (f32[8,128]{1,0:T(8,128)}, f32[8,128]{1,0:T(8,128)S(1)}, u32[]{:S(2)}, u32[]{:S(2)}) collective-permute-start(f32[8,128]{1,0:T(8,128)} %tile.1.own_ref), channel_id=1, source_target_pairs={{0,1},{1,2},{2,3},{3,4},{4,5},{5,6},{6,7},{7,8},{8,9},{9,10},{10,1... | collective-permute-start | bytes 12296 | tf_op jit(solution)/shard_map/ppermute | solution.py:135
  13.0 7.1 %collective-permute-start.1 = (f32[8,128]{1,0:T(8,128)}, f32[8,128]{1,0:T(8,128)S(1)}, u32[]{:S(2)}, u32[]{:S(2)}) collective-permute-start(f32[8,128]{1,0:T(8,128)} %tile.1.own_ref), channel_id=1, source_target_pairs={{16,0},{32,16},{48,32},{64,48},{80,64},{96,80},{112,96},{17,1},{33... | collective-permute-start | bytes 12296 | tf_op jit(solution)/shard_map/ppermute | solution.py:135
  14.5 5.6 %copy-start.5 = (f32[8,128]{1,0:T(8,128)}, f32[8,128]{1,0:T(8,128)S(1)}, u32[]{:S(2)}) copy-start(f32[8,128]{1,0:T(8,128)S(1)} %collective-permute-done.3.ay_ref) | copy-start | bytes 12292
  14.5 5.6 %collective-permute-start = (f32[8,128]{1,0:T(8,128)}, f32[8,128]{1,0:T(8,128)S(1)}, u32[]{:S(2)}, u32[]{:S(2)}) collective-permute-start(f32[8,128]{1,0:T(8,128)} %tile.1.own_ref), channel_id=1, source_target_pairs={{0,16},{16,32},{32,48},{48,64},{64,80},{80,96},{96,112},{1,17},{17... | collective-permute-start | bytes 12296 | tf_op jit(solution)/shard_map/ppermute | solution.py:135
  20.1 0.6 copy-start.6
  20.1 0.6 copy-start.7
  20.7 0.6 copy-start.8
  23.5 1.4 %collective-permute-start.4 = (f32[1,272]{1,0:T(1,128)}, f32[1,272]{1,0:T(1,128)S(1)}, u32[]{:S(2)}, u32[]{:S(2)}) collective-permute-start(f32[1,272]{1,0:T(1,128)} %source.1.src_ref), channel_id=1, source_target_pairs={{0,16},{16,0},{1,17},{17,1},{2,18},{18,2},{3,19},{19,3},{4,20},{20... | collective-permute-start | bytes 3272 | tf_op jit(solution)/shard_map/ppermute | solution.py:287
  24.8 1.6 %copy-start.1 = (f32[272,2048]{1,0:T(8,128)S(1)}, f32[272,2048]{1,0:T(8,128)}, u32[]{:S(2)}) copy-start(f32[272,2048]{1,0:T(8,128)} %fa_ref.7) | copy-start | bytes 6684676
  26.5 0.7 copy-start.3
  37.4 38.2 %collective-permute-start.7 = (f32[16,72,128]{2,1,0:T(8,128)}, f32[16,72,128]{2,1,0:T(8,128)}, u32[]{:S(2)}, u32[]{:S(2)}) collective-permute-start(f32[16,72,128]{2,1,0:T(8,128)} %bins.4), channel_id=1, source_target_pairs={{0,64},{32,96},{64,0},{96,32},{1,65},{33,97},{65,1},{97,33},{2,66}... | collective-permute-start | bytes 1769480 | tf_op jit(solution)/shard_map/ppermute | solution.py:270
  50.7 13.6 %copy-start.4 = (f32[1,272]{1,0:T(1,128)S(1)}, f32[1,272]{1,0:T(1,128)}, u32[]{:S(2)}) copy-start(f32[1,272]{1,0:T(1,128)} %source.1.src_ref) | copy-start | bytes 3268
  50.7 24.9 %collective-permute-start.8 = (f32[16,72,128]{2,1,0:T(8,128)}, f32[16,72,128]{2,1,0:T(8,128)}, u32[]{:S(2)}, u32[]{:S(2)}) collective-permute-start(f32[16,72,128]{2,1,0:T(8,128)} %bins.5), channel_id=1, source_target_pairs={{0,32},{32,64},{64,96},{96,0},{1,33},{33,65},{65,97},{97,1},{2,34}... | collective-permute-start | bytes 1769480 | tf_op jit(solution)/shard_map/ppermute | solution.py:270
  61.6 15.3 %collective-permute-start.9 = (f32[16,72,128]{2,1,0:T(8,128)}, f32[16,72,128]{2,1,0:T(8,128)}, u32[]{:S(2)}, u32[]{:S(2)}) collective-permute-start(f32[16,72,128]{2,1,0:T(8,128)} %bins.6), channel_id=1, source_target_pairs={{0,96},{32,0},{64,32},{96,64},{1,97},{33,1},{65,33},{97,65},{2,98}... | collective-permute-start | bytes 1769480 | tf_op jit(solution)/shard_map/ppermute | solution.py:270
  64.3 1.6 %copy-start.2 = (f32[272,2048]{1,0:T(8,128)S(1)}, f32[272,2048]{1,0:T(8,128)}, u32[]{:S(2)}) copy-start(f32[272,2048]{1,0:T(8,128)} %fa_ref.7) | copy-start | bytes 6684676
  78.5 7.7 %collective-permute-start.10 = (f32[4,72,128]{2,1,0:T(8,128)S(1)}, f32[4,72,128]{2,1,0:T(8,128)S(1)}, u32[]{:S(2)}, u32[]{:S(2)}) collective-permute-start(f32[4,72,128]{2,1,0:T(8,128)S(1)} %get-tuple-element.9), channel_id=1, source_target_pairs={{0,8},{4,12},{8,0},{12,4},{1,9},{5,13},{9,1},{13,5},{2,10},{6,14},... | collective-permute-start | bytes 442376 | tf_op jit(solution)/shard_map/ppermute | solution.py:270
  78.7 7.6 %collective-permute-start.12 = (f32[4,72,128]{2,1,0:T(8,128)S(1)}, f32[4,72,128]{2,1,0:T(8,128)S(1)}, u32[]{:S(2)}, u32[]{:S(2)}) collective-permute-start(f32[4,72,128]{2,1,0:T(8,128)S(1)} %get-tuple-element.10), channel_id=1, source_target_pairs={{0,12},{4,0},{8,4},{12,8},{1,13},{5,1},{9,5},{13,9},{2,14},{6,2},{... | collective-permute-start | bytes 442376 | tf_op jit(solution)/shard_map/ppermute | solution.py:270
  79.7 8.0 %collective-permute-start.11 = (f32[4,72,128]{2,1,0:T(8,128)S(1)}, f32[4,72,128]{2,1,0:T(8,128)S(1)}, u32[]{:S(2)}, u32[]{:S(2)}) collective-permute-start(f32[4,72,128]{2,1,0:T(8,128)S(1)} %get-tuple-element.11), channel_id=1, source_target_pairs={{0,4},{4,8},{8,12},{12,0},{1,5},{5,9},{9,13},{13,1},{2,6},{6,10},{... | collective-permute-start | bytes 442376 | tf_op jit(solution)/shard_map/ppermute | solution.py:270
  87.8 5.5 %collective-permute-start.13 = (f32[72,128]{1,0:T(8,128)S(1)}, f32[72,128]{1,0:T(8,128)S(1)}, u32[]{:S(2)}, u32[]{:S(2)}) collective-permute-start(f32[72,128]{1,0:T(8,128)S(1)} %get-tuple-element.12), channel_id=1, source_target_pairs={{0,2},{1,3},{2,0},{3,1},{4,6},{5,7},{6,4},{7,5},{8,10},{9,11},{10,... | collective-permute-start | bytes 110600 | tf_op jit(solution)/shard_map/ppermute | solution.py:270
  88.2 5.6 %collective-permute-start.15 = (f32[72,128]{1,0:T(8,128)S(1)}, f32[72,128]{1,0:T(8,128)S(1)}, u32[]{:S(2)}, u32[]{:S(2)}) collective-permute-start(f32[72,128]{1,0:T(8,128)S(1)} %get-tuple-element.13), channel_id=1, source_target_pairs={{0,3},{1,0},{2,1},{3,2},{4,7},{5,4},{6,5},{7,6},{8,11},{9,8},{10,9... | collective-permute-start | bytes 110600 | tf_op jit(solution)/shard_map/ppermute | solution.py:270
  90.7 5.2 %collective-permute-start.14 = (f32[72,128]{1,0:T(8,128)S(1)}, f32[72,128]{1,0:T(8,128)S(1)}, u32[]{:S(2)}, u32[]{:S(2)}) collective-permute-start(f32[72,128]{1,0:T(8,128)S(1)} %get-tuple-element.14), channel_id=1, source_target_pairs={{0,1},{1,2},{2,3},{3,0},{4,5},{5,6},{6,7},{7,4},{8,9},{9,10},{10,1... | collective-permute-start | bytes 110600 | tf_op jit(solution)/shard_map/ppermute | solution.py:270

commit v4 on v2

--- a/solution.py
+++ b/solution.py
@@ -11,9 +11,9 @@
 LANES = 640
 RADIX = 15
 ROWS = 36
-BLOCK = 128
+UNROLL = 16
 SAMPLES = 512
-CHIP = ("x", "y", "z")
+ORDER = (("x", "y", "z"), ("z", "x", "y"))
 AXIAL = ("x", "core")
 AZIMUTHAL = ("y", "z")
 MEAN_FLOW = 0.5
@@ -148,39 +148,47 @@
     )
 
 
-def half_kernel(core_ref, delay_ref, fraction_ref, delay_out, fraction_out):
-    delay_out[...] = delay_ref[...]
-    fraction_out[...] = fraction_ref[...]
-
-
-def other_half(core, delay, fraction):
-    width = delay.shape[1] // 8
-    taken = pl.BlockSpec((SLOTS, width), lambda n, c: (0, 2 * n + 1 - c[0]))
-    given = pl.BlockSpec((SLOTS, width), lambda n, c: (0, n))
+def turn_kernel(core_ref, own_delay, own_fraction, other_delay, other_fraction, own_ref, other_ref):
+    for delay, fraction, out in (
+        (own_delay, own_fraction, own_ref),
+        (other_delay, other_fraction, other_ref),
+    ):
+        for at in (0, 128):
+            rows = slice(at, at + 128)
+            for base in (0, 128):
+                out[rows, base : base + 128] = delay[base : base + 128, rows].astype(jnp.float32).T
+                out[rows, 256 + base : 384 + base] = fraction[base : base + 128, rows].T
+            rest = [
+                delay[256:272, rows].astype(jnp.float32),
+                fraction[256:272, rows],
+                jnp.zeros((96, 128), jnp.float32),
+            ]
+            out[rows, 512:640] = jnp.concatenate(rest, axis=0).T
+
+
+def turned(core, delay, fraction):
+    mine = pl.BlockSpec((SLOTS, 256), lambda n, c: (0, 2 * n + c[0]))
+    other = pl.BlockSpec((SLOTS, 256), lambda n, c: (0, 2 * n + 1 - c[0]))
+    shape = jax.ShapeDtypeStruct((1024, LANES), jnp.float32)
     return pl.pallas_call(
-        half_kernel,
+        turn_kernel,
         grid_spec=pltpu.PrefetchScalarGridSpec(
-            num_scalar_prefetch=1, grid=(4,), in_specs=[taken] * 2, out_specs=[given] * 2
+            num_scalar_prefetch=1,
+            grid=(4,),
+            in_specs=[mine, mine, other, other],
+            out_specs=[pl.BlockSpec((256, LANES), lambda n, c: (n, 0))] * 2,
         ),
-        out_shape=[
-            jax.ShapeDtypeStruct((SLOTS, 4 * width), jnp.int32),
-            jax.ShapeDtypeStruct((SLOTS, 4 * width), jnp.float32),
-        ],
-        name="other_half",
-    )(core, delay, fraction)
-
-
-def bins_kernel(core_ref, src_ref, src_b_ref, da_ref, fa_ref, db_ref, fb_ref, out_ref, d_t, f_t, hi_s, *, unroll=2):
-    def flip(a_ref, b_ref, dst, cast):
-        for n, (r, base) in enumerate(((a_ref, 0), (a_ref, 128), (b_ref, 0), (b_ref, 128))):
-            dst[:, n * 128:(n + 1) * 128] = cast(r[base:base + 128, :]).T
-        rest = jnp.concatenate([cast(a_ref[256:272, :]), cast(b_ref[256:272, :]), jnp.zeros((96, 128), jnp.float32)], axis=0)
-        dst[:, 512:640] = rest.T
-    flip(da_ref, db_ref, d_t, lambda v: v.astype(jnp.float32))
-    flip(fa_ref, fb_ref, f_t, lambda v: v)
+        out_shape=[shape, shape],
+        compiler_params=pltpu.CompilerParams(vmem_limit_bytes=32 * 1024 * 1024),
+        name="turned",
+    )(core, delay, fraction, delay, fraction)
+
+
+def bins_kernel(part_ref, src_ref, src_b_ref, own_ref, sib_ref, out_ref, hi_s):
     src = jnp.concatenate(
         [src_ref[:, :256], src_b_ref[:, :256], src_ref[:, 256:], src_b_ref[:, 256:],
          jnp.zeros((1, 96), jnp.float32)], axis=1)
+    first16 = lax.broadcasted_iota(jnp.int32, (8, 128), 1) < 16
     row16 = lax.broadcasted_iota(jnp.int32, (16, LANES), 0)
     half = (row16 >= 8).astype(jnp.float32)
     count_lo = row16.astype(jnp.float32).astype(jnp.bfloat16)
@@ -192,9 +200,13 @@
     diag8 = lane8 == lax.broadcasted_iota(jnp.int32, (8, 128), 0)
 
     def group(g, slot):
-        rows = pl.ds(pl.multiple_of(g * 8, 8), 8)
-        k = d_t[rows, :]
-        f = f_t[rows, :]
+        row = part_ref[0] + (g // 8) * part_ref[1] + (g // 2 % 4) * part_ref[2] + (g % 2) * 8
+        rows = pl.ds(pl.multiple_of(row, 8), 8)
+        last, last_b = own_ref[rows, 512:], sib_ref[rows, 512:]
+        last_k = jnp.where(first16, last, pltpu.roll(last_b, 16, 1))
+        last_f = jnp.where(first16, pltpu.roll(last, 112, 1), last_b)
+        k = jnp.concatenate([own_ref[rows, :256], sib_ref[rows, :256], last_k], axis=1)
+        f = jnp.concatenate([own_ref[rows, 256:512], sib_ref[rows, 256:512], last_f], axis=1)
         c = src * (25.6 / (512.0 + k))
         up = f * c
         low = c - up
@@ -233,42 +245,68 @@
         extra = [jnp.sum(jnp.where(diag8, r[256 + 8 * e:264 + 8 * e], 0.0), axis=0, keepdims=True) for e in range(4)]
         return jnp.concatenate([main] + extra, axis=0)
 
-    def pair(p, _):
-        two = [group(2 * p + t, t) for t in range(2)]
-        out_ref[p] = jnp.concatenate(two, axis=0)
+    def several(p, _):
+        for t in range(0, UNROLL, 2):
+            g = UNROLL * p + t
+            out_ref[g // 2] = jnp.concatenate([group(g, t), group(g + 1, t + 1)], axis=0)
         return 0
-    lax.fori_loop(0, BLOCK // 16, pair, 0, unroll=False)
-
-def bins(core, src, src_b, delay, frac, delay_b, frac_b, first, blocks):
-    own = lambda n, c: (0, ((n + first) // 2) * 4 + c[0] * 2 + (n + first) % 2)
-    sib = lambda n, c: (0, n + first)
-    spec = pl.BlockSpec((SLOTS, BLOCK), own)
-    spec_b = pl.BlockSpec((SLOTS, BLOCK), sib)
+
+    lax.fori_loop(0, 32 // UNROLL, several, 0)
+
+
+def bins(part, src, src_b, own, sibling):
+    vmem = pl.BlockSpec(memory_space=pltpu.VMEM)
     return pl.pallas_call(
         bins_kernel,
-        grid_spec=pltpu.PrefetchScalarGridSpec(
-            num_scalar_prefetch=1, grid=(blocks,),
-            in_specs=[pl.BlockSpec((1, SLOTS), lambda n, c: (0, 0))] * 2 + [spec, spec, spec_b, spec_b],
-            out_specs=pl.BlockSpec((8, 2 * ROWS, 128), lambda n, c: (n, 0, 0)),
-            scratch_shapes=[pltpu.VMEM((BLOCK, LANES), jnp.float32), pltpu.VMEM((BLOCK, LANES), jnp.float32), pltpu.VMEM((2, 8, LANES), jnp.float32)],
+        in_specs=[pl.BlockSpec(memory_space=pltpu.SMEM)] + [vmem] * 4,
+        out_specs=vmem,
+        scratch_shapes=[pltpu.VMEM((UNROLL, 8, LANES), jnp.float32)],
+        out_shape=jax.ShapeDtypeStruct((16, 2 * ROWS, 128), jnp.float32),
+        compiler_params=pltpu.CompilerParams(vmem_limit_bytes=32 * 1024 * 1024),
+        cost_estimate=pl.CostEstimate(
+            flops=32 * 2 * 288 * 256 * LANES, bytes_accessed=8 * 256 * LANES, transcendentals=0
         ),
-        out_shape=jax.ShapeDtypeStruct((8 * blocks, 2 * ROWS, 128), jnp.float32),
-        compiler_params=pltpu.CompilerParams(vmem_limit_bytes=48 * 1024 * 1024),
         name="bins",
-    )(core, src, src_b, delay, frac, delay_b, frac_b)
+    )(part, src, src_b, own, sibling)
+
+
+def shifted(array, phase, step):
+    moves = []
+    for i in range(128):
+        at = {"x": i // 32, "core": i // 16 % 2, "y": i // 4 % 4, "z": i % 4}
+        axis = ORDER[at["core"]][phase]
+        at[axis] = (at[axis] + step) % 4
+        moves.append((i, at["x"] * 32 + at["core"] * 16 + at["y"] * 4 + at["z"]))
+    return lax.ppermute(array, AXIAL + AZIMUTHAL, moves)
+
+
+def summed(source, source_b, own, sibling):
+    core = lax.axis_index("core")
+    pick = lambda of: jnp.where(core == 0, of(ORDER[0]), of(ORDER[1]))
+    here = [pick(lambda order: lax.axis_index(order[phase])) for phase in range(3)]
+    rows = {"x": 256, "y": 64, "z": 16}
+    steps = [pick(lambda order: rows[order[phase]]) for phase in range(3)]
+    got = []
+    for d in (2, 1, 3, 0):
+        part = jnp.stack([(here[0] + d) % 4 * steps[0], steps[1], steps[2]]).astype(jnp.int32)
+        sums = bins(part, source, source_b, own, sibling)
+        got.append(shifted(sums, 0, d) if d else sums)
+    total = (got[0] + got[1] + got[2] + got[3]).reshape(4, 4, 2 * ROWS, 128)
+    for phase in (1, 2):
+        block = lambda d: lax.dynamic_index_in_dim(total, (here[phase] + d) % 4, 0, keepdims=False)
+        got = [shifted(block(d), phase, d) for d in (2, 1, 3)]
+        total = block(0) + got[0] + got[1] + got[2]
+    return total
 
 
 def local(state, surf_index, surf_count, delay, fraction):
     core = lax.axis_index("core").reshape(1)
     swap = [(0, 1), (1, 0)]
-    delay_b, fraction_b = other_half(core, delay, fraction)
-    delay_b = lax.ppermute(delay_b, "core", swap)
-    fraction_b = lax.ppermute(fraction_b, "core", swap)
+    own, other = turned(core, delay, fraction)
+    sibling = lax.ppermute(other, "core", swap)
     source = slot_source(state, surf_index, surf_count)
     source_b = lax.ppermute(source, "core", swap)
-    sums = bins(core, source, source_b, delay, fraction, delay_b, fraction_b, 0, 8)
-    parts = lax.all_to_all(sums, CHIP, 0, 0, tiled=True)
-    total = jnp.sum(parts, axis=0)
+    total = summed(source, source_b, own, sibling)
     total = total.reshape(2, ROWS, 16, 8).transpose(0, 3, 1, 2).reshape(16, ROWS, 16)
     carry = jnp.pad(total[:, :34, 15:], ((0, 0), (1, 0), (0, 14)))
     return (total[:, :35, :RADIX] + carry).reshape(16, 35 * RADIX)[:, :SAMPLES]

time: 104 us -> 85.1 us (0.82)
  blocking collectives: 42.7 us -> 0 us
  starting transfers between devices: 11.2 us -> 26.3 us
  waiting for transfers between devices: 3.18 us -> 15.4 us
  Pallas kernels: 42.4 us -> 33.1 us
  local copies, waits for them, and re-layouts: 3.68 us -> 6.97 us
  other arithmetic: 0.23 us -> 1.95 us
    all_to_all x1 -> x0, blocking collectives: 42.7 us -> none  [local(): parts = lax.all_to_all(sums, CHIP, 0, 0, tiled=True)]
    ppermute x2 -> x10, starting transfers between devices: 0.51 us -> 14.7 us  [the longest x9 14.7 us: shifted(): return lax.ppermute(array, AXIAL + AZIMUTHAL, moves)]
    ppermute x2 -> x10, waiting for transfers between devices: 0.01 us -> 14.2 us  [the longest x9 14.2 us: shifted(): return lax.ppermute(array, AXIAL + AZIMUTHAL, moves)]
    pallas_call x2 -> x5, Pallas kernels: 38.4 us -> 29.1 us  [the longest x4 25.9 us: bins(): pl.pallas_call(bins_kernel, in_specs=[pl.BlockSpec(memory_space=pltpu.SME...]
    unnamed x14 -> x18, local copies, waits for them, and re-layouts: 1.85 us -> 5.07 us
    add x0 -> x3, other arithmetic: none -> 1.57 us  [the longest x1 1.52 us: summed(): total = (got[0] + got[1] + got[2] + got[3]).reshape(4, 4, 2 * ROWS, 128)]
    ppermute x4, waiting for transfers between devices: 1.82 us -> 0.29 us  [around(): return (lax.ppermute(tile, axes, up), lax.ppermute(tile, axes, down))]
    ppermute x1, starting transfers between devices: 0.01 us -> 1.18 us  [local(): source_b = lax.ppermute(source, 'core', swap)]
  transfers between devices with their start and end apart: 7 -> 15, of which waited for: 3 -> 9; matrix products, arithmetic and copies ran while one was open for 1% -> 1% of each run, Pallas kernels for 4% -> 28%
where the time goes in v4:
time: 85.1 us; the launch traced here: 84.6 us
  Pallas kernels  33.1 us (39%)
  starting transfers between devices  26.3 us (31%)
  waiting for transfers between devices  15.4 us (18%)
  local copies, waits for them, and re-layouts  6.97 us (8%)
  other arithmetic  1.95 us (2%)
    pallas_call x4, Pallas kernels, bins(): pl.pallas_call(bins_kernel, in_specs=[pl.BlockSpec(memory_space=pltpu.SME...  25.9 us
    ppermute x9, starting transfers between devices, shifted(): return lax.ppermute(array, AXIAL + AZIMUTHAL, moves)  14.7 us
    ppermute x9, waiting for transfers between devices, shifted(): return lax.ppermute(array, AXIAL + AZIMUTHAL, moves)  14.2 us
    ppermute x4, starting transfers between devices, around(): return (lax.ppermute(tile, axes, up), lax.ppermute(tile, axes, down))  10.4 us
    unnamed x18, local copies, waits for them, and re-layouts  5.07 us
    pallas_call x1, Pallas kernels, turned(): pl.pallas_call(turn_kernel, grid_spec=pltpu.PrefetchScalarGridSpec(num_sc...  3.26 us
    pallas_call x1, Pallas kernels, slot_source(): pl.pallas_call(source_kernel, in_specs=[vmem] * 7 + [pl.BlockSpec(memory_...  2.11 us
    pallas_call x1, Pallas kernels, slot_source(): pl.pallas_call(tile_kernel, in_specs=[vmem], out_specs=vmem, out_shape=ja...  1.85 us
  transfers between devices with their start and end apart: 15, of which 9 were waited for; matrix products, arithmetic and copies ran while one was open for 1% of the time, Pallas kernels for 28%

profile of v4, /device:TPU:0, one launch (start us, length us, event | category | flops | bytes accessed | tf_op | source)
XLA Modules:
  0.0 84.6 jit_solution(3173910280658658984)
XLA Ops:
  0.0 1.6 %copy-done = s32[272,2048]{1,0:T(8,128)S(1)} copy-done((s32[272,2048]{1,0:T(8,128)S(1)}, s32[272,2048]{1,0:T(8,128)}, u32[]{:S(2)}) %copy-start) | copy-done | bytes 2228248
  1.6 1.6 %copy-done.1 = f32[272,2048]{1,0:T(8,128)S(1)} copy-done((f32[272,2048]{1,0:T(8,128)S(1)}, f32[272,2048]{1,0:T(8,128)}, u32[]{:S(2)}) %copy-start.1) | copy-done | bytes 2228248
  3.3 3.3 %turned.1 = (f32[1024,640]{1,0:T(8,128)S(1)}, f32[1024,640]{1,0:T(8,128)}) custom-call(s32[1]{0:T(128)} %bitcast.4.core_ref, s32[272,2048]{1,0:T(8,128)S(1)} %copy-done, f32[272,2048]{1,0:T(8,128)S(1)} %copy-done.1, s32[272,2048]{1,0:T(8,128)S(1)} %copy-done, f32[272,2048]{1,0:T(8,128)S(1)} %copy-done.1), custom_call_target="tpu_custom_call" | custom-call | tf_op jit(solution)/shard_map/turned/pallas_call | solution.py:173
  6.5 1.8 %tile.1.own_ref = f32[8,128]{1,0:T(8,128)} custom-call(f32[5,64,128]{2,1,0:T(8,128)} %bitcast.42), custom_call_target="tpu_custom_call" | custom-call | tf_op jit(solution)/shard_map/tile/pallas_call | solution.py:124
  8.4 2.4 %collective-permute-start = (f32[8,128]{1,0:T(8,128)}, f32[8,128]{1,0:T(8,128)S(1)}, u32[]{:S(2)}, u32[]{:S(2)}) collective-permute-start(f32[8,128]{1,0:T(8,128)} %tile.1.own_ref), channel_id=1, source_target_pairs={{0,16},{16,32},{32,48},{48,64},{64,80},{80,96},{96,112},{1,17},{17... | collective-permute-start | bytes 12296 | tf_op jit(solution)/shard_map/ppermute | solution.py:135
  10.8 1.3 %collective-permute-start.1 = (f32[8,128]{1,0:T(8,128)}, f32[8,128]{1,0:T(8,128)S(1)}, u32[]{:S(2)}, u32[]{:S(2)}) collective-permute-start(f32[8,128]{1,0:T(8,128)} %tile.1.own_ref), channel_id=1, source_target_pairs={{16,0},{32,16},{48,32},{64,48},{80,64},{96,80},{112,96},{17,1},{33... | collective-permute-start | bytes 12296 | tf_op jit(solution)/shard_map/ppermute | solution.py:135
  12.1 2.1 %collective-permute-start.2 = (f32[8,128]{1,0:T(8,128)}, f32[8,128]{1,0:T(8,128)S(1)}, u32[]{:S(2)}, u32[]{:S(2)}) collective-permute-start(f32[8,128]{1,0:T(8,128)} %tile.1.own_ref), channel_id=1, source_target_pairs={{0,1},{1,2},{2,3},{3,4},{4,5},{5,6},{6,7},{7,8},{8,9},{9,10},{10,1... | collective-permute-start | bytes 12296 | tf_op jit(solution)/shard_map/ppermute | solution.py:135
  14.2 4.7 %collective-permute-start.3 = (f32[8,128]{1,0:T(8,128)}, f32[8,128]{1,0:T(8,128)S(1)}, u32[]{:S(2)}, u32[]{:S(2)}) collective-permute-start(f32[8,128]{1,0:T(8,128)} %tile.1.own_ref), channel_id=1, source_target_pairs={{1,0},{2,1},{3,2},{4,3},{5,4},{6,5},{7,6},{8,7},{9,8},{10,9},{11,1... | collective-permute-start | bytes 12296 | tf_op jit(solution)/shard_map/ppermute | solution.py:135
  18.8 0.1 add_add_fusion.3.part_ref
  18.9 0.1 add_add_fusion.1.part_ref
  19.0 0.6 reshape.22.index_ref
  20.2 0.3 collective-permute-done.2.by_ref
  20.5 0.3 copy-done.4
  20.8 0.0 copy-done.5
  20.8 0.3 copy-done.6
  21.1 0.6 copy-done.7
  21.7 2.1 %source.1.src_ref = f32[1,272]{1,0:T(1,128)} custom-call(f32[1024,64]{1,0:T(8,128)} %constant.110.clone.map_ref, f32[8,128]{1,0:T(8,128)} %tile.1.own_ref, f32[8,128]{1,0:T(8,128)} %copy-done.4, f32[8,128]{1,0:T(8,128)} %copy-done.5, f32[8,128]{1,0:T(8,128)} %copy-done.6, f32[8,128]{1,0:T(8,128)} %copy-done.7, s32[1,272]{1,0:T(1,128)} %reshape.22.index_ref, ...), custom_call_target="tpu_custom_call" | custom-call | tf_op jit(solution)/shard_map/source/pallas_call | solution.py:139
  23.8 1.2 %collective-permute-start.4 = (f32[1,272]{1,0:T(1,128)}, f32[1,272]{1,0:T(1,128)S(1)}, u32[]{:S(2)}, u32[]{:S(2)}) collective-permute-start(f32[1,272]{1,0:T(1,128)} %source.1.src_ref), channel_id=1, source_target_pairs={{0,16},{16,0},{1,17},{17,1},{2,18},{18,2},{3,19},{19,3},{4,20},{20... | collective-permute-start | bytes 3272 | tf_op jit(solution)/shard_map/ppermute | solution.py:308
  25.0 0.1 add_add_fusion.2.part_ref
  25.1 1.0 %collective-permute-done.4.src_b_ref = f32[1,272]{1,0:T(1,128)S(1)} collective-permute-done((f32[1,272]{1,0:T(1,128)}, f32[1,272]{1,0:T(1,128)S(1)}, u32[]{:S(2)}, u32[]{:S(2)}) %collective-permute-start.4) | collective-permute-done | bytes 1120 | tf_op jit(solution)/shard_map/ppermute | solution.py:308
  26.0 0.6 copy-done.2
  26.7 6.0 %bins.6 = f32[16,72,128]{2,1,0:T(8,128)S(1)} custom-call(s32[3]{0:T(128)S(1)} %add_add_fusion.3.part_ref, f32[1,272]{1,0:T(1,128)S(1)} %copy-done.2, f32[1,272]{1,0:T(1,128)S(1)} %collective-permute-done.4.src_b_ref, f32[1024,640]{1,0:T(8,128)S(1)} %get-tuple-element.7.own_ref, f32[1024,640]{1,0:T(8,128)} %collective-permute-done.5.sib_ref), custom_call_target="tpu_custom_call" | custom-call | flops 3019898880 | bytes 1310720 | tf_op jit(solution)/shard_map/bins/pallas_call | solution.py:259
  32.7 3.8 %collective-permute-start.8 = (f32[16,72,128]{2,1,0:T(8,128)S(1)}, f32[16,72,128]{2,1,0:T(8,128)}, u32[]{:S(2)}, u32[]{:S(2)}) collective-permute-start(f32[16,72,128]{2,1,0:T(8,128)S(1)} %bins.6), channel_id=1, source_target_pairs={{0,96},{1,97},{2,98},{3,99},{4,100},{5,101},{6,102},{7,103},{8,104... | collective-permute-start | bytes 1769480 | tf_op jit(solution)/shard_map/ppermute | solution.py:280
  36.5 6.9 %bins.4 = f32[16,72,128]{2,1,0:T(8,128)} custom-call(s32[3]{0:T(128)S(1)} %add_add_fusion.1.part_ref, f32[1,272]{1,0:T(1,128)S(1)} %copy-done.2, f32[1,272]{1,0:T(1,128)S(1)} %collective-permute-done.4.src_b_ref, f32[1024,640]{1,0:T(8,128)S(1)} %get-tuple-element.7.own_ref, f32[1024,640]{1,0:T(8,128)} %collective-permute-done.5.sib_ref), custom_call_target="tpu_custom_call" | custom-call | flops 3019898880 | bytes 1310720 | tf_op jit(solution)/shard_map/bins/pallas_call | solution.py:259
  43.4 0.8 collective-permute-start.6
  44.2 6.9 %bins.5 = f32[16,72,128]{2,1,0:T(8,128)} custom-call(s32[3]{0:T(128)S(1)} %add_add_fusion.2.part_ref, f32[1,272]{1,0:T(1,128)S(1)} %copy-done.2, f32[1,272]{1,0:T(1,128)S(1)} %collective-permute-done.4.src_b_ref, f32[1024,640]{1,0:T(8,128)S(1)} %get-tuple-element.7.own_ref, f32[1024,640]{1,0:T(8,128)} %collective-permute-done.5.sib_ref), custom_call_target="tpu_custom_call" | custom-call | flops 3019898880 | bytes 1310720 | tf_op jit(solution)/shard_map/bins/pallas_call | solution.py:259
  51.1 0.9 %collective-permute-start.7 = (f32[16,72,128]{2,1,0:T(8,128)}, f32[16,72,128]{2,1,0:T(8,128)}, u32[]{:S(2)}, u32[]{:S(2)}) collective-permute-start(f32[16,72,128]{2,1,0:T(8,128)} %bins.5), channel_id=1, source_target_pairs={{0,32},{1,33},{2,34},{3,35},{4,36},{5,37},{6,38},{7,39},{8,40},{9,... | collective-permute-start | bytes 1769480 | tf_op jit(solution)/shard_map/ppermute | solution.py:280
  52.0 0.1 add_add_fusion.4.part_ref
  52.1 6.1 %bins.7 = f32[16,72,128]{2,1,0:T(8,128)S(1)} custom-call(s32[3]{0:T(128)S(1)} %add_add_fusion.4.part_ref, f32[1,272]{1,0:T(1,128)S(1)} %copy-done.3, f32[1,272]{1,0:T(1,128)S(1)} %collective-permute-done.4.src_b_ref, f32[1024,640]{1,0:T(8,128)S(1)} %get-tuple-element.7.own_ref, f32[1024,640]{1,0:T(8,128)} %collective-permute-done.5.sib_ref), custom_call_target="tpu_custom_call" | custom-call | flops 3019898880 | bytes 1310720 | tf_op jit(solution)/shard_map/bins/pallas_call | solution.py:259
  58.2 4.4 %collective-permute-done.7 = f32[16,72,128]{2,1,0:T(8,128)} collective-permute-done((f32[16,72,128]{2,1,0:T(8,128)}, f32[16,72,128]{2,1,0:T(8,128)}, u32[]{:S(2)}, u32[]{:S(2)}) %collective-permute-start.7) | collective-permute-done | bytes 589856 | tf_op jit(solution)/shard_map/ppermute | solution.py:280
  62.5 1.5 %add_add_fusion = f32[16,72,128]{2,1,0:T(8,128)S(1)} fusion(f32[16,72,128]{2,1,0:T(8,128)S(1)} %bins.7, f32[16,72,128]{2,1,0:T(8,128)} %collective-permute-done.8, f32[16,72,128]{2,1,0:T(8,128)} %collective-permute-done.6, f32[16,72,128]{2,1,0:T(8,128)} %collective-permute-done.7), kind=kLoop, calls=%fused_computation | loop fusion | flops 442368 | bytes 2949120 | tf_op jit(solution)/shard_map/add | solution.py:294
  64.1 0.8 collective-permute-start.11
  64.9 1.3 %collective-permute-start.10 = (f32[4,72,128]{2,1,0:T(8,128)S(1)}, f32[4,72,128]{2,1,0:T(8,128)S(1)}, u32[]{:S(2)}, u32[]{:S(2)}) collective-permute-start(f32[4,72,128]{2,1,0:T(8,128)S(1)} %get-tuple-element.11), channel_id=1, source_target_pairs={{0,4},{1,5},{2,6},{3,7},{4,8},{5,9},{6,10},{7,11},{8,12},{9,13},{1... | collective-permute-start | bytes 442376 | tf_op jit(solution)/shard_map/ppermute | solution.py:280
  66.2 0.8 collective-permute-start.9
  67.0 2.3 %collective-permute-done.11 = f32[4,72,128]{2,1,0:T(8,128)S(1)} collective-permute-done((f32[4,72,128]{2,1,0:T(8,128)S(1)}, f32[4,72,128]{2,1,0:T(8,128)S(1)}, u32[]{:S(2)}, u32[]{:S(2)}) %collective-permute-start.11) | collective-permute-done | bytes 147488 | tf_op jit(solution)/shard_map/ppermute | solution.py:280
  69.3 2.0 %collective-permute-done.10 = f32[4,72,128]{2,1,0:T(8,128)S(1)} collective-permute-done((f32[4,72,128]{2,1,0:T(8,128)S(1)}, f32[4,72,128]{2,1,0:T(8,128)S(1)}, u32[]{:S(2)}, u32[]{:S(2)}) %collective-permute-start.10) | collective-permute-done | bytes 147488 | tf_op jit(solution)/shard_map/ppermute | solution.py:280
  71.3 1.6 %collective-permute-done.9 = f32[4,72,128]{2,1,0:T(8,128)S(1)} collective-permute-done((f32[4,72,128]{2,1,0:T(8,128)S(1)}, f32[4,72,128]{2,1,0:T(8,128)S(1)}, u32[]{:S(2)}, u32[]{:S(2)}) %collective-permute-start.9) | collective-permute-done | bytes 147488 | tf_op jit(solution)/shard_map/ppermute | solution.py:280
  72.9 4.7 %collective-permute-start.14 = (f32[72,128]{1,0:T(8,128)S(1)}, f32[72,128]{1,0:T(8,128)S(1)}, u32[]{:S(2)}, u32[]{:S(2)}) collective-permute-start(f32[72,128]{1,0:T(8,128)S(1)} %get-tuple-element.13), channel_id=1, source_target_pairs={{0,3},{1,0},{2,1},{3,2},{4,7},{5,4},{6,5},{7,6},{8,11},{9,8},{10,9... | collective-permute-start | bytes 110600 | tf_op jit(solution)/shard_map/ppermute | solution.py:280
  77.7 1.5 %collective-permute-start.12 = (f32[72,128]{1,0:T(8,128)S(1)}, f32[72,128]{1,0:T(8,128)S(1)}, u32[]{:S(2)}, u32[]{:S(2)}) collective-permute-start(f32[72,128]{1,0:T(8,128)S(1)} %get-tuple-element.12), channel_id=1, source_target_pairs={{0,2},{1,3},{2,0},{3,1},{4,6},{5,7},{6,4},{7,5},{8,10},{9,11},{10,... | collective-permute-start | bytes 110600 | tf_op jit(solution)/shard_map/ppermute | solution.py:280
  79.2 0.1 collective-permute-done.14
  79.3 3.5 %collective-permute-done.13 = f32[72,128]{1,0:T(8,128)S(1)} collective-permute-done((f32[72,128]{1,0:T(8,128)S(1)}, f32[72,128]{1,0:T(8,128)S(1)}, u32[]{:S(2)}, u32[]{:S(2)}) %collective-permute-start.13) | collective-permute-done | bytes 36896 | tf_op jit(solution)/shard_map/ppermute | solution.py:280
  82.8 0.4 collective-permute-done.12
  83.2 0.1 copy.9
  83.3 0.1 reshape.25
  83.5 0.1 slice_add_fusion
  83.6 0.2 copy.11
  83.9 0.1 reshape.27
  84.0 0.6 slice.14
  (25 shorter events, 0.2 us)
Async XLA Ops:
  0.0 1.6 %copy-start = (s32[272,2048]{1,0:T(8,128)S(1)}, s32[272,2048]{1,0:T(8,128)}, u32[]{:S(2)}) copy-start(s32[272,2048]{1,0:T(8,128)} %other_delay.1) | copy-start | bytes 6684676
  1.6 1.6 %copy-start.1 = (f32[272,2048]{1,0:T(8,128)S(1)}, f32[272,2048]{1,0:T(8,128)}, u32[]{:S(2)}) copy-start(f32[272,2048]{1,0:T(8,128)} %other_fraction.1) | copy-start | bytes 6684676
  3.3 15.7 %copy-start.8 = (s32[272]{0:T(512)S(1)}, s32[272]{0:T(512)}, u32[]{:S(2)}) copy-start(s32[272]{0:T(512)} %param.7) | copy-start | bytes 3268
  6.5 19.5 %collective-permute-start.5 = (f32[1024,640]{1,0:T(8,128)}, f32[1024,640]{1,0:T(8,128)}, u32[]{:S(2)}, u32[]{:S(2)}) collective-permute-start(f32[1024,640]{1,0:T(8,128)} %get-tuple-element.8), channel_id=1, source_target_pairs={{0,16},{16,0},{1,17},{17,1},{2,18},{18,2},{3,19},{19,3},{4,20},{20... | collective-permute-start | bytes 7864328 | tf_op jit(solution)/shard_map/ppermute | solution.py:306
  8.4 11.8 %collective-permute-start = (f32[8,128]{1,0:T(8,128)}, f32[8,128]{1,0:T(8,128)S(1)}, u32[]{:S(2)}, u32[]{:S(2)}) collective-permute-start(f32[8,128]{1,0:T(8,128)} %tile.1.own_ref), channel_id=1, source_target_pairs={{0,16},{16,32},{32,48},{48,64},{64,80},{80,96},{96,112},{1,17},{17... | collective-permute-start | bytes 12296 | tf_op jit(solution)/shard_map/ppermute | solution.py:135
  10.8 9.4 %collective-permute-start.1 = (f32[8,128]{1,0:T(8,128)}, f32[8,128]{1,0:T(8,128)S(1)}, u32[]{:S(2)}, u32[]{:S(2)}) collective-permute-start(f32[8,128]{1,0:T(8,128)} %tile.1.own_ref), channel_id=1, source_target_pairs={{16,0},{32,16},{48,32},{64,48},{80,64},{96,80},{112,96},{17,1},{33... | collective-permute-start | bytes 12296 | tf_op jit(solution)/shard_map/ppermute | solution.py:135
  12.1 8.4 %collective-permute-start.2 = (f32[8,128]{1,0:T(8,128)}, f32[8,128]{1,0:T(8,128)S(1)}, u32[]{:S(2)}, u32[]{:S(2)}) collective-permute-start(f32[8,128]{1,0:T(8,128)} %tile.1.own_ref), channel_id=1, source_target_pairs={{0,1},{1,2},{2,3},{3,4},{4,5},{5,6},{6,7},{7,8},{8,9},{9,10},{10,1... | collective-permute-start | bytes 12296 | tf_op jit(solution)/shard_map/ppermute | solution.py:135
  14.2 6.4 %collective-permute-start.3 = (f32[8,128]{1,0:T(8,128)}, f32[8,128]{1,0:T(8,128)S(1)}, u32[]{:S(2)}, u32[]{:S(2)}) collective-permute-start(f32[8,128]{1,0:T(8,128)} %tile.1.own_ref), channel_id=1, source_target_pairs={{1,0},{2,1},{3,2},{4,3},{5,4},{6,5},{7,6},{8,7},{9,8},{10,9},{11,1... | collective-permute-start | bytes 12296 | tf_op jit(solution)/shard_map/ppermute | solution.py:135
  20.2 0.6 copy-start.4
  20.2 0.6 copy-start.5
  20.5 0.6 copy-start.6
  21.1 0.6 copy-start.7
  23.8 2.2 %collective-permute-start.4 = (f32[1,272]{1,0:T(1,128)}, f32[1,272]{1,0:T(1,128)S(1)}, u32[]{:S(2)}, u32[]{:S(2)}) collective-permute-start(f32[1,272]{1,0:T(1,128)} %source.1.src_ref), channel_id=1, source_target_pairs={{0,16},{16,0},{1,17},{17,1},{2,18},{18,2},{3,19},{19,3},{4,20},{20... | collective-permute-start | bytes 3272 | tf_op jit(solution)/shard_map/ppermute | solution.py:308
  26.0 0.6 copy-start.2
  32.7 25.4 %collective-permute-start.8 = (f32[16,72,128]{2,1,0:T(8,128)S(1)}, f32[16,72,128]{2,1,0:T(8,128)}, u32[]{:S(2)}, u32[]{:S(2)}) collective-permute-start(f32[16,72,128]{2,1,0:T(8,128)S(1)} %bins.6), channel_id=1, source_target_pairs={{0,96},{1,97},{2,98},{3,99},{4,100},{5,101},{6,102},{7,103},{8,104... | collective-permute-start | bytes 1769480 | tf_op jit(solution)/shard_map/ppermute | solution.py:280
  43.4 8.7 %copy-start.3 = (f32[1,272]{1,0:T(1,128)S(1)}, f32[1,272]{1,0:T(1,128)}, u32[]{:S(2)}) copy-start(f32[1,272]{1,0:T(1,128)} %source.1.src_ref) | copy-start | bytes 3268
  43.4 14.7 %collective-permute-start.6 = (f32[16,72,128]{2,1,0:T(8,128)}, f32[16,72,128]{2,1,0:T(8,128)}, u32[]{:S(2)}, u32[]{:S(2)}) collective-permute-start(f32[16,72,128]{2,1,0:T(8,128)} %bins.4), channel_id=1, source_target_pairs={{0,64},{1,65},{2,66},{3,67},{4,68},{5,69},{6,70},{7,71},{8,72},{9,... | collective-permute-start | bytes 1769480 | tf_op jit(solution)/shard_map/ppermute | solution.py:280
  51.1 11.4 %collective-permute-start.7 = (f32[16,72,128]{2,1,0:T(8,128)}, f32[16,72,128]{2,1,0:T(8,128)}, u32[]{:S(2)}, u32[]{:S(2)}) collective-permute-start(f32[16,72,128]{2,1,0:T(8,128)} %bins.5), channel_id=1, source_target_pairs={{0,32},{1,33},{2,34},{3,35},{4,36},{5,37},{6,38},{7,39},{8,40},{9,... | collective-permute-start | bytes 1769480 | tf_op jit(solution)/shard_map/ppermute | solution.py:280
  64.1 5.2 %collective-permute-start.11 = (f32[4,72,128]{2,1,0:T(8,128)S(1)}, f32[4,72,128]{2,1,0:T(8,128)S(1)}, u32[]{:S(2)}, u32[]{:S(2)}) collective-permute-start(f32[4,72,128]{2,1,0:T(8,128)S(1)} %get-tuple-element.10), channel_id=1, source_target_pairs={{0,12},{1,13},{2,14},{3,15},{4,0},{5,1},{6,2},{7,3},{8,4},{9,5},{1... | collective-permute-start | bytes 442376 | tf_op jit(solution)/shard_map/ppermute | solution.py:280
  64.9 6.4 %collective-permute-start.10 = (f32[4,72,128]{2,1,0:T(8,128)S(1)}, f32[4,72,128]{2,1,0:T(8,128)S(1)}, u32[]{:S(2)}, u32[]{:S(2)}) collective-permute-start(f32[4,72,128]{2,1,0:T(8,128)S(1)} %get-tuple-element.11), channel_id=1, source_target_pairs={{0,4},{1,5},{2,6},{3,7},{4,8},{5,9},{6,10},{7,11},{8,12},{9,13},{1... | collective-permute-start | bytes 442376 | tf_op jit(solution)/shard_map/ppermute | solution.py:280
  66.2 6.7 %collective-permute-start.9 = (f32[4,72,128]{2,1,0:T(8,128)S(1)}, f32[4,72,128]{2,1,0:T(8,128)S(1)}, u32[]{:S(2)}, u32[]{:S(2)}) collective-permute-start(f32[4,72,128]{2,1,0:T(8,128)S(1)} %get-tuple-element.9), channel_id=1, source_target_pairs={{0,8},{1,9},{2,10},{3,11},{4,12},{5,13},{6,14},{7,15},{8,0},{9,1},... | collective-permute-start | bytes 442376 | tf_op jit(solution)/shard_map/ppermute | solution.py:280
  72.9 6.4 %collective-permute-start.14 = (f32[72,128]{1,0:T(8,128)S(1)}, f32[72,128]{1,0:T(8,128)S(1)}, u32[]{:S(2)}, u32[]{:S(2)}) collective-permute-start(f32[72,128]{1,0:T(8,128)S(1)} %get-tuple-element.13), channel_id=1, source_target_pairs={{0,3},{1,0},{2,1},{3,2},{4,7},{5,4},{6,5},{7,6},{8,11},{9,8},{10,9... | collective-permute-start | bytes 110600 | tf_op jit(solution)/shard_map/ppermute | solution.py:280
  77.7 5.2 %collective-permute-start.13 = (f32[72,128]{1,0:T(8,128)S(1)}, f32[72,128]{1,0:T(8,128)S(1)}, u32[]{:S(2)}, u32[]{:S(2)}) collective-permute-start(f32[72,128]{1,0:T(8,128)S(1)} %get-tuple-element.14), channel_id=1, source_target_pairs={{0,1},{1,2},{2,3},{3,0},{4,5},{5,6},{6,7},{7,4},{8,9},{9,10},{10,1... | collective-permute-start | bytes 110600 | tf_op jit(solution)/shard_map/ppermute | solution.py:280
  77.7 5.6 %collective-permute-start.12 = (f32[72,128]{1,0:T(8,128)S(1)}, f32[72,128]{1,0:T(8,128)S(1)}, u32[]{:S(2)}, u32[]{:S(2)}) collective-permute-start(f32[72,128]{1,0:T(8,128)S(1)} %get-tuple-element.12), channel_id=1, source_target_pairs={{0,2},{1,3},{2,0},{3,1},{4,6},{5,7},{6,4},{7,5},{8,10},{9,11},{10,... | collective-permute-start | bytes 110600 | tf_op jit(solution)/shard_map/ppermute | solution.py:280

commit v5 on v4

--- a/solution.py
+++ b/solution.py
@@ -34,121 +34,11 @@
     return table
 
 
-def line_operators():
-    table = lobatto_matrix()
-
-    def derivative(flux, value, speed):
-        out = np.zeros((8,) + flux.shape[1:])
-        for start in (1, 5):
-            def common(low):
-                mean = 0.5 * (flux[low] + flux[low + 1])
-                return mean - 0.5 * speed * (value[low + 1] - value[low])
-            for i in range(4):
-                out[start - 1 + i] = sum(table[i, j] * flux[start + j] for j in range(4))
-            out[start + 2] += 6.0 * (common(start + 3) - flux[start + 3])
-            out[start - 1] -= 6.0 * (common(start - 1) - flux[start])
-        return out
-
-    def maps(along_axial):
-        result = []
-        for place in range(3):
-            unit = np.zeros((24, 8, 128))
-            for point in range(64):
-                line, other = (point // 8, point % 8) if along_axial else (point % 8, point // 8)
-                unit[place * 8 + line, other, point] = 1.0
-            value = unit[7:17]
-            speed_of = np.zeros((24, 8, 128))
-            for point in range(64):
-                line, other = (point // 8, point % 8) if along_axial else (point % 8, point // 8)
-                speed_of[place * 8 + line, other, 64 + point] = 1.0
-            velocity = speed_of[7:17]
-            if along_axial:
-                change = derivative(MEAN_FLOW * value + velocity, value, 1.5)
-            else:
-                change = np.swapaxes(derivative(velocity, value, 1.0), 0, 1)
-            result.append(-TIME_STEP * change.reshape(64, 128).T)
-        return result
-
-    before_x, own_x, after_x = maps(True)
-    before_y, own_y, after_y = maps(False)
-    eye = np.eye(64)
-    own_x[:64] += eye
-    own_x[:64] -= TIME_STEP * (table[0, 0] - 6.0 * (0.5 - 0.5 - 1.0)) * eye
-    low = -TIME_STEP * -6.0 * (0.5 + 0.5) * eye
-    near_a = np.concatenate([low, -TIME_STEP * table[0, 1] * eye])
-    near_b = np.concatenate([-TIME_STEP * table[0, 2] * eye, -TIME_STEP * table[0, 3] * eye])
-    every = [own_x, own_y, near_a, near_b, before_x, after_x, before_y, after_y]
-    return np.concatenate(every).astype(np.float32)
-
-
-def tile_kernel(state_ref, tile_ref):
-    at = 4 * (state_ref.shape[2] // 8)
-    pick = lax.broadcasted_iota(jnp.int32, (8, 128), 1) == (
-        lax.broadcasted_iota(jnp.int32, (8, 128), 0) + (at - 1)
-    )
-    pick = pick.astype(jnp.float32)
-
-    def points(field):
-        return lax.dot_general(
-            pick, field, (((1,), (1,)), ((), ())),
-            precision=lax.Precision.HIGHEST, preferred_element_type=jnp.float32,
-        )
-
-    value = points(state_ref[3] + state_ref[4])
-    axial = points(state_ref[1])
-    azimuthal = points(state_ref[2])
-    rows = [
-        jnp.concatenate([value[1:2], axial[1:2]], axis=1),
-        jnp.concatenate([value[1:2], azimuthal[1:2]], axis=1),
-        jnp.concatenate([value[0:1], value[2:3]], axis=1),
-        jnp.concatenate([value[3:4], value[4:5]], axis=1),
-        jnp.zeros((4, 128), jnp.float32),
-    ]
-    tile_ref[...] = jnp.concatenate(rows, axis=0)
-
-
-def source_kernel(map_ref, own_ref, bx_ref, ax_ref, by_ref, ay_ref, index_ref, count_ref, source_ref):
-    rows = [own_ref[0:1], own_ref[1:2], own_ref[2:3], own_ref[3:4],
-            bx_ref[0:1], ax_ref[0:1], by_ref[1:2], ay_ref[1:2]]
-    exact = dict(precision=lax.Precision.HIGHEST, preferred_element_type=jnp.float32)
-    plane = jnp.dot(jnp.concatenate(rows, axis=1), map_ref[...], **exact)
-    points = lax.broadcasted_iota(jnp.int32, (64, SLOTS), 0)
-    hit = (index_ref[...] == points).astype(jnp.float32)
-    source = jnp.dot(plane, hit, **exact)
-    live = lax.broadcasted_iota(jnp.int32, (1, SLOTS), 1) < count_ref[0, 0]
-    source_ref[...] = jnp.where(live, source, 0.0)
-
-
-def slot_source(state, surf_index, surf_count):
-    vmem = pl.BlockSpec(memory_space=pltpu.VMEM)
-    tile = pl.pallas_call(
-        tile_kernel,
-        in_specs=[vmem],
-        out_specs=vmem,
-        out_shape=jax.ShapeDtypeStruct((8, 128), jnp.float32),
-        name="tile",
-    )(state.reshape(5, 64, state.shape[3]))
-
-    def around(axes, size, wrap):
-        up = [(i, (i + 1) % size) for i in range(size if wrap else size - 1)]
-        down = [(j, i) for i, j in up]
-        return lax.ppermute(tile, axes, up), lax.ppermute(tile, axes, down)
-
-    before_x, after_x = around(AXIAL, lax.axis_size(AXIAL), False)
-    before_y, after_y = around(AZIMUTHAL, lax.axis_size(AZIMUTHAL), True)
-    return pl.pallas_call(
-        source_kernel,
-        in_specs=[vmem] * 7 + [pl.BlockSpec(memory_space=pltpu.SMEM)],
-        out_specs=vmem,
-        out_shape=jax.ShapeDtypeStruct((1, SLOTS), jnp.float32),
-        name="source",
-    )(
-        jnp.asarray(line_operators()), tile, before_x, after_x, before_y, after_y,
-        surf_index.reshape(1, SLOTS), surf_count,
-    )
-
-
-def turn_kernel(core_ref, own_delay, own_fraction, other_delay, other_fraction, own_ref, other_ref):
+def in_vmem(*arrays):
+    return [pltpu.with_memory_space_constraint(array, pltpu.VMEM) for array in arrays]
+
+
+def first_kernel(core_ref, state_ref, own_delay, own_fraction, other_delay, other_fraction, own_ref, other_ref, tile_ref):
     for delay, fraction, out in (
         (own_delay, own_fraction, own_ref),
         (other_delay, other_fraction, other_ref),
@@ -165,23 +55,159 @@
             ]
             out[rows, 512:640] = jnp.concatenate(rest, axis=0).T
 
-
-def turned(core, delay, fraction):
+    @pl.when(pl.program_id(0) == 0)
+    def _():
+        at = 4 * (state_ref.shape[2] // 8)
+        value = state_ref[3] + state_ref[4]
+        axial = jnp.concatenate([value, state_ref[1]], axis=0).T[at - 8 : at + 8]
+        azimuthal = jnp.concatenate([value, state_ref[2]], axis=0).T[at : at + 8]
+        first = lax.broadcasted_iota(jnp.int32, (1, 128), 1) < 64
+        after = pltpu.roll(axial, 64, 1)
+        rows = [
+            axial[8:9],
+            azimuthal[0:1],
+            jnp.where(first, axial[7:8], after[9:10]),
+            jnp.where(first, axial[10:11], after[11:12]),
+            jnp.zeros((4, 128), jnp.float32),
+        ]
+        tile_ref[...] = jnp.concatenate(rows, axis=0)
+
+
+def first(core, state, delay, fraction):
     mine = pl.BlockSpec((SLOTS, 256), lambda n, c: (0, 2 * n + c[0]))
     other = pl.BlockSpec((SLOTS, 256), lambda n, c: (0, 2 * n + 1 - c[0]))
-    shape = jax.ShapeDtypeStruct((1024, LANES), jnp.float32)
+    state = state.reshape(5, 64, state.shape[3])
+    delay, fraction, state = (
+        pltpu.with_memory_space_constraint(array, pltpu.HBM) for array in (delay, fraction, state)
+    )
     return pl.pallas_call(
-        turn_kernel,
+        first_kernel,
         grid_spec=pltpu.PrefetchScalarGridSpec(
             num_scalar_prefetch=1,
             grid=(4,),
-            in_specs=[mine, mine, other, other],
-            out_specs=[pl.BlockSpec((256, LANES), lambda n, c: (n, 0))] * 2,
+            in_specs=[pl.BlockSpec(state.shape, lambda n, c: (0, 0, 0)), mine, mine, other, other],
+            out_specs=[pl.BlockSpec((256, LANES), lambda n, c: (n, 0))] * 2
+            + [pl.BlockSpec((8, 128), lambda n, c: (0, 0))],
         ),
-        out_shape=[shape, shape],
+        out_shape=[
+            pltpu.VMEM((1024, LANES), jnp.float32),
+            pltpu.VMEM((1024, LANES), jnp.float32),
+            pltpu.VMEM((8, 128), jnp.float32),
+        ],
         compiler_params=pltpu.CompilerParams(vmem_limit_bytes=32 * 1024 * 1024),
-        name="turned",
-    )(core, delay, fraction, delay, fraction)
+        name="first",
+    )(core, state, delay, fraction, delay, fraction)
+
+
+def by_node(node, values):
+    out = jnp.full(node.shape, values[0], jnp.float32)
+    for n in (1, 2, 3):
+        out = jnp.where(node == n, jnp.float32(values[n]), out)
+    return out
+
+
+def source_kernel(place_ref, own_ref, core_ref, chip_ref, even_ref, odd_ref, index_ref, count_ref, source_ref):
+    table = lobatto_matrix()
+    point = lax.broadcasted_iota(jnp.int32, (1, 128), 1)
+    axial, azimuthal = point // 8, point % 8
+    second = place_ref[0] == 1
+    odd = place_ref[1] == 1
+    no_before, no_after = place_ref[2] == 0, place_ref[2] == 7
+    core, chip = core_ref[...], chip_ref[...]
+    before_x = jnp.where(no_before, 0.0, jnp.where(second, core, chip))[0:1]
+    after_x = jnp.where(no_after, 0.0, jnp.where(second, chip, core))[0:1]
+    even, odd_tile = even_ref[...], odd_ref[...]
+    before_y = jnp.where(odd, even, odd_tile)[1:2]
+    after_y = jnp.where(odd, odd_tile, even)[1:2]
+
+    def to_lane(array, shift):
+        return pltpu.roll(array, shift % 128, 1)
+
+    def split(row, mean):
+        value, velocity = row, to_lane(row, -64)
+        return (MEAN_FLOW * value if mean else 0.0) + velocity, value
+
+    def derivative(own, before, after, width, coordinate, speed, mean):
+        node = coordinate % 4
+        flux, value = split(own, mean)
+        out = 0.0
+        for shift in range(-3, 4):
+            weights = [table[n, n + shift] if 0 <= n + shift < 4 else 0.0 for n in range(4)]
+            moved = flux if shift == 0 else to_lane(flux, -shift * width)
+            out = out + by_node(node, weights) * moved
+        sides = []
+        for outside, end, step, back in ((after, 7, -width, 7 * width), (before, 0, width, -7 * width)):
+            there_flux, there_value = split(outside, mean)
+            at_end = coordinate == end
+            sides.append((
+                jnp.where(at_end, to_lane(there_flux, back), to_lane(flux, step)),
+                jnp.where(at_end, to_lane(there_value, back), to_lane(value, step)),
+            ))
+        (up_flux, up_value), (low_flux, low_value) = sides
+        up = 0.5 * (flux + up_flux) - 0.5 * speed * (up_value - value)
+        low = 0.5 * (low_flux + flux) - 0.5 * speed * (value - low_value)
+        out = out + jnp.where(node == 3, 6.0 * (up - flux), 0.0)
+        return out - jnp.where(node == 0, 6.0 * (low - flux), 0.0)
+
+    own = own_ref[0:4]
+    change = derivative(own[0:1], before_x, after_x, 8, axial, 1.5, True)
+    change = change + derivative(own[1:2], before_y, after_y, 1, azimuthal, 1.0, False)
+    value, lower = own[0:1], own[2:3]
+    radial = (
+        np.float32(table[0, 0]) * value
+        + np.float32(table[0, 1]) * to_lane(own[2:3], -64)
+        + np.float32(table[0, 2]) * own[3:4]
+        + np.float32(table[0, 3]) * to_lane(own[3:4], -64)
+    )
+    common = 0.5 * (lower + value) - 0.5 * (value - lower)
+    change = change + (radial - 6.0 * (common - value))
+    plane = jnp.where(point < 64, value - TIME_STEP * change, 0.0)
+    terms = []
+    for _ in range(3):
+        term = plane.astype(jnp.bfloat16).astype(jnp.float32)
+        terms.append(term)
+        plane = plane - term
+    rows = jnp.concatenate(terms + [jnp.zeros((5, 128), jnp.float32)], axis=0).astype(jnp.bfloat16)
+    points = lax.broadcasted_iota(jnp.int32, (128, SLOTS), 0)
+    index = index_ref[...].reshape(1, SLOTS)
+    hit = jnp.where(index == points, 1.0, 0.0).astype(jnp.bfloat16)
+    source = jnp.dot(rows, hit, preferred_element_type=jnp.float32)
+    source = source[0:1] + source[1:2] + source[2:3]
+    live = lax.broadcasted_iota(jnp.int32, (1, SLOTS), 1) < count_ref[0, 0]
+    source_ref[...] = jnp.where(live, source, 0.0)
+
+
+def neighbour(kind):
+    moves = []
+    for i in range(128):
+        axial, azimuthal = i // 16, i % 16
+        if kind == "core":
+            axial ^= 1
+        elif kind == "chip":
+            axial = (axial + 1 if axial % 2 else axial - 1) % 8
+        elif kind == "even":
+            azimuthal ^= 1
+        else:
+            azimuthal = (azimuthal + 1 if azimuthal % 2 else azimuthal - 1) % 16
+        moves.append((i, axial * 16 + azimuthal))
+    return moves
+
+
+def slot_source(tile, surf_index, surf_count):
+    tiles = [
+        lax.ppermute(tile, AXIAL + AZIMUTHAL, neighbour(kind)) for kind in ("core", "chip", "even", "odd")
+    ]
+    axial = lax.axis_index(AXIAL)
+    place = jnp.stack([axial % 2, lax.axis_index(AZIMUTHAL) % 2, axial]).astype(jnp.int32)
+    vmem = pl.BlockSpec(memory_space=pltpu.VMEM)
+    smem = pl.BlockSpec(memory_space=pltpu.SMEM)
+    return pl.pallas_call(
+        source_kernel,
+        in_specs=[smem] + [vmem] * 6 + [smem],
+        out_specs=vmem,
+        out_shape=pltpu.VMEM((1, SLOTS), jnp.float32),
+        name="source",
+    )(place, *in_vmem(tile, *tiles, surf_index), surf_count)
 
 
 def bins_kernel(part_ref, src_ref, src_b_ref, own_ref, sib_ref, out_ref, hi_s):
@@ -261,13 +287,13 @@
         in_specs=[pl.BlockSpec(memory_space=pltpu.SMEM)] + [vmem] * 4,
         out_specs=vmem,
         scratch_shapes=[pltpu.VMEM((UNROLL, 8, LANES), jnp.float32)],
-        out_shape=jax.ShapeDtypeStruct((16, 2 * ROWS, 128), jnp.float32),
+        out_shape=pltpu.VMEM((16, 2 * ROWS, 128), jnp.float32),
         compiler_params=pltpu.CompilerParams(vmem_limit_bytes=32 * 1024 * 1024),
         cost_estimate=pl.CostEstimate(
             flops=32 * 2 * 288 * 256 * LANES, bytes_accessed=8 * 256 * LANES, transcendentals=0
         ),
         name="bins",
-    )(part, src, src_b, own, sibling)
+    )(part, *in_vmem(src, src_b, own, sibling))
 
 
 def shifted(array, phase, step):
@@ -302,9 +328,9 @@
 def local(state, surf_index, surf_count, delay, fraction):
     core = lax.axis_index("core").reshape(1)
     swap = [(0, 1), (1, 0)]
-    own, other = turned(core, delay, fraction)
+    own, other, tile = first(core, state, delay, fraction)
     sibling = lax.ppermute(other, "core", swap)
-    source = slot_source(state, surf_index, surf_count)
+    source = slot_source(tile, surf_index, surf_count)
     source_b = lax.ppermute(source, "core", swap)
     total = summed(source, source_b, own, sibling)
     total = total.reshape(2, ROWS, 16, 8).transpose(0, 3, 1, 2).reshape(16, ROWS, 16)

time: 85.1 us -> 74.6 us (0.88)
  local copies, waits for them, and re-layouts: 6.97 us -> 1.32 us
  starting transfers between devices: 26.3 us -> 21.6 us
  Pallas kernels: 33.1 us -> 32.1 us
    unnamed x18 -> x2, local copies, waits for them, and re-layouts: 5.07 us -> 0.01 us
    ppermute x9, starting transfers between devices: 14.7 us -> 11.7 us  [shifted(): return lax.ppermute(array, AXIAL + AZIMUTHAL, moves)]
    ppermute x1, starting transfers between devices: 1.18 us -> 0.01 us  [local(): source_b = lax.ppermute(source, 'core', swap)]
    pallas_call x3 -> x2, Pallas kernels: 7.22 us -> 6.29 us  [the longest x1 5.34 us: first(): pl.pallas_call(first_kernel, grid_spec=pltpu.PrefetchScalarGridSpec(num_s...]
  transfers between devices with their start and end apart: 15 -> 15, of which waited for: 9 -> 8; matrix products, arithmetic and copies ran while one was open for 1% -> 1% of each run, Pallas kernels for 28% -> 28%
where the time goes in v5:
time: 74.6 us; the launch traced here: 74.3 us
  Pallas kernels  32.1 us (43%)
  starting transfers between devices  21.6 us (29%)
  waiting for transfers between devices  15.9 us (21%)
  other arithmetic  2.56 us (3%)
  local copies, waits for them, and re-layouts  1.32 us (2%)
  between operations  0.8 us (1%)
    pallas_call x4, Pallas kernels, bins(): pl.pallas_call(bins_kernel, in_specs=[pl.BlockSpec(memory_space=pltpu.SME...  25.9 us
    ppermute x9, waiting for transfers between devices, shifted(): return lax.ppermute(array, AXIAL + AZIMUTHAL, moves)  14.3 us
    ppermute x9, starting transfers between devices, shifted(): return lax.ppermute(array, AXIAL + AZIMUTHAL, moves)  11.7 us
    ppermute x4, starting transfers between devices, slot_source(): lax.ppermute(tile, AXIAL + AZIMUTHAL, neighbour(kind))  9.86 us
    pallas_call x1, Pallas kernels, first(): pl.pallas_call(first_kernel, grid_spec=pltpu.PrefetchScalarGridSpec(num_s...  5.34 us
    add x1, other arithmetic, summed(): total = (got[0] + got[1] + got[2] + got[3]).reshape(4, 4, 2 * ROWS, 128)  1.53 us
  transfers between devices with their start and end apart: 15, of which 8 were waited for; matrix products, arithmetic and copies ran while one was open for 1% of the time, Pallas kernels for 28%

profile of v5, /device:TPU:0, one launch (start us, length us, event | category | flops | bytes accessed | tf_op | source)
XLA Modules:
  0.0 74.3 jit_solution(15160918698942892631)
XLA Ops:
  0.0 5.3 %first.1 = (f32[1024,640]{1,0:T(8,128)S(1)}, f32[1024,640]{1,0:T(8,128)}, f32[8,128]{1,0:T(8,128)S(1)}) custom-call(s32[1]{0:T(128)} %bitcast.6.core_ref, f32[5,64,128]{2,1,0:T(8,128)} %bitcast.45, s32[272,2048]{1,0:T(8,128)} %other_delay.1, f32[272,2048]{1,0:T(8,128)} %other_fraction.1, s32[272,2048]{1,0:T(8,128)} %other_delay.1, f32[272,2048]{1,0:T(8,128)} %other_fraction.1), custom_call_target="tpu_custom_call" | custom-call | tf_op jit(solution)/shard_map/first/pallas_call | solution.py:83
  5.3 0.0 collective-permute-start.5
  5.3 0.5 collective-permute-start
  5.9 2.5 %collective-permute-start.1 = (f32[8,128]{1,0:T(8,128)S(1)}, f32[8,128]{1,0:T(8,128)S(1)}, u32[]{:S(2)}, u32[]{:S(2)}) collective-permute-start(f32[8,128]{1,0:T(8,128)S(1)} %get-tuple-element.8.own_ref), channel_id=1, source_target_pairs={{0,112},{1,113},{2,114},{3,115},{4,116},{5,117},{6,118},{7,119},{8... | collective-permute-start | bytes 12296 | tf_op jit(solution)/shard_map/ppermute | solution.py:198
  8.3 1.9 %collective-permute-start.2 = (f32[8,128]{1,0:T(8,128)S(1)}, f32[8,128]{1,0:T(8,128)S(1)}, u32[]{:S(2)}, u32[]{:S(2)}) collective-permute-start(f32[8,128]{1,0:T(8,128)S(1)} %get-tuple-element.8.own_ref), channel_id=1, source_target_pairs={{0,1},{1,0},{2,3},{3,2},{4,5},{5,4},{6,7},{7,6},{8,9},{9,8},{10,11... | collective-permute-start | bytes 12296 | tf_op jit(solution)/shard_map/ppermute | solution.py:198
  10.2 5.0 %collective-permute-start.3 = (f32[8,128]{1,0:T(8,128)S(1)}, f32[8,128]{1,0:T(8,128)S(1)}, u32[]{:S(2)}, u32[]{:S(2)}) collective-permute-start(f32[8,128]{1,0:T(8,128)S(1)} %get-tuple-element.8.own_ref), channel_id=1, source_target_pairs={{0,15},{1,2},{2,1},{3,4},{4,3},{5,6},{6,5},{7,8},{8,7},{9,10},{10,... | collective-permute-start | bytes 12296 | tf_op jit(solution)/shard_map/ppermute | solution.py:198
  15.2 0.1 add_add_fusion.3.part_ref
  15.3 0.1 add_add_fusion.1.part_ref
  15.4 0.6 pad_add_fusion.place_ref
  16.6 0.0 collective-permute-done.core_ref
  16.6 0.0 collective-permute-done.1.chip_ref
  16.6 0.0 collective-permute-done.2.even_ref
  16.6 0.5 collective-permute-done.3.odd_ref
  17.2 1.0 %source.1.src_ref = f32[1,272]{1,0:T(1,128)S(1)} custom-call(s32[3]{0:T(128)} %pad_add_fusion.place_ref, f32[8,128]{1,0:T(8,128)S(1)} %get-tuple-element.8.own_ref, f32[8,128]{1,0:T(8,128)S(1)} %collective-permute-done.core_ref, f32[8,128]{1,0:T(8,128)S(1)} %collective-permute-done.1.chip_ref, f32[8,128]{1,0:T(8,128)S(1)} %collective-permute-done.2.even_ref, ...), custom_call_target="tpu_custom_call" | custom-call | tf_op jit(solution)/shard_map/source/pallas_call | solution.py:204
  18.1 0.0 collective-permute-start.4
  18.1 0.1 add_add_fusion.2.part_ref
  18.2 1.1 %collective-permute-done.4.src_b_ref = f32[1,272]{1,0:T(1,128)S(1)} collective-permute-done((f32[1,272]{1,0:T(1,128)S(1)}, f32[1,272]{1,0:T(1,128)S(1)}, u32[]{:S(2)}, u32[]{:S(2)}) %collective-permute-start.4) | collective-permute-done | bytes 1120 | tf_op jit(solution)/shard_map/ppermute | solution.py:334
  19.3 0.0 collective-permute-done.5.sib_ref
  19.3 6.1 %bins.6 = f32[16,72,128]{2,1,0:T(8,128)S(1)} custom-call(s32[3]{0:T(128)S(1)} %add_add_fusion.3.part_ref, f32[1,272]{1,0:T(1,128)S(1)} %source.1.src_ref, f32[1,272]{1,0:T(1,128)S(1)} %collective-permute-done.4.src_b_ref, f32[1024,640]{1,0:T(8,128)S(1)} %get-tuple-element.9.own_ref, f32[1024,640]{1,0:T(8,128)} %collective-permute-done.5.sib_ref), custom_call_target="tpu_custom_call" | custom-call | flops 3019898880 | bytes 1310720 | tf_op jit(solution)/shard_map/bins/pallas_call | solution.py:285
  25.3 0.9 %collective-permute-start.8 = (f32[16,72,128]{2,1,0:T(8,128)S(1)}, f32[16,72,128]{2,1,0:T(8,128)}, u32[]{:S(2)}, u32[]{:S(2)}) collective-permute-start(f32[16,72,128]{2,1,0:T(8,128)S(1)} %bins.6), channel_id=1, source_target_pairs={{0,96},{1,97},{2,98},{3,99},{4,100},{5,101},{6,102},{7,103},{8,104... | collective-permute-start | bytes 1769480 | tf_op jit(solution)/shard_map/ppermute | solution.py:306
  26.2 6.9 %bins.4 = f32[16,72,128]{2,1,0:T(8,128)} custom-call(s32[3]{0:T(128)S(1)} %add_add_fusion.1.part_ref, f32[1,272]{1,0:T(1,128)S(1)} %source.1.src_ref, f32[1,272]{1,0:T(1,128)S(1)} %collective-permute-done.4.src_b_ref, f32[1024,640]{1,0:T(8,128)S(1)} %get-tuple-element.9.own_ref, f32[1024,640]{1,0:T(8,128)} %collective-permute-done.5.sib_ref), custom_call_target="tpu_custom_call" | custom-call | flops 3019898880 | bytes 1310720 | tf_op jit(solution)/shard_map/bins/pallas_call | solution.py:285
  33.1 0.6 collective-permute-start.6
  33.7 6.9 %bins.5 = f32[16,72,128]{2,1,0:T(8,128)} custom-call(s32[3]{0:T(128)S(1)} %add_add_fusion.2.part_ref, f32[1,272]{1,0:T(1,128)S(1)} %source.1.src_ref, f32[1,272]{1,0:T(1,128)S(1)} %collective-permute-done.4.src_b_ref, f32[1024,640]{1,0:T(8,128)S(1)} %get-tuple-element.9.own_ref, f32[1024,640]{1,0:T(8,128)} %collective-permute-done.5.sib_ref), custom_call_target="tpu_custom_call" | custom-call | flops 3019898880 | bytes 1310720 | tf_op jit(solution)/shard_map/bins/pallas_call | solution.py:285
  40.6 0.8 %collective-permute-start.7 = (f32[16,72,128]{2,1,0:T(8,128)}, f32[16,72,128]{2,1,0:T(8,128)}, u32[]{:S(2)}, u32[]{:S(2)}) collective-permute-start(f32[16,72,128]{2,1,0:T(8,128)} %bins.5), channel_id=1, source_target_pairs={{0,32},{1,33},{2,34},{3,35},{4,36},{5,37},{6,38},{7,39},{8,40},{9,... | collective-permute-start | bytes 1769480 | tf_op jit(solution)/shard_map/ppermute | solution.py:306
  41.4 0.1 add_add_fusion.4.part_ref
  41.5 6.0 %bins.7 = f32[16,72,128]{2,1,0:T(8,128)S(1)} custom-call(s32[3]{0:T(128)S(1)} %add_add_fusion.4.part_ref, f32[1,272]{1,0:T(1,128)S(1)} %source.1.src_ref, f32[1,272]{1,0:T(1,128)S(1)} %collective-permute-done.4.src_b_ref, f32[1024,640]{1,0:T(8,128)S(1)} %get-tuple-element.9.own_ref, f32[1024,640]{1,0:T(8,128)} %collective-permute-done.5.sib_ref), custom_call_target="tpu_custom_call" | custom-call | flops 3019898880 | bytes 1310720 | tf_op jit(solution)/shard_map/bins/pallas_call | solution.py:285
  47.5 0.0 collective-permute-done.8
  47.5 0.0 collective-permute-done.6
  47.5 4.5 %collective-permute-done.7 = f32[16,72,128]{2,1,0:T(8,128)} collective-permute-done((f32[16,72,128]{2,1,0:T(8,128)}, f32[16,72,128]{2,1,0:T(8,128)}, u32[]{:S(2)}, u32[]{:S(2)}) %collective-permute-start.7) | collective-permute-done | bytes 589856 | tf_op jit(solution)/shard_map/ppermute | solution.py:306
  52.0 1.5 %add_add_fusion = f32[16,72,128]{2,1,0:T(8,128)S(1)} fusion(f32[16,72,128]{2,1,0:T(8,128)S(1)} %bins.7, f32[16,72,128]{2,1,0:T(8,128)} %collective-permute-done.8, f32[16,72,128]{2,1,0:T(8,128)} %collective-permute-done.6, f32[16,72,128]{2,1,0:T(8,128)} %collective-permute-done.7), kind=kLoop, calls=%fused_computation | loop fusion | flops 442368 | bytes 2949120 | tf_op jit(solution)/shard_map/add | solution.py:320
  53.6 1.9 %collective-permute-start.11 = (f32[4,72,128]{2,1,0:T(8,128)S(1)}, f32[4,72,128]{2,1,0:T(8,128)S(1)}, u32[]{:S(2)}, u32[]{:S(2)}) collective-permute-start(f32[4,72,128]{2,1,0:T(8,128)S(1)} %get-tuple-element.12), channel_id=1, source_target_pairs={{0,12},{1,13},{2,14},{3,15},{4,0},{5,1},{6,2},{7,3},{8,4},{9,5},{1... | collective-permute-start | bytes 442376 | tf_op jit(solution)/shard_map/ppermute | solution.py:306
  55.5 0.2 collective-permute-start.10
  55.7 2.0 %collective-permute-start.9 = (f32[4,72,128]{2,1,0:T(8,128)S(1)}, f32[4,72,128]{2,1,0:T(8,128)S(1)}, u32[]{:S(2)}, u32[]{:S(2)}) collective-permute-start(f32[4,72,128]{2,1,0:T(8,128)S(1)} %get-tuple-element.11), channel_id=1, source_target_pairs={{0,8},{1,9},{2,10},{3,11},{4,12},{5,13},{6,14},{7,15},{8,0},{9,1},... | collective-permute-start | bytes 442376 | tf_op jit(solution)/shard_map/ppermute | solution.py:306
  57.7 1.1 %collective-permute-done.11 = f32[4,72,128]{2,1,0:T(8,128)S(1)} collective-permute-done((f32[4,72,128]{2,1,0:T(8,128)S(1)}, f32[4,72,128]{2,1,0:T(8,128)S(1)}, u32[]{:S(2)}, u32[]{:S(2)}) %collective-permute-start.11) | collective-permute-done | bytes 147488 | tf_op jit(solution)/shard_map/ppermute | solution.py:306
  58.8 4.6 %collective-permute-done.10 = f32[4,72,128]{2,1,0:T(8,128)S(1)} collective-permute-done((f32[4,72,128]{2,1,0:T(8,128)S(1)}, f32[4,72,128]{2,1,0:T(8,128)S(1)}, u32[]{:S(2)}, u32[]{:S(2)}) %collective-permute-start.10) | collective-permute-done | bytes 147488 | tf_op jit(solution)/shard_map/ppermute | solution.py:306
  63.4 0.0 collective-permute-done.9
  63.5 3.8 %collective-permute-start.14 = (f32[72,128]{1,0:T(8,128)S(1)}, f32[72,128]{1,0:T(8,128)S(1)}, u32[]{:S(2)}, u32[]{:S(2)}) collective-permute-start(f32[72,128]{1,0:T(8,128)S(1)} %get-tuple-element.15), channel_id=1, source_target_pairs={{0,3},{1,0},{2,1},{3,2},{4,7},{5,4},{6,5},{7,6},{8,11},{9,8},{10,9... | collective-permute-start | bytes 110600 | tf_op jit(solution)/shard_map/ppermute | solution.py:306
  67.3 0.0 collective-permute-start.13
  67.3 1.5 %collective-permute-start.12 = (f32[72,128]{1,0:T(8,128)S(1)}, f32[72,128]{1,0:T(8,128)S(1)}, u32[]{:S(2)}, u32[]{:S(2)}) collective-permute-start(f32[72,128]{1,0:T(8,128)S(1)} %get-tuple-element.14), channel_id=1, source_target_pairs={{0,2},{1,3},{2,0},{3,1},{4,6},{5,7},{6,4},{7,5},{8,10},{9,11},{10,... | collective-permute-start | bytes 110600 | tf_op jit(solution)/shard_map/ppermute | solution.py:306
  68.8 0.1 collective-permute-done.14
  68.9 3.5 %collective-permute-done.13 = f32[72,128]{1,0:T(8,128)S(1)} collective-permute-done((f32[72,128]{1,0:T(8,128)S(1)}, f32[72,128]{1,0:T(8,128)S(1)}, u32[]{:S(2)}, u32[]{:S(2)}) %collective-permute-start.13) | collective-permute-done | bytes 36896 | tf_op jit(solution)/shard_map/ppermute | solution.py:306
  72.5 0.4 collective-permute-done.12
  72.9 0.1 copy.8
  73.0 0.1 reshape.21
  73.2 0.1 slice_add_fusion
  73.3 0.2 copy.10
  73.5 0.1 reshape.23
  73.6 0.6 slice.14
  (8 shorter events, 0.2 us)
Async XLA Ops:
  0.0 17.2 %copy-start = (s32[272]{0:T(512)S(1)}, s32[272]{0:T(512)}, u32[]{:S(2)}) copy-start(s32[272]{0:T(512)} %index_ref.1) | copy-start | bytes 3268
  5.3 13.9 %collective-permute-start.5 = (f32[1024,640]{1,0:T(8,128)}, f32[1024,640]{1,0:T(8,128)}, u32[]{:S(2)}, u32[]{:S(2)}) collective-permute-start(f32[1024,640]{1,0:T(8,128)} %get-tuple-element.10), channel_id=1, source_target_pairs={{0,16},{16,0},{1,17},{17,1},{2,18},{18,2},{3,19},{19,3},{4,20},{20... | collective-permute-start | bytes 7864328 | tf_op jit(solution)/shard_map/ppermute | solution.py:332
  5.3 11.3 %collective-permute-start = (f32[8,128]{1,0:T(8,128)S(1)}, f32[8,128]{1,0:T(8,128)S(1)}, u32[]{:S(2)}, u32[]{:S(2)}) collective-permute-start(f32[8,128]{1,0:T(8,128)S(1)} %get-tuple-element.8.own_ref), channel_id=1, source_target_pairs={{0,16},{1,17},{2,18},{3,19},{4,20},{5,21},{6,22},{7,23},{8,24},{9,... | collective-permute-start | bytes 12296 | tf_op jit(solution)/shard_map/ppermute | solution.py:198
  5.9 10.8 %collective-permute-start.1 = (f32[8,128]{1,0:T(8,128)S(1)}, f32[8,128]{1,0:T(8,128)S(1)}, u32[]{:S(2)}, u32[]{:S(2)}) collective-permute-start(f32[8,128]{1,0:T(8,128)S(1)} %get-tuple-element.8.own_ref), channel_id=1, source_target_pairs={{0,112},{1,113},{2,114},{3,115},{4,116},{5,117},{6,118},{7,119},{8... | collective-permute-start | bytes 12296 | tf_op jit(solution)/shard_map/ppermute | solution.py:198
  8.3 8.3 %collective-permute-start.2 = (f32[8,128]{1,0:T(8,128)S(1)}, f32[8,128]{1,0:T(8,128)S(1)}, u32[]{:S(2)}, u32[]{:S(2)}) collective-permute-start(f32[8,128]{1,0:T(8,128)S(1)} %get-tuple-element.8.own_ref), channel_id=1, source_target_pairs={{0,1},{1,0},{2,3},{3,2},{4,5},{5,4},{6,7},{7,6},{8,9},{9,8},{10,11... | collective-permute-start | bytes 12296 | tf_op jit(solution)/shard_map/ppermute | solution.py:198
  10.2 6.9 %collective-permute-start.3 = (f32[8,128]{1,0:T(8,128)S(1)}, f32[8,128]{1,0:T(8,128)S(1)}, u32[]{:S(2)}, u32[]{:S(2)}) collective-permute-start(f32[8,128]{1,0:T(8,128)S(1)} %get-tuple-element.8.own_ref), channel_id=1, source_target_pairs={{0,15},{1,2},{2,1},{3,4},{4,3},{5,6},{6,5},{7,8},{8,7},{9,10},{10,... | collective-permute-start | bytes 12296 | tf_op jit(solution)/shard_map/ppermute | solution.py:198
  18.1 1.2 %collective-permute-start.4 = (f32[1,272]{1,0:T(1,128)S(1)}, f32[1,272]{1,0:T(1,128)S(1)}, u32[]{:S(2)}, u32[]{:S(2)}) collective-permute-start(f32[1,272]{1,0:T(1,128)S(1)} %source.1.src_ref), channel_id=1, source_target_pairs={{0,16},{16,0},{1,17},{17,1},{2,18},{18,2},{3,19},{19,3},{4,20},{20... | collective-permute-start | bytes 3272 | tf_op jit(solution)/shard_map/ppermute | solution.py:334
  25.3 22.2 %collective-permute-start.8 = (f32[16,72,128]{2,1,0:T(8,128)S(1)}, f32[16,72,128]{2,1,0:T(8,128)}, u32[]{:S(2)}, u32[]{:S(2)}) collective-permute-start(f32[16,72,128]{2,1,0:T(8,128)S(1)} %bins.6), channel_id=1, source_target_pairs={{0,96},{1,97},{2,98},{3,99},{4,100},{5,101},{6,102},{7,103},{8,104... | collective-permute-start | bytes 1769480 | tf_op jit(solution)/shard_map/ppermute | solution.py:306
  33.1 14.4 %collective-permute-start.6 = (f32[16,72,128]{2,1,0:T(8,128)}, f32[16,72,128]{2,1,0:T(8,128)}, u32[]{:S(2)}, u32[]{:S(2)}) collective-permute-start(f32[16,72,128]{2,1,0:T(8,128)} %bins.4), channel_id=1, source_target_pairs={{0,64},{1,65},{2,66},{3,67},{4,68},{5,69},{6,70},{7,71},{8,72},{9,... | collective-permute-start | bytes 1769480 | tf_op jit(solution)/shard_map/ppermute | solution.py:306
  40.6 11.5 %collective-permute-start.7 = (f32[16,72,128]{2,1,0:T(8,128)}, f32[16,72,128]{2,1,0:T(8,128)}, u32[]{:S(2)}, u32[]{:S(2)}) collective-permute-start(f32[16,72,128]{2,1,0:T(8,128)} %bins.5), channel_id=1, source_target_pairs={{0,32},{1,33},{2,34},{3,35},{4,36},{5,37},{6,38},{7,39},{8,40},{9,... | collective-permute-start | bytes 1769480 | tf_op jit(solution)/shard_map/ppermute | solution.py:306
  53.6 5.2 %collective-permute-start.11 = (f32[4,72,128]{2,1,0:T(8,128)S(1)}, f32[4,72,128]{2,1,0:T(8,128)S(1)}, u32[]{:S(2)}, u32[]{:S(2)}) collective-permute-start(f32[4,72,128]{2,1,0:T(8,128)S(1)} %get-tuple-element.12), channel_id=1, source_target_pairs={{0,12},{1,13},{2,14},{3,15},{4,0},{5,1},{6,2},{7,3},{8,4},{9,5},{1... | collective-permute-start | bytes 442376 | tf_op jit(solution)/shard_map/ppermute | solution.py:306
  55.5 7.9 %collective-permute-start.10 = (f32[4,72,128]{2,1,0:T(8,128)S(1)}, f32[4,72,128]{2,1,0:T(8,128)S(1)}, u32[]{:S(2)}, u32[]{:S(2)}) collective-permute-start(f32[4,72,128]{2,1,0:T(8,128)S(1)} %get-tuple-element.13), channel_id=1, source_target_pairs={{0,4},{1,5},{2,6},{3,7},{4,8},{5,9},{6,10},{7,11},{8,12},{9,13},{1... | collective-permute-start | bytes 442376 | tf_op jit(solution)/shard_map/ppermute | solution.py:306
  55.7 7.7 %collective-permute-start.9 = (f32[4,72,128]{2,1,0:T(8,128)S(1)}, f32[4,72,128]{2,1,0:T(8,128)S(1)}, u32[]{:S(2)}, u32[]{:S(2)}) collective-permute-start(f32[4,72,128]{2,1,0:T(8,128)S(1)} %get-tuple-element.11), channel_id=1, source_target_pairs={{0,8},{1,9},{2,10},{3,11},{4,12},{5,13},{6,14},{7,15},{8,0},{9,1},... | collective-permute-start | bytes 442376 | tf_op jit(solution)/shard_map/ppermute | solution.py:306
  63.5 5.4 %collective-permute-start.14 = (f32[72,128]{1,0:T(8,128)S(1)}, f32[72,128]{1,0:T(8,128)S(1)}, u32[]{:S(2)}, u32[]{:S(2)}) collective-permute-start(f32[72,128]{1,0:T(8,128)S(1)} %get-tuple-element.15), channel_id=1, source_target_pairs={{0,3},{1,0},{2,1},{3,2},{4,7},{5,4},{6,5},{7,6},{8,11},{9,8},{10,9... | collective-permute-start | bytes 110600 | tf_op jit(solution)/shard_map/ppermute | solution.py:306
  67.3 5.2 %collective-permute-start.13 = (f32[72,128]{1,0:T(8,128)S(1)}, f32[72,128]{1,0:T(8,128)S(1)}, u32[]{:S(2)}, u32[]{:S(2)}) collective-permute-start(f32[72,128]{1,0:T(8,128)S(1)} %get-tuple-element.16), channel_id=1, source_target_pairs={{0,1},{1,2},{2,3},{3,0},{4,5},{5,6},{6,7},{7,4},{8,9},{9,10},{10,1... | collective-permute-start | bytes 110600 | tf_op jit(solution)/shard_map/ppermute | solution.py:306
  67.3 5.6 %collective-permute-start.12 = (f32[72,128]{1,0:T(8,128)S(1)}, f32[72,128]{1,0:T(8,128)S(1)}, u32[]{:S(2)}, u32[]{:S(2)}) collective-permute-start(f32[72,128]{1,0:T(8,128)S(1)} %get-tuple-element.14), channel_id=1, source_target_pairs={{0,2},{1,3},{2,0},{3,1},{4,6},{5,7},{6,4},{7,5},{8,10},{9,11},{10,... | collective-permute-start | bytes 110600 | tf_op jit(solution)/shard_map/ppermute | solution.py:306

commit v6 on v5

--- a/solution.py
+++ b/solution.py
@@ -1,3 +1,5 @@
+import functools
+
 import jax
 import jax.numpy as jnp
 import numpy as np
@@ -11,9 +13,10 @@
 LANES = 640
 RADIX = 15
 ROWS = 36
+STEPS = (2, 1, 3, 0)
 UNROLL = 16
 SAMPLES = 512
-ORDER = (("x", "y", "z"), ("z", "x", "y"))
+ORDER = (("x", "y", "z"), ("y", "x", "z"))
 AXIAL = ("x", "core")
 AZIMUTHAL = ("y", "z")
 MEAN_FLOW = 0.5
@@ -86,15 +89,18 @@
             num_scalar_prefetch=1,
             grid=(4,),
             in_specs=[pl.BlockSpec(state.shape, lambda n, c: (0, 0, 0)), mine, mine, other, other],
-            out_specs=[pl.BlockSpec((256, LANES), lambda n, c: (n, 0))] * 2
-            + [pl.BlockSpec((8, 128), lambda n, c: (0, 0))],
+            out_specs=[
+                pl.BlockSpec((256, LANES), lambda n, c: (n, 0)),
+                pl.BlockSpec((256, LANES), lambda n, c: (n, 0)),
+                pl.BlockSpec((8, 128), lambda n, c: (0, 0)),
+            ],
         ),
         out_shape=[
-            pltpu.VMEM((1024, LANES), jnp.float32),
-            pltpu.VMEM((1024, LANES), jnp.float32),
+            jax.ShapeDtypeStruct((1024, LANES), jnp.float32),
+            jax.ShapeDtypeStruct((1024, LANES), jnp.float32),
             pltpu.VMEM((8, 128), jnp.float32),
         ],
-        compiler_params=pltpu.CompilerParams(vmem_limit_bytes=32 * 1024 * 1024),
+        compiler_params=pltpu.CompilerParams(vmem_limit_bytes=16 * 1024 * 1024),
         name="first",
     )(core, state, delay, fraction, delay, fraction)
 
@@ -106,16 +112,17 @@
     return out
 
 
-def source_kernel(place_ref, own_ref, core_ref, chip_ref, even_ref, odd_ref, index_ref, count_ref, source_ref):
+def source_kernel(own_ref, core_ref, chip_ref, even_ref, odd_ref, index_ref, count_ref, source_ref):
     table = lobatto_matrix()
     point = lax.broadcasted_iota(jnp.int32, (1, 128), 1)
     axial, azimuthal = point // 8, point % 8
-    second = place_ref[0] == 1
-    odd = place_ref[1] == 1
-    no_before, no_after = place_ref[2] == 0, place_ref[2] == 7
-    core, chip = core_ref[...], chip_ref[...]
-    before_x = jnp.where(no_before, 0.0, jnp.where(second, core, chip))[0:1]
-    after_x = jnp.where(no_after, 0.0, jnp.where(second, chip, core))[0:1]
+    x, core = lax.axis_index("x"), lax.axis_index("core")
+    second = core == 1
+    odd = lax.rem(lax.axis_index("z"), 2) == 1
+    no_before, no_after = x * 2 + core == 0, x * 2 + core == 7
+    core_tile, chip = core_ref[...], chip_ref[...]
+    before_x = jnp.where(no_before, 0.0, jnp.where(second, core_tile, chip))[0:1]
+    after_x = jnp.where(no_after, 0.0, jnp.where(second, chip, core_tile))[0:1]
     even, odd_tile = even_ref[...], odd_ref[...]
     before_y = jnp.where(odd, even, odd_tile)[1:2]
     after_y = jnp.where(odd, odd_tile, even)[1:2]
@@ -197,20 +204,24 @@
     tiles = [
         lax.ppermute(tile, AXIAL + AZIMUTHAL, neighbour(kind)) for kind in ("core", "chip", "even", "odd")
     ]
-    axial = lax.axis_index(AXIAL)
-    place = jnp.stack([axial % 2, lax.axis_index(AZIMUTHAL) % 2, axial]).astype(jnp.int32)
     vmem = pl.BlockSpec(memory_space=pltpu.VMEM)
     smem = pl.BlockSpec(memory_space=pltpu.SMEM)
     return pl.pallas_call(
         source_kernel,
-        in_specs=[smem] + [vmem] * 6 + [smem],
+        in_specs=[vmem] * 6 + [smem],
         out_specs=vmem,
         out_shape=pltpu.VMEM((1, SLOTS), jnp.float32),
+        compiler_params=pltpu.CompilerParams(vmem_limit_bytes=8 * 1024 * 1024),
         name="source",
-    )(place, *in_vmem(tile, *tiles, surf_index), surf_count)
-
-
-def bins_kernel(part_ref, src_ref, src_b_ref, own_ref, sib_ref, out_ref, hi_s):
+    )(*in_vmem(tile, *tiles, surf_index), surf_count)
+
+
+def bins_kernel(ahead, src_ref, src_b_ref, both_ref, out_ref, hi_s):
+    own_ref, sib_ref = both_ref.at[0], both_ref.at[1]
+    core = lax.axis_index("core")
+    to = (here(0) + ahead) & 3
+    base = to * jnp.where(core == 0, 256, 64)
+    stride = jnp.where(core == 0, 64, 256)
     src = jnp.concatenate(
         [src_ref[:, :256], src_b_ref[:, :256], src_ref[:, 256:], src_b_ref[:, 256:],
          jnp.zeros((1, 96), jnp.float32)], axis=1)
@@ -226,7 +237,7 @@
     diag8 = lane8 == lax.broadcasted_iota(jnp.int32, (8, 128), 0)
 
     def group(g, slot):
-        row = part_ref[0] + (g // 8) * part_ref[1] + (g // 2 % 4) * part_ref[2] + (g % 2) * 8
+        row = base + (g // 8) * stride + (g % 8) * 8
         rows = pl.ds(pl.multiple_of(row, 8), 8)
         last, last_b = own_ref[rows, 512:], sib_ref[rows, 512:]
         last_k = jnp.where(first16, last, pltpu.roll(last_b, 16, 1))
@@ -280,20 +291,44 @@
     lax.fori_loop(0, 32 // UNROLL, several, 0)
 
 
-def bins(part, src, src_b, own, sibling):
+def bins(ahead, src, src_b, both):
     vmem = pl.BlockSpec(memory_space=pltpu.VMEM)
     return pl.pallas_call(
-        bins_kernel,
-        in_specs=[pl.BlockSpec(memory_space=pltpu.SMEM)] + [vmem] * 4,
+        functools.partial(bins_kernel, ahead),
+        in_specs=[vmem] * 3,
         out_specs=vmem,
         scratch_shapes=[pltpu.VMEM((UNROLL, 8, LANES), jnp.float32)],
         out_shape=pltpu.VMEM((16, 2 * ROWS, 128), jnp.float32),
-        compiler_params=pltpu.CompilerParams(vmem_limit_bytes=32 * 1024 * 1024),
+        compiler_params=pltpu.CompilerParams(vmem_limit_bytes=16 * 1024 * 1024),
         cost_estimate=pl.CostEstimate(
             flops=32 * 2 * 288 * 256 * LANES, bytes_accessed=8 * 256 * LANES, transcendentals=0
         ),
         name="bins",
-    )(part, *in_vmem(src, src_b, own, sibling))
+    )(*in_vmem(src, src_b, both))
+
+
+def keep_kernel(own_ref, sib_ref, to_ref, sems):
+    copies = [
+        pltpu.make_async_copy(array.at[pl.ds(128 * n, 128)], to_ref.at[k, pl.ds(128 * n, 128)], sems.at[k, n])
+        for n in range(8)
+        for k, array in enumerate((own_ref, sib_ref))
+    ]
+    for copy in copies:
+        copy.start()
+    for copy in copies:
+        copy.wait()
+
+
+def kept(own, sibling):
+    return pl.pallas_call(
+        keep_kernel,
+        in_specs=[pl.BlockSpec(memory_space=pl.ANY)] * 2,
+        out_specs=pl.BlockSpec(memory_space=pltpu.VMEM),
+        out_shape=pltpu.VMEM((2,) + own.shape, own.dtype),
+        scratch_shapes=[pltpu.SemaphoreType.DMA((2, 8))],
+        compiler_params=pltpu.CompilerParams(vmem_limit_bytes=8 * 1024 * 1024),
+        name="kept",
+    )(own, sibling)
 
 
 def shifted(array, phase, step):
@@ -306,33 +341,48 @@
     return lax.ppermute(array, AXIAL + AZIMUTHAL, moves)
 
 
-def summed(source, source_b, own, sibling):
-    core = lax.axis_index("core")
-    pick = lambda of: jnp.where(core == 0, of(ORDER[0]), of(ORDER[1]))
-    here = [pick(lambda order: lax.axis_index(order[phase])) for phase in range(3)]
-    rows = {"x": 256, "y": 64, "z": 16}
-    steps = [pick(lambda order: rows[order[phase]]) for phase in range(3)]
-    got = []
-    for d in (2, 1, 3, 0):
-        part = jnp.stack([(here[0] + d) % 4 * steps[0], steps[1], steps[2]]).astype(jnp.int32)
-        sums = bins(part, source, source_b, own, sibling)
-        got.append(shifted(sums, 0, d) if d else sums)
-    total = (got[0] + got[1] + got[2] + got[3]).reshape(4, 4, 2 * ROWS, 128)
-    for phase in (1, 2):
-        block = lambda d: lax.dynamic_index_in_dim(total, (here[phase] + d) % 4, 0, keepdims=False)
-        got = [shifted(block(d), phase, d) for d in (2, 1, 3)]
-        total = block(0) + got[0] + got[1] + got[2]
-    return total
+def here(phase):
+    return jnp.where(
+        lax.axis_index("core") == 0, lax.axis_index(ORDER[0][phase]), lax.axis_index(ORDER[1][phase])
+    )
+
+
+def merge_kernel(phase, *refs):
+    pieces, blocks = refs[:4], refs[4:]
+    for block, step in zip(blocks, STEPS):
+        at = (here(phase) + step) & 3
+        block[...] = (pieces[0][at] + pieces[1][at]) + (pieces[2][at] + pieces[3][at])
+
+
+def merged(pieces, phase):
+    vmem = pl.BlockSpec(memory_space=pltpu.VMEM)
+    return pl.pallas_call(
+        functools.partial(merge_kernel, phase),
+        in_specs=[vmem] * 4,
+        out_specs=[vmem] * 4,
+        out_shape=[pltpu.VMEM(pieces[0].shape[1:], jnp.float32)] * 4,
+        compiler_params=pltpu.CompilerParams(vmem_limit_bytes=8 * 1024 * 1024),
+        name="merged",
+    )(*in_vmem(*pieces))
+
+
+def summed(source, source_b, both):
+    blocks = [bins(step, source, source_b, both) for step in STEPS]
+    for phase in range(3):
+        blocks = [shifted(block, phase, step) if step else block for block, step in zip(blocks, STEPS)]
+        if phase < 2:
+            blocks = merged([block.reshape((4, -1) + block.shape[-2:]) if block.shape[0] == 16 else block for block in blocks], phase + 1)
+    return (blocks[0] + blocks[1]) + (blocks[2] + blocks[3])
 
 
 def local(state, surf_index, surf_count, delay, fraction):
     core = lax.axis_index("core").reshape(1)
     swap = [(0, 1), (1, 0)]
     own, other, tile = first(core, state, delay, fraction)
-    sibling = lax.ppermute(other, "core", swap)
+    both = kept(own, lax.ppermute(other, "core", swap))
     source = slot_source(tile, surf_index, surf_count)
     source_b = lax.ppermute(source, "core", swap)
-    total = summed(source, source_b, own, sibling)
+    total = summed(source, source_b, both)
     total = total.reshape(2, ROWS, 16, 8).transpose(0, 3, 1, 2).reshape(16, ROWS, 16)
     carry = jnp.pad(total[:, :34, 15:], ((0, 0), (1, 0), (0, 14)))
     return (total[:, :35, :RADIX] + carry).reshape(16, 35 * RADIX)[:, :SAMPLES]

time: 74.6 us -> 60.9 us (0.82)
  Pallas kernels: 32.1 us -> 23.3 us
  waiting for transfers between devices: 15.9 us -> 11.1 us
  other arithmetic: 2.56 us -> 0.1 us
  starting transfers between devices: 21.6 us -> 23.7 us
    pallas_call x5 -> x8, Pallas kernels: 26.8 us -> 19.2 us  [the longest x4 16.9 us: bins(): pl.pallas_call(functools.partial(bins_kernel, ahead), in_specs=[vmem] * 3...]
    ppermute x9, waiting for transfers between devices: 14.3 us -> 10 us  [shifted(): return lax.ppermute(array, AXIAL + AZIMUTHAL, moves)]
    ppermute x9, starting transfers between devices: 11.7 us -> 14.5 us  [shifted(): return lax.ppermute(array, AXIAL + AZIMUTHAL, moves)]
    add x3 -> x1, other arithmetic: 1.58 us -> 0.01 us  [summed(): return blocks[0] + blocks[1] + (blocks[2] + blocks[3])]
    pallas_call x1, Pallas kernels: 5.34 us -> 4.09 us  [first(): pl.pallas_call(first_kernel, grid_spec=pltpu.PrefetchScalarGridSpec(num_s...]
    ppermute x1, waiting for transfers between devices: 1.06 us -> 0.01 us  [local(): source_b = lax.ppermute(source, 'core', swap)]
    another operation x5 -> x0, other arithmetic: 0.9 us -> none  [the longest x1 0.59 us: slot_source(): jnp.stack([axial % 2, lax.axis_index(AZIMUTHAL) % 2, axial])]
  transfers between devices with their start and end apart: 15 -> 15, of which waited for: 8 -> 7; matrix products, arithmetic and copies ran while one was open for 1% -> 0% of each run, Pallas kernels for 28% -> 25%
where the time goes in v6:
time: 60.9 us; the launch traced here: 60.3 us
  starting transfers between devices  23.7 us (39%)
  Pallas kernels  23.3 us (38%)
  waiting for transfers between devices  11.1 us (18%)
  local copies, waits for them, and re-layouts  1.26 us (2%)
  between operations  0.81 us (1%)
    pallas_call x4, Pallas kernels, bins(): pl.pallas_call(functools.partial(bins_kernel, ahead), in_specs=[vmem] * 3...  16.9 us
    ppermute x9, starting transfers between devices, shifted(): return lax.ppermute(array, AXIAL + AZIMUTHAL, moves)  14.5 us
    ppermute x9, waiting for transfers between devices, shifted(): return lax.ppermute(array, AXIAL + AZIMUTHAL, moves)  10 us
    ppermute x4, starting transfers between devices, slot_source(): lax.ppermute(tile, AXIAL + AZIMUTHAL, neighbour(kind))  9.18 us
    pallas_call x1, Pallas kernels, first(): pl.pallas_call(first_kernel, grid_spec=pltpu.PrefetchScalarGridSpec(num_s...  4.09 us
    pallas_call x1, Pallas kernels, kept(): pl.pallas_call(keep_kernel, in_specs=[pl.BlockSpec(memory_space=pl.ANY)]...  1.8 us
  transfers between devices with their start and end apart: 15, of which 7 were waited for; matrix products, arithmetic and copies ran while one was open for 0% of the time, Pallas kernels for 25%

profile of v6, /device:TPU:0, one launch (start us, length us, event | category | flops | bytes accessed | tf_op | source)
XLA Modules:
  0.0 60.3 jit_solution(3760934033222346814)
XLA Ops:
  0.0 0.0 copy-start
  0.0 4.1 %first.1 = (f32[1024,640]{1,0:T(8,128)S(1)}, f32[1024,640]{1,0:T(8,128)S(1)}, f32[8,128]{1,0:T(8,128)S(1)}) custom-call(s32[1]{0:T(128)} %bitcast.core_ref, f32[5,64,128]{2,1,0:T(8,128)} %bitcast.17, s32[272,2048]{1,0:T(8,128)} %other_delay.1, f32[272,2048]{1,0:T(8,128)} %other_fraction.1, s32[272,2048]{1,0:T(8,128)} %other_delay.1, f32[272,2048]{1,0:T(8,128)} %other_fraction.1), custom_call_target="tpu_custom_call" | custom-call | tf_op jit(solution)/shard_map/first/pallas_call | solution.py:86
  4.1 0.1 collective-permute-start.5
  4.2 6.7 %collective-permute-start.3 = (f32[8,128]{1,0:T(8,128)S(1)}, f32[8,128]{1,0:T(8,128)S(1)}, u32[]{:S(2)}, u32[]{:S(2)}) collective-permute-start(f32[8,128]{1,0:T(8,128)S(1)} %get-tuple-element.16.own_ref), channel_id=1, source_target_pairs={{0,15},{1,2},{2,1},{3,4},{4,3},{5,6},{6,5},{7,8},{8,7},{9,10},{10,... | collective-permute-start | bytes 12296 | tf_op jit(solution)/shard_map/ppermute | solution.py:205
  10.9 0.0 collective-permute-start.2
  10.9 2.5 %collective-permute-start.1 = (f32[8,128]{1,0:T(8,128)S(1)}, f32[8,128]{1,0:T(8,128)S(1)}, u32[]{:S(2)}, u32[]{:S(2)}) collective-permute-start(f32[8,128]{1,0:T(8,128)S(1)} %get-tuple-element.16.own_ref), channel_id=1, source_target_pairs={{0,112},{1,113},{2,114},{3,115},{4,116},{5,117},{6,118},{7,119},{8... | collective-permute-start | bytes 12296 | tf_op jit(solution)/shard_map/ppermute | solution.py:205
  13.4 0.0 collective-permute-start
  14.0 0.0 collective-permute-done.3.odd_ref
  14.0 0.4 collective-permute-done.2.even_ref
  14.5 0.6 %collective-permute-done.1.chip_ref = f32[8,128]{1,0:T(8,128)S(1)} collective-permute-done((f32[8,128]{1,0:T(8,128)S(1)}, f32[8,128]{1,0:T(8,128)S(1)}, u32[]{:S(2)}, u32[]{:S(2)}) %collective-permute-start.1) | collective-permute-done | bytes 4128 | tf_op jit(solution)/shard_map/ppermute | solution.py:205
  15.1 0.0 collective-permute-done.core_ref
  15.1 0.0 copy-done
  15.1 0.3 source.1.src_ref
  15.4 0.0 collective-permute-start.4
  15.4 0.0 collective-permute-done.5.sib_ref
  15.4 1.8 %kept.1.both_ref = f32[2,1024,640]{2,1,0:T(8,128)S(1)} custom-call(f32[1024,640]{1,0:T(8,128)S(1)} %get-tuple-element.17.own_ref, f32[1024,640]{1,0:T(8,128)S(1)} %collective-permute-done.5.sib_ref), custom_call_target="tpu_custom_call" | custom-call | tf_op jit(solution)/shard_map/kept/pallas_call | solution.py:323
  17.2 0.0 collective-permute-done.4.src_b_ref
  17.2 4.2 %bins.4 = f32[16,72,128]{2,1,0:T(8,128)S(1)} custom-call(f32[1,272]{1,0:T(1,128)S(1)} %source.1.src_ref, f32[1,272]{1,0:T(1,128)S(1)} %collective-permute-done.4.src_b_ref, f32[2,1024,640]{2,1,0:T(8,128)S(1)} %kept.1.both_ref), custom_call_target="tpu_custom_call" | custom-call | flops 3019898880 | bytes 1310720 | tf_op jit(solution)/shard_map/bins/pallas_call | solution.py:296
  21.5 2.5 %collective-permute-start.6 = (f32[16,72,128]{2,1,0:T(8,128)S(1)}, f32[16,72,128]{2,1,0:T(8,128)S(1)}, u32[]{:S(2)}, u32[]{:S(2)}) collective-permute-start(f32[16,72,128]{2,1,0:T(8,128)S(1)} %bins.4), channel_id=1, source_target_pairs={{0,64},{1,65},{2,66},{3,67},{4,68},{5,69},{6,70},{7,71},{8,72},{9,... | collective-permute-start | bytes 1769480 | tf_op jit(solution)/shard_map/ppermute | solution.py:341
  24.0 4.2 %bins.5 = f32[16,72,128]{2,1,0:T(8,128)S(1)} custom-call(f32[1,272]{1,0:T(1,128)S(1)} %source.1.src_ref, f32[1,272]{1,0:T(1,128)S(1)} %collective-permute-done.4.src_b_ref, f32[2,1024,640]{2,1,0:T(8,128)S(1)} %kept.1.both_ref), custom_call_target="tpu_custom_call" | custom-call | flops 3019898880 | bytes 1310720 | tf_op jit(solution)/shard_map/bins/pallas_call | solution.py:296
  28.2 1.4 %collective-permute-start.7 = (f32[16,72,128]{2,1,0:T(8,128)S(1)}, f32[16,72,128]{2,1,0:T(8,128)S(1)}, u32[]{:S(2)}, u32[]{:S(2)}) collective-permute-start(f32[16,72,128]{2,1,0:T(8,128)S(1)} %bins.5), channel_id=1, source_target_pairs={{0,32},{1,33},{2,34},{3,35},{4,36},{5,37},{6,38},{7,39},{8,40},{9,... | collective-permute-start | bytes 1769480 | tf_op jit(solution)/shard_map/ppermute | solution.py:341
  29.6 4.2 %bins.6 = f32[16,72,128]{2,1,0:T(8,128)S(1)} custom-call(f32[1,272]{1,0:T(1,128)S(1)} %source.1.src_ref, f32[1,272]{1,0:T(1,128)S(1)} %collective-permute-done.4.src_b_ref, f32[2,1024,640]{2,1,0:T(8,128)S(1)} %kept.1.both_ref), custom_call_target="tpu_custom_call" | custom-call | flops 3019898880 | bytes 1310720 | tf_op jit(solution)/shard_map/bins/pallas_call | solution.py:296
  33.9 2.1 %collective-permute-start.8 = (f32[16,72,128]{2,1,0:T(8,128)S(1)}, f32[16,72,128]{2,1,0:T(8,128)S(1)}, u32[]{:S(2)}, u32[]{:S(2)}) collective-permute-start(f32[16,72,128]{2,1,0:T(8,128)S(1)} %bins.6), channel_id=1, source_target_pairs={{0,96},{1,97},{2,98},{3,99},{4,100},{5,101},{6,102},{7,103},{8,104... | collective-permute-start | bytes 1769480 | tf_op jit(solution)/shard_map/ppermute | solution.py:341
  36.0 4.2 %bins.7 = f32[16,72,128]{2,1,0:T(8,128)S(1)} custom-call(f32[1,272]{1,0:T(1,128)S(1)} %source.1.src_ref, f32[1,272]{1,0:T(1,128)S(1)} %collective-permute-done.4.src_b_ref, f32[2,1024,640]{2,1,0:T(8,128)S(1)} %kept.1.both_ref), custom_call_target="tpu_custom_call" | custom-call | flops 3019898880 | bytes 1310720 | tf_op jit(solution)/shard_map/bins/pallas_call | solution.py:296
  40.2 0.0 collective-permute-done.6
  40.3 0.0 collective-permute-done.7
  40.3 3.7 %collective-permute-done.8 = f32[16,72,128]{2,1,0:T(8,128)S(1)} collective-permute-done((f32[16,72,128]{2,1,0:T(8,128)S(1)}, f32[16,72,128]{2,1,0:T(8,128)S(1)}, u32[]{:S(2)}, u32[]{:S(2)}) %collective-permute-start.8) | collective-permute-done | bytes 589856 | tf_op jit(solution)/shard_map/ppermute | solution.py:341
  44.0 0.1 merged.2
  44.1 0.7 %collective-permute-start.9 = (f32[4,72,128]{2,1,0:T(8,128)S(1)}, f32[4,72,128]{2,1,0:T(8,128)S(1)}, u32[]{:S(2)}, u32[]{:S(2)}) collective-permute-start(f32[4,72,128]{2,1,0:T(8,128)S(1)} %get-tuple-element.19), channel_id=1, source_target_pairs={{0,8},{1,9},{2,10},{3,11},{4,12},{5,13},{6,14},{7,15},{8,0},{9,1},... | collective-permute-start | bytes 442376 | tf_op jit(solution)/shard_map/ppermute | solution.py:341
  44.9 1.0 %collective-permute-start.10 = (f32[4,72,128]{2,1,0:T(8,128)S(1)}, f32[4,72,128]{2,1,0:T(8,128)S(1)}, u32[]{:S(2)}, u32[]{:S(2)}) collective-permute-start(f32[4,72,128]{2,1,0:T(8,128)S(1)} %get-tuple-element.20), channel_id=1, source_target_pairs={{0,4},{1,5},{2,6},{3,7},{4,8},{5,9},{6,10},{7,11},{8,12},{9,13},{1... | collective-permute-start | bytes 442376 | tf_op jit(solution)/shard_map/ppermute | solution.py:341
  45.8 2.3 %collective-permute-start.11 = (f32[4,72,128]{2,1,0:T(8,128)S(1)}, f32[4,72,128]{2,1,0:T(8,128)S(1)}, u32[]{:S(2)}, u32[]{:S(2)}) collective-permute-start(f32[4,72,128]{2,1,0:T(8,128)S(1)} %get-tuple-element.21), channel_id=1, source_target_pairs={{0,12},{1,13},{2,14},{3,15},{4,0},{5,1},{6,2},{7,3},{8,4},{9,5},{1... | collective-permute-start | bytes 442376 | tf_op jit(solution)/shard_map/ppermute | solution.py:341
  48.1 2.9 %collective-permute-done.9.refs_0_ = f32[4,72,128]{2,1,0:T(8,128)S(1)} collective-permute-done((f32[4,72,128]{2,1,0:T(8,128)S(1)}, f32[4,72,128]{2,1,0:T(8,128)S(1)}, u32[]{:S(2)}, u32[]{:S(2)}) %collective-permute-start.9) | collective-permute-done | bytes 147488 | tf_op jit(solution)/shard_map/ppermute | solution.py:341
  51.0 1.5 %collective-permute-done.10.refs_1_ = f32[4,72,128]{2,1,0:T(8,128)S(1)} collective-permute-done((f32[4,72,128]{2,1,0:T(8,128)S(1)}, f32[4,72,128]{2,1,0:T(8,128)S(1)}, u32[]{:S(2)}, u32[]{:S(2)}) %collective-permute-start.10) | collective-permute-done | bytes 147488 | tf_op jit(solution)/shard_map/ppermute | solution.py:341
  52.5 0.0 collective-permute-done.11.refs_2_
  52.5 0.4 collective-permute-start.12
  52.9 1.6 %collective-permute-start.13 = (f32[72,128]{1,0:T(8,128)S(1)}, f32[72,128]{1,0:T(8,128)S(1)}, u32[]{:S(2)}, u32[]{:S(2)}) collective-permute-start(f32[72,128]{1,0:T(8,128)S(1)} %get-tuple-element.24), channel_id=1, source_target_pairs={{0,1},{1,2},{2,3},{3,0},{4,5},{5,6},{6,7},{7,4},{8,9},{9,10},{10,1... | collective-permute-start | bytes 110600 | tf_op jit(solution)/shard_map/ppermute | solution.py:341
  54.5 2.5 %collective-permute-start.14 = (f32[72,128]{1,0:T(8,128)S(1)}, f32[72,128]{1,0:T(8,128)S(1)}, u32[]{:S(2)}, u32[]{:S(2)}) collective-permute-start(f32[72,128]{1,0:T(8,128)S(1)} %get-tuple-element.25), channel_id=1, source_target_pairs={{0,3},{1,0},{2,1},{3,2},{4,7},{5,4},{6,5},{7,6},{8,11},{9,8},{10,9... | collective-permute-start | bytes 110600 | tf_op jit(solution)/shard_map/ppermute | solution.py:341
  57.0 1.0 %collective-permute-done.12 = f32[72,128]{1,0:T(8,128)S(1)} collective-permute-done((f32[72,128]{1,0:T(8,128)S(1)}, f32[72,128]{1,0:T(8,128)S(1)}, u32[]{:S(2)}, u32[]{:S(2)}) %collective-permute-start.12) | collective-permute-done | bytes 36896 | tf_op jit(solution)/shard_map/ppermute | solution.py:341
  58.0 0.9 %collective-permute-done.13 = f32[72,128]{1,0:T(8,128)S(1)} collective-permute-done((f32[72,128]{1,0:T(8,128)S(1)}, f32[72,128]{1,0:T(8,128)S(1)}, u32[]{:S(2)}, u32[]{:S(2)}) %collective-permute-start.13) | collective-permute-done | bytes 36896 | tf_op jit(solution)/shard_map/ppermute | solution.py:341
  58.9 0.0 collective-permute-done.14
  58.9 0.1 copy.6
  59.0 0.1 reshape.33
  59.2 0.1 slice_add_fusion
  59.3 0.2 copy.8
  59.6 0.1 reshape.35
  59.7 0.6 %slice.14 = f32[16,512]{1,0:T(8,128)} slice(f32[16,525]{1,0:T(8,128)S(1)} %reshape.35), slice={[0:16], [0:512]} | slice | bytes 65536 | tf_op jit(solution)/shard_map/slice | solution.py:388
  (4 shorter events, 0.1 us)
Async XLA Ops:
  0.0 15.1 %copy-start = (s32[272]{0:T(512)S(1)}, s32[272]{0:T(512)}, u32[]{:S(2)}) copy-start(s32[272]{0:T(512)} %index_ref.1) | copy-start | bytes 3268
  4.1 11.3 %collective-permute-start.5 = (f32[1024,640]{1,0:T(8,128)S(1)}, f32[1024,640]{1,0:T(8,128)S(1)}, u32[]{:S(2)}, u32[]{:S(2)}) collective-permute-start(f32[1024,640]{1,0:T(8,128)S(1)} %get-tuple-element.18), channel_id=1, source_target_pairs={{0,16},{16,0},{1,17},{17,1},{2,18},{18,2},{3,19},{19,3},{4,20},{20... | collective-permute-start | bytes 7864328 | tf_op jit(solution)/shard_map/ppermute | solution.py:382
  4.2 9.8 %collective-permute-start.3 = (f32[8,128]{1,0:T(8,128)S(1)}, f32[8,128]{1,0:T(8,128)S(1)}, u32[]{:S(2)}, u32[]{:S(2)}) collective-permute-start(f32[8,128]{1,0:T(8,128)S(1)} %get-tuple-element.16.own_ref), channel_id=1, source_target_pairs={{0,15},{1,2},{2,1},{3,4},{4,3},{5,6},{6,5},{7,8},{8,7},{9,10},{10,... | collective-permute-start | bytes 12296 | tf_op jit(solution)/shard_map/ppermute | solution.py:205
  10.9 3.6 %collective-permute-start.2 = (f32[8,128]{1,0:T(8,128)S(1)}, f32[8,128]{1,0:T(8,128)S(1)}, u32[]{:S(2)}, u32[]{:S(2)}) collective-permute-start(f32[8,128]{1,0:T(8,128)S(1)} %get-tuple-element.16.own_ref), channel_id=1, source_target_pairs={{0,1},{1,0},{2,3},{3,2},{4,5},{5,4},{6,7},{7,6},{8,9},{9,8},{10,11... | collective-permute-start | bytes 12296 | tf_op jit(solution)/shard_map/ppermute | solution.py:205
  10.9 4.2 %collective-permute-start.1 = (f32[8,128]{1,0:T(8,128)S(1)}, f32[8,128]{1,0:T(8,128)S(1)}, u32[]{:S(2)}, u32[]{:S(2)}) collective-permute-start(f32[8,128]{1,0:T(8,128)S(1)} %get-tuple-element.16.own_ref), channel_id=1, source_target_pairs={{0,112},{1,113},{2,114},{3,115},{4,116},{5,117},{6,118},{7,119},{8... | collective-permute-start | bytes 12296 | tf_op jit(solution)/shard_map/ppermute | solution.py:205
  13.4 1.7 %collective-permute-start = (f32[8,128]{1,0:T(8,128)S(1)}, f32[8,128]{1,0:T(8,128)S(1)}, u32[]{:S(2)}, u32[]{:S(2)}) collective-permute-start(f32[8,128]{1,0:T(8,128)S(1)} %get-tuple-element.16.own_ref), channel_id=1, source_target_pairs={{0,16},{1,17},{2,18},{3,19},{4,20},{5,21},{6,22},{7,23},{8,24},{9,... | collective-permute-start | bytes 12296 | tf_op jit(solution)/shard_map/ppermute | solution.py:205
  15.4 1.8 %collective-permute-start.4 = (f32[1,272]{1,0:T(1,128)S(1)}, f32[1,272]{1,0:T(1,128)S(1)}, u32[]{:S(2)}, u32[]{:S(2)}) collective-permute-start(f32[1,272]{1,0:T(1,128)S(1)} %source.1.src_ref), channel_id=1, source_target_pairs={{0,16},{16,0},{1,17},{17,1},{2,18},{18,2},{3,19},{19,3},{4,20},{20... | collective-permute-start | bytes 3272 | tf_op jit(solution)/shard_map/ppermute | solution.py:384
  21.5 18.8 %collective-permute-start.6 = (f32[16,72,128]{2,1,0:T(8,128)S(1)}, f32[16,72,128]{2,1,0:T(8,128)S(1)}, u32[]{:S(2)}, u32[]{:S(2)}) collective-permute-start(f32[16,72,128]{2,1,0:T(8,128)S(1)} %bins.4), channel_id=1, source_target_pairs={{0,64},{1,65},{2,66},{3,67},{4,68},{5,69},{6,70},{7,71},{8,72},{9,... | collective-permute-start | bytes 1769480 | tf_op jit(solution)/shard_map/ppermute | solution.py:341
  28.2 12.1 %collective-permute-start.7 = (f32[16,72,128]{2,1,0:T(8,128)S(1)}, f32[16,72,128]{2,1,0:T(8,128)S(1)}, u32[]{:S(2)}, u32[]{:S(2)}) collective-permute-start(f32[16,72,128]{2,1,0:T(8,128)S(1)} %bins.5), channel_id=1, source_target_pairs={{0,32},{1,33},{2,34},{3,35},{4,36},{5,37},{6,38},{7,39},{8,40},{9,... | collective-permute-start | bytes 1769480 | tf_op jit(solution)/shard_map/ppermute | solution.py:341
  33.9 10.1 %collective-permute-start.8 = (f32[16,72,128]{2,1,0:T(8,128)S(1)}, f32[16,72,128]{2,1,0:T(8,128)S(1)}, u32[]{:S(2)}, u32[]{:S(2)}) collective-permute-start(f32[16,72,128]{2,1,0:T(8,128)S(1)} %bins.6), channel_id=1, source_target_pairs={{0,96},{1,97},{2,98},{3,99},{4,100},{5,101},{6,102},{7,103},{8,104... | collective-permute-start | bytes 1769480 | tf_op jit(solution)/shard_map/ppermute | solution.py:341
  44.1 6.8 %collective-permute-start.9 = (f32[4,72,128]{2,1,0:T(8,128)S(1)}, f32[4,72,128]{2,1,0:T(8,128)S(1)}, u32[]{:S(2)}, u32[]{:S(2)}) collective-permute-start(f32[4,72,128]{2,1,0:T(8,128)S(1)} %get-tuple-element.19), channel_id=1, source_target_pairs={{0,8},{1,9},{2,10},{3,11},{4,12},{5,13},{6,14},{7,15},{8,0},{9,1},... | collective-permute-start | bytes 442376 | tf_op jit(solution)/shard_map/ppermute | solution.py:341
  44.9 7.6 %collective-permute-start.10 = (f32[4,72,128]{2,1,0:T(8,128)S(1)}, f32[4,72,128]{2,1,0:T(8,128)S(1)}, u32[]{:S(2)}, u32[]{:S(2)}) collective-permute-start(f32[4,72,128]{2,1,0:T(8,128)S(1)} %get-tuple-element.20), channel_id=1, source_target_pairs={{0,4},{1,5},{2,6},{3,7},{4,8},{5,9},{6,10},{7,11},{8,12},{9,13},{1... | collective-permute-start | bytes 442376 | tf_op jit(solution)/shard_map/ppermute | solution.py:341
  45.8 6.6 %collective-permute-start.11 = (f32[4,72,128]{2,1,0:T(8,128)S(1)}, f32[4,72,128]{2,1,0:T(8,128)S(1)}, u32[]{:S(2)}, u32[]{:S(2)}) collective-permute-start(f32[4,72,128]{2,1,0:T(8,128)S(1)} %get-tuple-element.21), channel_id=1, source_target_pairs={{0,12},{1,13},{2,14},{3,15},{4,0},{5,1},{6,2},{7,3},{8,4},{9,5},{1... | collective-permute-start | bytes 442376 | tf_op jit(solution)/shard_map/ppermute | solution.py:341
  52.5 5.5 %collective-permute-start.12 = (f32[72,128]{1,0:T(8,128)S(1)}, f32[72,128]{1,0:T(8,128)S(1)}, u32[]{:S(2)}, u32[]{:S(2)}) collective-permute-start(f32[72,128]{1,0:T(8,128)S(1)} %get-tuple-element.23), channel_id=1, source_target_pairs={{0,2},{1,3},{2,0},{3,1},{4,6},{5,7},{6,4},{7,5},{8,10},{9,11},{10,... | collective-permute-start | bytes 110600 | tf_op jit(solution)/shard_map/ppermute | solution.py:341
  52.9 6.0 %collective-permute-start.13 = (f32[72,128]{1,0:T(8,128)S(1)}, f32[72,128]{1,0:T(8,128)S(1)}, u32[]{:S(2)}, u32[]{:S(2)}) collective-permute-start(f32[72,128]{1,0:T(8,128)S(1)} %get-tuple-element.24), channel_id=1, source_target_pairs={{0,1},{1,2},{2,3},{3,0},{4,5},{5,6},{6,7},{7,4},{8,9},{9,10},{10,1... | collective-permute-start | bytes 110600 | tf_op jit(solution)/shard_map/ppermute | solution.py:341
  54.5 4.4 %collective-permute-start.14 = (f32[72,128]{1,0:T(8,128)S(1)}, f32[72,128]{1,0:T(8,128)S(1)}, u32[]{:S(2)}, u32[]{:S(2)}) collective-permute-start(f32[72,128]{1,0:T(8,128)S(1)} %get-tuple-element.25), channel_id=1, source_target_pairs={{0,3},{1,0},{2,1},{3,2},{4,7},{5,4},{6,5},{7,6},{8,11},{9,8},{10,9... | collective-permute-start | bytes 110600 | tf_op jit(solution)/shard_map/ppermute | solution.py:341

commit v7 on v6

--- a/solution.py
+++ b/solution.py
@@ -14,7 +14,6 @@
 RADIX = 15
 ROWS = 36
 STEPS = (2, 1, 3, 0)
-UNROLL = 16
 SAMPLES = 512
 ORDER = (("x", "y", "z"), ("y", "x", "z"))
 AXIAL = ("x", "core")
@@ -42,14 +41,18 @@
 
 
 def first_kernel(core_ref, state_ref, own_delay, own_fraction, other_delay, other_fraction, own_ref, other_ref, tile_ref):
+    own_block = own_ref.at[pl.ds(pl.multiple_of(pl.program_id(0) * 256, 256), 256)]
     for delay, fraction, out in (
-        (own_delay, own_fraction, own_ref),
+        (own_delay, own_fraction, own_block),
         (other_delay, other_fraction, other_ref),
     ):
         for at in (0, 128):
             rows = slice(at, at + 128)
+            two = (delay[0:128, rows] + 512 * delay[128:256, rows]).astype(jnp.float32).T
+            second = jnp.floor(two * (1.0 / 512.0))
+            out[rows, 0:128] = two - 512.0 * second
+            out[rows, 128:256] = second
             for base in (0, 128):
-                out[rows, base : base + 128] = delay[base : base + 128, rows].astype(jnp.float32).T
                 out[rows, 256 + base : 384 + base] = fraction[base : base + 128, rows].T
             rest = [
                 delay[256:272, rows].astype(jnp.float32),
@@ -90,13 +93,13 @@
             grid=(4,),
             in_specs=[pl.BlockSpec(state.shape, lambda n, c: (0, 0, 0)), mine, mine, other, other],
             out_specs=[
-                pl.BlockSpec((256, LANES), lambda n, c: (n, 0)),
+                pl.BlockSpec(memory_space=pltpu.VMEM),
                 pl.BlockSpec((256, LANES), lambda n, c: (n, 0)),
                 pl.BlockSpec((8, 128), lambda n, c: (0, 0)),
             ],
         ),
         out_shape=[
-            jax.ShapeDtypeStruct((1024, LANES), jnp.float32),
+            pltpu.VMEM((1024, LANES), jnp.float32),
             jax.ShapeDtypeStruct((1024, LANES), jnp.float32),
             pltpu.VMEM((8, 128), jnp.float32),
         ],
@@ -216,8 +219,7 @@
     )(*in_vmem(tile, *tiles, surf_index), surf_count)
 
 
-def bins_kernel(ahead, src_ref, src_b_ref, both_ref, out_ref, hi_s):
-    own_ref, sib_ref = both_ref.at[0], both_ref.at[1]
+def bins_kernel(ahead, start, count, src_ref, src_b_ref, own_ref, sib_ref, out_ref, hi_s):
     core = lax.axis_index("core")
     to = (here(0) + ahead) & 3
     base = to * jnp.where(core == 0, 256, 64)
@@ -282,53 +284,46 @@
         extra = [jnp.sum(jnp.where(diag8, r[256 + 8 * e:264 + 8 * e], 0.0), axis=0, keepdims=True) for e in range(4)]
         return jnp.concatenate([main] + extra, axis=0)
 
-    def several(p, _):
-        for t in range(0, UNROLL, 2):
-            g = UNROLL * p + t
-            out_ref[g // 2] = jnp.concatenate([group(g, t), group(g + 1, t + 1)], axis=0)
-        return 0
-
-    lax.fori_loop(0, 32 // UNROLL, several, 0)
-
-
-def bins(ahead, src, src_b, both):
+    for t in range(0, count, 2):
+        out_ref[t // 2] = jnp.concatenate([group(start + t, t), group(start + t + 1, t + 1)], axis=0)
+
+
+def bins(ahead, half, src, src_b, own, sibling):
     vmem = pl.BlockSpec(memory_space=pltpu.VMEM)
+    start, count = (0, 32) if half is None else (16 * half, 16)
     return pl.pallas_call(
-        functools.partial(bins_kernel, ahead),
-        in_specs=[vmem] * 3,
+        functools.partial(bins_kernel, ahead, start, count),
+        in_specs=[vmem] * 4,
         out_specs=vmem,
-        scratch_shapes=[pltpu.VMEM((UNROLL, 8, LANES), jnp.float32)],
-        out_shape=pltpu.VMEM((16, 2 * ROWS, 128), jnp.float32),
+        scratch_shapes=[pltpu.VMEM((count, 8, LANES), jnp.float32)],
+        out_shape=pltpu.VMEM((count // 2, 2 * ROWS, 128), jnp.float32),
         compiler_params=pltpu.CompilerParams(vmem_limit_bytes=16 * 1024 * 1024),
         cost_estimate=pl.CostEstimate(
             flops=32 * 2 * 288 * 256 * LANES, bytes_accessed=8 * 256 * LANES, transcendentals=0
         ),
         name="bins",
-    )(*in_vmem(src, src_b, both))
-
-
-def keep_kernel(own_ref, sib_ref, to_ref, sems):
-    copies = [
-        pltpu.make_async_copy(array.at[pl.ds(128 * n, 128)], to_ref.at[k, pl.ds(128 * n, 128)], sems.at[k, n])
-        for n in range(8)
-        for k, array in enumerate((own_ref, sib_ref))
-    ]
+    )(*in_vmem(src, src_b, own, sibling))
+
+
+def keep_kernel(from_ref, to_ref, sems):
+    rows = [pl.ds(128 * n, 128) for n in range(8)]
+    copies = [pltpu.make_async_copy(from_ref.at[r], to_ref.at[r], sems.at[n]) for n, r in enumerate(rows)]
     for copy in copies:
         copy.start()
     for copy in copies:
         copy.wait()
 
 
-def kept(own, sibling):
+def kept(array):
     return pl.pallas_call(
         keep_kernel,
-        in_specs=[pl.BlockSpec(memory_space=pl.ANY)] * 2,
+        in_specs=[pl.BlockSpec(memory_space=pl.ANY)],
         out_specs=pl.BlockSpec(memory_space=pltpu.VMEM),
-        out_shape=pltpu.VMEM((2,) + own.shape, own.dtype),
-        scratch_shapes=[pltpu.SemaphoreType.DMA((2, 8))],
+        out_shape=pltpu.VMEM(array.shape, array.dtype),
+        scratch_shapes=[pltpu.SemaphoreType.DMA((8,))],
         compiler_params=pltpu.CompilerParams(vmem_limit_bytes=8 * 1024 * 1024),
         name="kept",
-    )(own, sibling)
+    )(array)
 
 
 def shifted(array, phase, step):
@@ -348,17 +343,21 @@
 
 
 def merge_kernel(phase, *refs):
-    pieces, blocks = refs[:4], refs[4:]
+    pieces, blocks = refs[:-4], refs[-4:]
     for block, step in zip(blocks, STEPS):
         at = (here(phase) + step) & 3
-        block[...] = (pieces[0][at] + pieces[1][at]) + (pieces[2][at] + pieces[3][at])
+        total = pieces[0][at] + pieces[1][at] + pieces[-1][at]
+        if len(pieces) == 4:
+            block[...] = total + pieces[2][at]
+        else:
+            block[...] = total + jnp.where(at < 2, pieces[2][at & 1], pieces[3][at & 1])
 
 
 def merged(pieces, phase):
     vmem = pl.BlockSpec(memory_space=pltpu.VMEM)
     return pl.pallas_call(
         functools.partial(merge_kernel, phase),
-        in_specs=[vmem] * 4,
+        in_specs=[vmem] * len(pieces),
         out_specs=[vmem] * 4,
         out_shape=[pltpu.VMEM(pieces[0].shape[1:], jnp.float32)] * 4,
         compiler_params=pltpu.CompilerParams(vmem_limit_bytes=8 * 1024 * 1024),
@@ -366,12 +365,16 @@
     )(*in_vmem(*pieces))
 
 
-def summed(source, source_b, both):
-    blocks = [bins(step, source, source_b, both) for step in STEPS]
-    for phase in range(3):
+def summed(source, source_b, own, sibling):
+    operands = (source, source_b, own, sibling)
+    parts = [(2, None), (1, None), (3, 0), (3, 1), (0, None)]
+    pieces = [bins(step, half, *operands) for step, half in parts]
+    pieces = [shifted(piece, 0, step) if step else piece for piece, (step, _) in zip(pieces, parts)]
+    blocks = merged([piece.reshape(-1, 4, 2 * ROWS, 128) for piece in pieces], 1)
+    for phase in (1, 2):
         blocks = [shifted(block, phase, step) if step else block for block, step in zip(blocks, STEPS)]
-        if phase < 2:
-            blocks = merged([block.reshape((4, -1) + block.shape[-2:]) if block.shape[0] == 16 else block for block in blocks], phase + 1)
+        if phase == 1:
+            blocks = merged(blocks, 2)
     return (blocks[0] + blocks[1]) + (blocks[2] + blocks[3])
 
 
@@ -379,10 +382,10 @@
     core = lax.axis_index("core").reshape(1)
     swap = [(0, 1), (1, 0)]
     own, other, tile = first(core, state, delay, fraction)
-    both = kept(own, lax.ppermute(other, "core", swap))
+    sibling = kept(lax.ppermute(other, "core", swap))
     source = slot_source(tile, surf_index, surf_count)
     source_b = lax.ppermute(source, "core", swap)
-    total = summed(source, source_b, both)
+    total = summed(source, source_b, own, sibling)
     total = total.reshape(2, ROWS, 16, 8).transpose(0, 3, 1, 2).reshape(16, ROWS, 16)
     carry = jnp.pad(total[:, :34, 15:], ((0, 0), (1, 0), (0, 14)))
     return (total[:, :35, :RADIX] + carry).reshape(16, 35 * RADIX)[:, :SAMPLES]

time: 60.9 us -> 58.5 us (0.961)
  Pallas kernels: 23.3 us -> 22 us
    pallas_call x5 -> x6, Pallas kernels: 18.7 us -> 17.6 us  [the longest x5 16.7 us: bins(): pl.pallas_call(functools.partial(bins_kernel, ahead, start, count), in_sp...]
    ppermute x9 -> x10, waiting for transfers between devices: 10 us -> 9.28 us  [shifted(): return lax.ppermute(array, AXIAL + AZIMUTHAL, moves)]
    ppermute x9 -> x10, starting transfers between devices: 14.5 us -> 14.3 us  [shifted(): return lax.ppermute(array, AXIAL + AZIMUTHAL, moves)]
  transfers between devices with their start and end apart: 15 -> 16, of which waited for: 7 -> 9; matrix products, arithmetic and copies ran while one was open for 0% -> 0% of each run, Pallas kernels for 25% -> 24%
where the time goes in v7:
time: 58.5 us; the launch traced here: 58.3 us
  starting transfers between devices  23.5 us (40%)
  Pallas kernels  22 us (38%)
  waiting for transfers between devices  10.6 us (18%)
  local copies, waits for them, and re-layouts  1.26 us (2%)
  between operations  0.82 us (1%)
    pallas_call x5, Pallas kernels, bins(): pl.pallas_call(functools.partial(bins_kernel, ahead, start, count), in_sp...  16.7 us
    ppermute x10, starting transfers between devices, shifted(): return lax.ppermute(array, AXIAL + AZIMUTHAL, moves)  14.3 us
    ppermute x10, waiting for transfers between devices, shifted(): return lax.ppermute(array, AXIAL + AZIMUTHAL, moves)  9.28 us
    ppermute x4, starting transfers between devices, slot_source(): lax.ppermute(tile, AXIAL + AZIMUTHAL, neighbour(kind))  9.18 us
    pallas_call x1, Pallas kernels, first(): pl.pallas_call(first_kernel, grid_spec=pltpu.PrefetchScalarGridSpec(num_s...  3.9 us
  transfers between devices with their start and end apart: 16, of which 9 were waited for; matrix products, arithmetic and copies ran while one was open for 0% of the time, Pallas kernels for 24%

profile of v7, /device:TPU:0, one launch (start us, length us, event | category | flops | bytes accessed | tf_op | source)
XLA Modules:
  0.0 58.3 jit_solution(12450028078412815716)
XLA Ops:
  0.0 3.9 %first.1 = (f32[1024,640]{1,0:T(8,128)S(1)}, f32[1024,640]{1,0:T(8,128)S(1)}, f32[8,128]{1,0:T(8,128)S(1)}) custom-call(s32[1]{0:T(128)} %bitcast.core_ref, f32[5,64,128]{2,1,0:T(8,128)} %bitcast.19, s32[272,2048]{1,0:T(8,128)} %other_delay.1, f32[272,2048]{1,0:T(8,128)} %other_fraction.1, s32[272,2048]{1,0:T(8,128)} %other_delay.1, f32[272,2048]{1,0:T(8,128)} %other_fraction.1), custom_call_target="tpu_custom_call" | custom-call | tf_op jit(solution)/shard_map/first/pallas_call | solution.py:89
  3.9 0.1 collective-permute-start.5
  4.0 6.7 %collective-permute-start.3 = (f32[8,128]{1,0:T(8,128)S(1)}, f32[8,128]{1,0:T(8,128)S(1)}, u32[]{:S(2)}, u32[]{:S(2)}) collective-permute-start(f32[8,128]{1,0:T(8,128)S(1)} %get-tuple-element.16.own_ref), channel_id=1, source_target_pairs={{0,15},{1,2},{2,1},{3,4},{4,3},{5,6},{6,5},{7,8},{8,7},{9,10},{10,... | collective-permute-start | bytes 12296 | tf_op jit(solution)/shard_map/ppermute | solution.py:208
  10.7 0.0 collective-permute-start.2
  10.7 2.5 %collective-permute-start.1 = (f32[8,128]{1,0:T(8,128)S(1)}, f32[8,128]{1,0:T(8,128)S(1)}, u32[]{:S(2)}, u32[]{:S(2)}) collective-permute-start(f32[8,128]{1,0:T(8,128)S(1)} %get-tuple-element.16.own_ref), channel_id=1, source_target_pairs={{0,112},{1,113},{2,114},{3,115},{4,116},{5,117},{6,118},{7,119},{8... | collective-permute-start | bytes 12296 | tf_op jit(solution)/shard_map/ppermute | solution.py:208
  13.2 0.0 collective-permute-start
  13.8 0.0 collective-permute-done.3.odd_ref
  13.9 0.4 collective-permute-done.2.even_ref
  14.3 0.6 %collective-permute-done.1.chip_ref = f32[8,128]{1,0:T(8,128)S(1)} collective-permute-done((f32[8,128]{1,0:T(8,128)S(1)}, f32[8,128]{1,0:T(8,128)S(1)}, u32[]{:S(2)}, u32[]{:S(2)}) %collective-permute-start.1) | collective-permute-done | bytes 4128 | tf_op jit(solution)/shard_map/ppermute | solution.py:208
  14.9 0.0 collective-permute-done.core_ref
  14.9 0.0 copy-done
  14.9 0.3 source.1.src_ref
  15.2 0.0 collective-permute-start.4
  15.2 0.0 collective-permute-done.5.from_ref
  15.2 0.9 %kept.1.sib_ref = f32[1024,640]{1,0:T(8,128)S(1)} custom-call(f32[1024,640]{1,0:T(8,128)S(1)} %collective-permute-done.5.from_ref), custom_call_target="tpu_custom_call" | custom-call | tf_op jit(solution)/shard_map/kept/pallas_call | solution.py:318
  16.1 0.2 collective-permute-done.4.src_b_ref
  16.4 4.1 %bins.5 = f32[16,72,128]{2,1,0:T(8,128)S(1)} custom-call(f32[1,272]{1,0:T(1,128)S(1)} %source.1.src_ref, f32[1,272]{1,0:T(1,128)S(1)} %collective-permute-done.4.src_b_ref, f32[1024,640]{1,0:T(8,128)S(1)} %get-tuple-element.17.own_ref, f32[1024,640]{1,0:T(8,128)S(1)} %kept.1.sib_ref), custom_call_target="tpu_custom_call" | custom-call | flops 3019898880 | bytes 1310720 | tf_op jit(solution)/shard_map/bins/pallas_call | solution.py:294
  20.5 2.5 %collective-permute-start.6 = (f32[16,72,128]{2,1,0:T(8,128)S(1)}, f32[16,72,128]{2,1,0:T(8,128)S(1)}, u32[]{:S(2)}, u32[]{:S(2)}) collective-permute-start(f32[16,72,128]{2,1,0:T(8,128)S(1)} %bins.5), channel_id=1, source_target_pairs={{0,64},{1,65},{2,66},{3,67},{4,68},{5,69},{6,70},{7,71},{8,72},{9,... | collective-permute-start | bytes 1769480 | tf_op jit(solution)/shard_map/ppermute | solution.py:336
  23.0 4.1 %bins.6 = f32[16,72,128]{2,1,0:T(8,128)S(1)} custom-call(f32[1,272]{1,0:T(1,128)S(1)} %source.1.src_ref, f32[1,272]{1,0:T(1,128)S(1)} %collective-permute-done.4.src_b_ref, f32[1024,640]{1,0:T(8,128)S(1)} %get-tuple-element.17.own_ref, f32[1024,640]{1,0:T(8,128)S(1)} %kept.1.sib_ref), custom_call_target="tpu_custom_call" | custom-call | flops 3019898880 | bytes 1310720 | tf_op jit(solution)/shard_map/bins/pallas_call | solution.py:294
  27.1 1.4 %collective-permute-start.7 = (f32[16,72,128]{2,1,0:T(8,128)S(1)}, f32[16,72,128]{2,1,0:T(8,128)S(1)}, u32[]{:S(2)}, u32[]{:S(2)}) collective-permute-start(f32[16,72,128]{2,1,0:T(8,128)S(1)} %bins.6), channel_id=1, source_target_pairs={{0,32},{1,33},{2,34},{3,35},{4,36},{5,37},{6,38},{7,39},{8,40},{9,... | collective-permute-start | bytes 1769480 | tf_op jit(solution)/shard_map/ppermute | solution.py:336
  28.6 2.2 %bins.7 = f32[8,72,128]{2,1,0:T(8,128)S(1)} custom-call(f32[1,272]{1,0:T(1,128)S(1)} %source.1.src_ref, f32[1,272]{1,0:T(1,128)S(1)} %collective-permute-done.4.src_b_ref, f32[1024,640]{1,0:T(8,128)S(1)} %get-tuple-element.17.own_ref, f32[1024,640]{1,0:T(8,128)S(1)} %kept.1.sib_ref), custom_call_target="tpu_custom_call" | custom-call | flops 3019898880 | bytes 1310720 | tf_op jit(solution)/shard_map/bins/pallas_call | solution.py:294
  30.7 2.2 %collective-permute-start.8 = (f32[8,72,128]{2,1,0:T(8,128)S(1)}, f32[8,72,128]{2,1,0:T(8,128)S(1)}, u32[]{:S(2)}, u32[]{:S(2)}) collective-permute-start(f32[8,72,128]{2,1,0:T(8,128)S(1)} %bins.7), channel_id=1, source_target_pairs={{0,96},{1,97},{2,98},{3,99},{4,100},{5,101},{6,102},{7,103},{8,104... | collective-permute-start | bytes 884744 | tf_op jit(solution)/shard_map/ppermute | solution.py:336
  32.9 2.2 %bins.8 = f32[8,72,128]{2,1,0:T(8,128)S(1)} custom-call(f32[1,272]{1,0:T(1,128)S(1)} %source.1.src_ref, f32[1,272]{1,0:T(1,128)S(1)} %collective-permute-done.4.src_b_ref, f32[1024,640]{1,0:T(8,128)S(1)} %get-tuple-element.17.own_ref, f32[1024,640]{1,0:T(8,128)S(1)} %kept.1.sib_ref), custom_call_target="tpu_custom_call" | custom-call | flops 3019898880 | bytes 1310720 | tf_op jit(solution)/shard_map/bins/pallas_call | solution.py:294
  35.0 0.1 collective-permute-start.9
  35.1 4.1 %bins.9 = f32[16,72,128]{2,1,0:T(8,128)S(1)} custom-call(f32[1,272]{1,0:T(1,128)S(1)} %source.1.src_ref, f32[1,272]{1,0:T(1,128)S(1)} %collective-permute-done.4.src_b_ref, f32[1024,640]{1,0:T(8,128)S(1)} %get-tuple-element.17.own_ref, f32[1024,640]{1,0:T(8,128)S(1)} %kept.1.sib_ref), custom_call_target="tpu_custom_call" | custom-call | flops 3019898880 | bytes 1310720 | tf_op jit(solution)/shard_map/bins/pallas_call | solution.py:294
  39.3 0.0 collective-permute-done.8
  39.3 2.5 %collective-permute-done.9 = f32[8,72,128]{2,1,0:T(8,128)S(1)} collective-permute-done((f32[8,72,128]{2,1,0:T(8,128)S(1)}, f32[8,72,128]{2,1,0:T(8,128)S(1)}, u32[]{:S(2)}, u32[]{:S(2)}) %collective-permute-start.9) | collective-permute-done | bytes 294944 | tf_op jit(solution)/shard_map/ppermute | solution.py:336
  41.8 0.0 collective-permute-done.6
  41.8 0.0 collective-permute-done.7
  41.8 0.2 merged.2
  42.0 0.7 %collective-permute-start.10 = (f32[4,72,128]{2,1,0:T(8,128)S(1)}, f32[4,72,128]{2,1,0:T(8,128)S(1)}, u32[]{:S(2)}, u32[]{:S(2)}) collective-permute-start(f32[4,72,128]{2,1,0:T(8,128)S(1)} %get-tuple-element.19), channel_id=1, source_target_pairs={{0,8},{1,9},{2,10},{3,11},{4,12},{5,13},{6,14},{7,15},{8,0},{9,1},... | collective-permute-start | bytes 442376 | tf_op jit(solution)/shard_map/ppermute | solution.py:336
  42.7 1.0 %collective-permute-start.11 = (f32[4,72,128]{2,1,0:T(8,128)S(1)}, f32[4,72,128]{2,1,0:T(8,128)S(1)}, u32[]{:S(2)}, u32[]{:S(2)}) collective-permute-start(f32[4,72,128]{2,1,0:T(8,128)S(1)} %get-tuple-element.20), channel_id=1, source_target_pairs={{0,4},{1,5},{2,6},{3,7},{4,8},{5,9},{6,10},{7,11},{8,12},{9,13},{1... | collective-permute-start | bytes 442376 | tf_op jit(solution)/shard_map/ppermute | solution.py:336
  43.7 2.3 %collective-permute-start.12 = (f32[4,72,128]{2,1,0:T(8,128)S(1)}, f32[4,72,128]{2,1,0:T(8,128)S(1)}, u32[]{:S(2)}, u32[]{:S(2)}) collective-permute-start(f32[4,72,128]{2,1,0:T(8,128)S(1)} %get-tuple-element.21), channel_id=1, source_target_pairs={{0,12},{1,13},{2,14},{3,15},{4,0},{5,1},{6,2},{7,3},{8,4},{9,5},{1... | collective-permute-start | bytes 442376 | tf_op jit(solution)/shard_map/ppermute | solution.py:336
  45.9 2.9 %collective-permute-done.10.refs_0_ = f32[4,72,128]{2,1,0:T(8,128)S(1)} collective-permute-done((f32[4,72,128]{2,1,0:T(8,128)S(1)}, f32[4,72,128]{2,1,0:T(8,128)S(1)}, u32[]{:S(2)}, u32[]{:S(2)}) %collective-permute-start.10) | collective-permute-done | bytes 147488 | tf_op jit(solution)/shard_map/ppermute | solution.py:336
  48.8 1.5 %collective-permute-done.11.refs_1_ = f32[4,72,128]{2,1,0:T(8,128)S(1)} collective-permute-done((f32[4,72,128]{2,1,0:T(8,128)S(1)}, f32[4,72,128]{2,1,0:T(8,128)S(1)}, u32[]{:S(2)}, u32[]{:S(2)}) %collective-permute-start.11) | collective-permute-done | bytes 147488 | tf_op jit(solution)/shard_map/ppermute | solution.py:336
  50.3 0.0 collective-permute-done.12.refs_2_
  50.3 0.1 collective-permute-start.13
  50.4 2.5 %collective-permute-start.14 = (f32[72,128]{1,0:T(8,128)S(1)}, f32[72,128]{1,0:T(8,128)S(1)}, u32[]{:S(2)}, u32[]{:S(2)}) collective-permute-start(f32[72,128]{1,0:T(8,128)S(1)} %get-tuple-element.24), channel_id=1, source_target_pairs={{0,1},{1,2},{2,3},{3,0},{4,5},{5,6},{6,7},{7,4},{8,9},{9,10},{10,1... | collective-permute-start | bytes 110600 | tf_op jit(solution)/shard_map/ppermute | solution.py:336
  52.9 1.6 %collective-permute-start.15 = (f32[72,128]{1,0:T(8,128)S(1)}, f32[72,128]{1,0:T(8,128)S(1)}, u32[]{:S(2)}, u32[]{:S(2)}) collective-permute-start(f32[72,128]{1,0:T(8,128)S(1)} %get-tuple-element.25), channel_id=1, source_target_pairs={{0,3},{1,0},{2,1},{3,2},{4,7},{5,4},{6,5},{7,6},{8,11},{9,8},{10,9... | collective-permute-start | bytes 110600 | tf_op jit(solution)/shard_map/ppermute | solution.py:336
  54.5 1.4 %collective-permute-done.13 = f32[72,128]{1,0:T(8,128)S(1)} collective-permute-done((f32[72,128]{1,0:T(8,128)S(1)}, f32[72,128]{1,0:T(8,128)S(1)}, u32[]{:S(2)}, u32[]{:S(2)}) %collective-permute-start.13) | collective-permute-done | bytes 36896 | tf_op jit(solution)/shard_map/ppermute | solution.py:336
  55.9 0.6 collective-permute-done.14
  56.5 0.4 collective-permute-done.15
  56.9 0.1 copy.6
  57.0 0.1 reshape.37
  57.2 0.1 slice_add_fusion
  57.3 0.2 copy.8
  57.5 0.1 reshape.39
  57.7 0.6 %slice.14 = f32[16,512]{1,0:T(8,128)} slice(f32[16,525]{1,0:T(8,128)S(1)} %reshape.39), slice={[0:16], [0:512]} | slice | bytes 65536 | tf_op jit(solution)/shard_map/slice | solution.py:391
  (5 shorter events, 0.1 us)
Async XLA Ops:
  0.0 14.9 %copy-start = (s32[272]{0:T(512)S(1)}, s32[272]{0:T(512)}, u32[]{:S(2)}) copy-start(s32[272]{0:T(512)} %index_ref.1) | copy-start | bytes 3268
  3.9 11.3 %collective-permute-start.5 = (f32[1024,640]{1,0:T(8,128)S(1)}, f32[1024,640]{1,0:T(8,128)S(1)}, u32[]{:S(2)}, u32[]{:S(2)}) collective-permute-start(f32[1024,640]{1,0:T(8,128)S(1)} %get-tuple-element.18), channel_id=1, source_target_pairs={{0,16},{16,0},{1,17},{17,1},{2,18},{18,2},{3,19},{19,3},{4,20},{20... | collective-permute-start | bytes 7864328 | tf_op jit(solution)/shard_map/ppermute | solution.py:385
  4.0 9.8 %collective-permute-start.3 = (f32[8,128]{1,0:T(8,128)S(1)}, f32[8,128]{1,0:T(8,128)S(1)}, u32[]{:S(2)}, u32[]{:S(2)}) collective-permute-start(f32[8,128]{1,0:T(8,128)S(1)} %get-tuple-element.16.own_ref), channel_id=1, source_target_pairs={{0,15},{1,2},{2,1},{3,4},{4,3},{5,6},{6,5},{7,8},{8,7},{9,10},{10,... | collective-permute-start | bytes 12296 | tf_op jit(solution)/shard_map/ppermute | solution.py:208
  10.7 3.6 %collective-permute-start.2 = (f32[8,128]{1,0:T(8,128)S(1)}, f32[8,128]{1,0:T(8,128)S(1)}, u32[]{:S(2)}, u32[]{:S(2)}) collective-permute-start(f32[8,128]{1,0:T(8,128)S(1)} %get-tuple-element.16.own_ref), channel_id=1, source_target_pairs={{0,1},{1,0},{2,3},{3,2},{4,5},{5,4},{6,7},{7,6},{8,9},{9,8},{10,11... | collective-permute-start | bytes 12296 | tf_op jit(solution)/shard_map/ppermute | solution.py:208
  10.7 4.2 %collective-permute-start.1 = (f32[8,128]{1,0:T(8,128)S(1)}, f32[8,128]{1,0:T(8,128)S(1)}, u32[]{:S(2)}, u32[]{:S(2)}) collective-permute-start(f32[8,128]{1,0:T(8,128)S(1)} %get-tuple-element.16.own_ref), channel_id=1, source_target_pairs={{0,112},{1,113},{2,114},{3,115},{4,116},{5,117},{6,118},{7,119},{8... | collective-permute-start | bytes 12296 | tf_op jit(solution)/shard_map/ppermute | solution.py:208
  13.2 1.7 %collective-permute-start = (f32[8,128]{1,0:T(8,128)S(1)}, f32[8,128]{1,0:T(8,128)S(1)}, u32[]{:S(2)}, u32[]{:S(2)}) collective-permute-start(f32[8,128]{1,0:T(8,128)S(1)} %get-tuple-element.16.own_ref), channel_id=1, source_target_pairs={{0,16},{1,17},{2,18},{3,19},{4,20},{5,21},{6,22},{7,23},{8,24},{9,... | collective-permute-start | bytes 12296 | tf_op jit(solution)/shard_map/ppermute | solution.py:208
  15.2 1.2 %collective-permute-start.4 = (f32[1,272]{1,0:T(1,128)S(1)}, f32[1,272]{1,0:T(1,128)S(1)}, u32[]{:S(2)}, u32[]{:S(2)}) collective-permute-start(f32[1,272]{1,0:T(1,128)S(1)} %source.1.src_ref), channel_id=1, source_target_pairs={{0,16},{16,0},{1,17},{17,1},{2,18},{18,2},{3,19},{19,3},{4,20},{20... | collective-permute-start | bytes 3272 | tf_op jit(solution)/shard_map/ppermute | solution.py:387
  20.5 21.3 %collective-permute-start.6 = (f32[16,72,128]{2,1,0:T(8,128)S(1)}, f32[16,72,128]{2,1,0:T(8,128)S(1)}, u32[]{:S(2)}, u32[]{:S(2)}) collective-permute-start(f32[16,72,128]{2,1,0:T(8,128)S(1)} %bins.5), channel_id=1, source_target_pairs={{0,64},{1,65},{2,66},{3,67},{4,68},{5,69},{6,70},{7,71},{8,72},{9,... | collective-permute-start | bytes 1769480 | tf_op jit(solution)/shard_map/ppermute | solution.py:336
  27.1 14.7 %collective-permute-start.7 = (f32[16,72,128]{2,1,0:T(8,128)S(1)}, f32[16,72,128]{2,1,0:T(8,128)S(1)}, u32[]{:S(2)}, u32[]{:S(2)}) collective-permute-start(f32[16,72,128]{2,1,0:T(8,128)S(1)} %bins.6), channel_id=1, source_target_pairs={{0,32},{1,33},{2,34},{3,35},{4,36},{5,37},{6,38},{7,39},{8,40},{9,... | collective-permute-start | bytes 1769480 | tf_op jit(solution)/shard_map/ppermute | solution.py:336
  30.7 8.6 %collective-permute-start.8 = (f32[8,72,128]{2,1,0:T(8,128)S(1)}, f32[8,72,128]{2,1,0:T(8,128)S(1)}, u32[]{:S(2)}, u32[]{:S(2)}) collective-permute-start(f32[8,72,128]{2,1,0:T(8,128)S(1)} %bins.7), channel_id=1, source_target_pairs={{0,96},{1,97},{2,98},{3,99},{4,100},{5,101},{6,102},{7,103},{8,104... | collective-permute-start | bytes 884744 | tf_op jit(solution)/shard_map/ppermute | solution.py:336
  35.0 6.8 %collective-permute-start.9 = (f32[8,72,128]{2,1,0:T(8,128)S(1)}, f32[8,72,128]{2,1,0:T(8,128)S(1)}, u32[]{:S(2)}, u32[]{:S(2)}) collective-permute-start(f32[8,72,128]{2,1,0:T(8,128)S(1)} %bins.8), channel_id=1, source_target_pairs={{0,96},{1,97},{2,98},{3,99},{4,100},{5,101},{6,102},{7,103},{8,104... | collective-permute-start | bytes 884744 | tf_op jit(solution)/shard_map/ppermute | solution.py:336
  42.0 6.8 %collective-permute-start.10 = (f32[4,72,128]{2,1,0:T(8,128)S(1)}, f32[4,72,128]{2,1,0:T(8,128)S(1)}, u32[]{:S(2)}, u32[]{:S(2)}) collective-permute-start(f32[4,72,128]{2,1,0:T(8,128)S(1)} %get-tuple-element.19), channel_id=1, source_target_pairs={{0,8},{1,9},{2,10},{3,11},{4,12},{5,13},{6,14},{7,15},{8,0},{9,1},... | collective-permute-start | bytes 442376 | tf_op jit(solution)/shard_map/ppermute | solution.py:336
  42.7 7.6 %collective-permute-start.11 = (f32[4,72,128]{2,1,0:T(8,128)S(1)}, f32[4,72,128]{2,1,0:T(8,128)S(1)}, u32[]{:S(2)}, u32[]{:S(2)}) collective-permute-start(f32[4,72,128]{2,1,0:T(8,128)S(1)} %get-tuple-element.20), channel_id=1, source_target_pairs={{0,4},{1,5},{2,6},{3,7},{4,8},{5,9},{6,10},{7,11},{8,12},{9,13},{1... | collective-permute-start | bytes 442376 | tf_op jit(solution)/shard_map/ppermute | solution.py:336
  43.7 6.6 %collective-permute-start.12 = (f32[4,72,128]{2,1,0:T(8,128)S(1)}, f32[4,72,128]{2,1,0:T(8,128)S(1)}, u32[]{:S(2)}, u32[]{:S(2)}) collective-permute-start(f32[4,72,128]{2,1,0:T(8,128)S(1)} %get-tuple-element.21), channel_id=1, source_target_pairs={{0,12},{1,13},{2,14},{3,15},{4,0},{5,1},{6,2},{7,3},{8,4},{9,5},{1... | collective-permute-start | bytes 442376 | tf_op jit(solution)/shard_map/ppermute | solution.py:336
  50.3 5.5 %collective-permute-start.13 = (f32[72,128]{1,0:T(8,128)S(1)}, f32[72,128]{1,0:T(8,128)S(1)}, u32[]{:S(2)}, u32[]{:S(2)}) collective-permute-start(f32[72,128]{1,0:T(8,128)S(1)} %get-tuple-element.23), channel_id=1, source_target_pairs={{0,2},{1,3},{2,0},{3,1},{4,6},{5,7},{6,4},{7,5},{8,10},{9,11},{10,... | collective-permute-start | bytes 110600 | tf_op jit(solution)/shard_map/ppermute | solution.py:336
  50.4 6.0 %collective-permute-start.14 = (f32[72,128]{1,0:T(8,128)S(1)}, f32[72,128]{1,0:T(8,128)S(1)}, u32[]{:S(2)}, u32[]{:S(2)}) collective-permute-start(f32[72,128]{1,0:T(8,128)S(1)} %get-tuple-element.24), channel_id=1, source_target_pairs={{0,1},{1,2},{2,3},{3,0},{4,5},{5,6},{6,7},{7,4},{8,9},{9,10},{10,1... | collective-permute-start | bytes 110600 | tf_op jit(solution)/shard_map/ppermute | solution.py:336
  52.9 4.0 %collective-permute-start.15 = (f32[72,128]{1,0:T(8,128)S(1)}, f32[72,128]{1,0:T(8,128)S(1)}, u32[]{:S(2)}, u32[]{:S(2)}) collective-permute-start(f32[72,128]{1,0:T(8,128)S(1)} %get-tuple-element.25), channel_id=1, source_target_pairs={{0,3},{1,0},{2,1},{3,2},{4,7},{5,4},{6,5},{7,6},{8,11},{9,8},{10,9... | collective-permute-start | bytes 110600 | tf_op jit(solution)/shard_map/ppermute | solution.py:336

commit v8 on v7

--- a/solution.py
+++ b/solution.py
@@ -41,13 +41,12 @@
 
 
 def first_kernel(core_ref, state_ref, own_delay, own_fraction, other_delay, other_fraction, own_ref, other_ref, tile_ref):
-    own_block = own_ref.at[pl.ds(pl.multiple_of(pl.program_id(0) * 256, 256), 256)]
+    own_block = own_ref.at[pl.ds(pl.multiple_of(pl.program_id(0) * 128, 128), 128)]
     for delay, fraction, out in (
         (own_delay, own_fraction, own_block),
         (other_delay, other_fraction, other_ref),
     ):
-        for at in (0, 128):
-            rows = slice(at, at + 128)
+        for rows in (slice(0, 128),):
             two = (delay[0:128, rows] + 512 * delay[128:256, rows]).astype(jnp.float32).T
             second = jnp.floor(two * (1.0 / 512.0))
             out[rows, 0:128] = two - 512.0 * second
@@ -80,8 +79,8 @@
 
 
 def first(core, state, delay, fraction):
-    mine = pl.BlockSpec((SLOTS, 256), lambda n, c: (0, 2 * n + c[0]))
-    other = pl.BlockSpec((SLOTS, 256), lambda n, c: (0, 2 * n + 1 - c[0]))
+    mine = pl.BlockSpec((SLOTS, 128), lambda n, c: (0, n // 2 * 4 + 2 * c[0] + n % 2))
+    other = pl.BlockSpec((SLOTS, 128), lambda n, c: (0, n // 2 * 4 + 2 - 2 * c[0] + n % 2))
     state = state.reshape(5, 64, state.shape[3])
     delay, fraction, state = (
         pltpu.with_memory_space_constraint(array, pltpu.HBM) for array in (delay, fraction, state)
@@ -90,11 +89,11 @@
         first_kernel,
         grid_spec=pltpu.PrefetchScalarGridSpec(
             num_scalar_prefetch=1,
-            grid=(4,),
+            grid=(8,),
             in_specs=[pl.BlockSpec(state.shape, lambda n, c: (0, 0, 0)), mine, mine, other, other],
             out_specs=[
                 pl.BlockSpec(memory_space=pltpu.VMEM),
-                pl.BlockSpec((256, LANES), lambda n, c: (n, 0)),
+                pl.BlockSpec((128, LANES), lambda n, c: (n, 0)),
                 pl.BlockSpec((8, 128), lambda n, c: (0, 0)),
             ],
         ),

time: 58.5 us -> 60.6 us (1.036)
  Pallas kernels: 22 us -> 24.1 us
    pallas_call x1, Pallas kernels: 3.9 us -> 5.94 us  [first(): pl.pallas_call(first_kernel, grid_spec=pltpu.PrefetchScalarGridSpec(num_s...]
  transfers between devices with their start and end apart: 16 -> 16, of which waited for: 9 -> 9; matrix products, arithmetic and copies ran while one was open for 0% -> 0% of each run, Pallas kernels for 24% -> 23%
where the time goes in v8:
time: 60.6 us; the launch traced here: 60.4 us
  Pallas kernels  24.1 us (40%)
  starting transfers between devices  23.6 us (39%)
  waiting for transfers between devices  10.6 us (17%)
  local copies, waits for them, and re-layouts  1.26 us (2%)
  between operations  0.82 us (1%)
    pallas_call x5, Pallas kernels, bins(): pl.pallas_call(functools.partial(bins_kernel, ahead, start, count), in_sp...  16.7 us
    ppermute x10, starting transfers between devices, shifted(): return lax.ppermute(array, AXIAL + AZIMUTHAL, moves)  14.3 us
    ppermute x10, waiting for transfers between devices, shifted(): return lax.ppermute(array, AXIAL + AZIMUTHAL, moves)  9.26 us
    ppermute x4, starting transfers between devices, slot_source(): lax.ppermute(tile, AXIAL + AZIMUTHAL, neighbour(kind))  9.2 us
    pallas_call x1, Pallas kernels, first(): pl.pallas_call(first_kernel, grid_spec=pltpu.PrefetchScalarGridSpec(num_s...  5.94 us
  transfers between devices with their start and end apart: 16, of which 9 were waited for; matrix products, arithmetic and copies ran while one was open for 0% of the time, Pallas kernels for 23%

profile of v8, /device:TPU:0, one launch (start us, length us, event | category | flops | bytes accessed | tf_op | source)
XLA Modules:
  0.0 60.4 jit_solution(483838910969061307)
XLA Ops:
  0.0 5.9 %first.1 = (f32[1024,640]{1,0:T(8,128)S(1)}, f32[1024,640]{1,0:T(8,128)S(1)}, f32[8,128]{1,0:T(8,128)S(1)}) custom-call(s32[1]{0:T(128)} %bitcast.core_ref, f32[5,64,128]{2,1,0:T(8,128)} %bitcast.19, s32[272,2048]{1,0:T(8,128)} %other_delay.1, f32[272,2048]{1,0:T(8,128)} %other_fraction.1, s32[272,2048]{1,0:T(8,128)} %other_delay.1, f32[272,2048]{1,0:T(8,128)} %other_fraction.1), custom_call_target="tpu_custom_call" | custom-call | tf_op jit(solution)/shard_map/first/pallas_call | solution.py:88
  6.0 0.1 collective-permute-start.5
  6.0 6.7 %collective-permute-start.3 = (f32[8,128]{1,0:T(8,128)S(1)}, f32[8,128]{1,0:T(8,128)S(1)}, u32[]{:S(2)}, u32[]{:S(2)}) collective-permute-start(f32[8,128]{1,0:T(8,128)S(1)} %get-tuple-element.16.own_ref), channel_id=1, source_target_pairs={{0,15},{1,2},{2,1},{3,4},{4,3},{5,6},{6,5},{7,8},{8,7},{9,10},{10,... | collective-permute-start | bytes 12296 | tf_op jit(solution)/shard_map/ppermute | solution.py:207
  12.7 0.0 collective-permute-start.2
  12.7 2.5 %collective-permute-start.1 = (f32[8,128]{1,0:T(8,128)S(1)}, f32[8,128]{1,0:T(8,128)S(1)}, u32[]{:S(2)}, u32[]{:S(2)}) collective-permute-start(f32[8,128]{1,0:T(8,128)S(1)} %get-tuple-element.16.own_ref), channel_id=1, source_target_pairs={{0,112},{1,113},{2,114},{3,115},{4,116},{5,117},{6,118},{7,119},{8... | collective-permute-start | bytes 12296 | tf_op jit(solution)/shard_map/ppermute | solution.py:207
  15.2 0.0 collective-permute-start
  15.9 0.0 collective-permute-done.3.odd_ref
  15.9 0.4 collective-permute-done.2.even_ref
  16.3 0.6 %collective-permute-done.1.chip_ref = f32[8,128]{1,0:T(8,128)S(1)} collective-permute-done((f32[8,128]{1,0:T(8,128)S(1)}, f32[8,128]{1,0:T(8,128)S(1)}, u32[]{:S(2)}, u32[]{:S(2)}) %collective-permute-start.1) | collective-permute-done | bytes 4128 | tf_op jit(solution)/shard_map/ppermute | solution.py:207
  17.0 0.0 collective-permute-done.core_ref
  17.0 0.0 copy-done
  17.0 0.3 source.1.src_ref
  17.3 0.0 collective-permute-start.4
  17.3 0.0 collective-permute-done.5.from_ref
  17.3 0.9 %kept.1.sib_ref = f32[1024,640]{1,0:T(8,128)S(1)} custom-call(f32[1024,640]{1,0:T(8,128)S(1)} %collective-permute-done.5.from_ref), custom_call_target="tpu_custom_call" | custom-call | tf_op jit(solution)/shard_map/kept/pallas_call | solution.py:317
  18.2 0.2 collective-permute-done.4.src_b_ref
  18.4 4.1 %bins.5 = f32[16,72,128]{2,1,0:T(8,128)S(1)} custom-call(f32[1,272]{1,0:T(1,128)S(1)} %source.1.src_ref, f32[1,272]{1,0:T(1,128)S(1)} %collective-permute-done.4.src_b_ref, f32[1024,640]{1,0:T(8,128)S(1)} %get-tuple-element.17.own_ref, f32[1024,640]{1,0:T(8,128)S(1)} %kept.1.sib_ref), custom_call_target="tpu_custom_call" | custom-call | flops 3019898880 | bytes 1310720 | tf_op jit(solution)/shard_map/bins/pallas_call | solution.py:293
  22.6 2.5 %collective-permute-start.6 = (f32[16,72,128]{2,1,0:T(8,128)S(1)}, f32[16,72,128]{2,1,0:T(8,128)S(1)}, u32[]{:S(2)}, u32[]{:S(2)}) collective-permute-start(f32[16,72,128]{2,1,0:T(8,128)S(1)} %bins.5), channel_id=1, source_target_pairs={{0,64},{1,65},{2,66},{3,67},{4,68},{5,69},{6,70},{7,71},{8,72},{9,... | collective-permute-start | bytes 1769480 | tf_op jit(solution)/shard_map/ppermute | solution.py:335
  25.1 4.1 %bins.6 = f32[16,72,128]{2,1,0:T(8,128)S(1)} custom-call(f32[1,272]{1,0:T(1,128)S(1)} %source.1.src_ref, f32[1,272]{1,0:T(1,128)S(1)} %collective-permute-done.4.src_b_ref, f32[1024,640]{1,0:T(8,128)S(1)} %get-tuple-element.17.own_ref, f32[1024,640]{1,0:T(8,128)S(1)} %kept.1.sib_ref), custom_call_target="tpu_custom_call" | custom-call | flops 3019898880 | bytes 1310720 | tf_op jit(solution)/shard_map/bins/pallas_call | solution.py:293
  29.2 1.4 %collective-permute-start.7 = (f32[16,72,128]{2,1,0:T(8,128)S(1)}, f32[16,72,128]{2,1,0:T(8,128)S(1)}, u32[]{:S(2)}, u32[]{:S(2)}) collective-permute-start(f32[16,72,128]{2,1,0:T(8,128)S(1)} %bins.6), channel_id=1, source_target_pairs={{0,32},{1,33},{2,34},{3,35},{4,36},{5,37},{6,38},{7,39},{8,40},{9,... | collective-permute-start | bytes 1769480 | tf_op jit(solution)/shard_map/ppermute | solution.py:335
  30.6 2.2 %bins.7 = f32[8,72,128]{2,1,0:T(8,128)S(1)} custom-call(f32[1,272]{1,0:T(1,128)S(1)} %source.1.src_ref, f32[1,272]{1,0:T(1,128)S(1)} %collective-permute-done.4.src_b_ref, f32[1024,640]{1,0:T(8,128)S(1)} %get-tuple-element.17.own_ref, f32[1024,640]{1,0:T(8,128)S(1)} %kept.1.sib_ref), custom_call_target="tpu_custom_call" | custom-call | flops 3019898880 | bytes 1310720 | tf_op jit(solution)/shard_map/bins/pallas_call | solution.py:293
  32.8 2.1 %collective-permute-start.8 = (f32[8,72,128]{2,1,0:T(8,128)S(1)}, f32[8,72,128]{2,1,0:T(8,128)S(1)}, u32[]{:S(2)}, u32[]{:S(2)}) collective-permute-start(f32[8,72,128]{2,1,0:T(8,128)S(1)} %bins.7), channel_id=1, source_target_pairs={{0,96},{1,97},{2,98},{3,99},{4,100},{5,101},{6,102},{7,103},{8,104... | collective-permute-start | bytes 884744 | tf_op jit(solution)/shard_map/ppermute | solution.py:335
  34.9 2.2 %bins.8 = f32[8,72,128]{2,1,0:T(8,128)S(1)} custom-call(f32[1,272]{1,0:T(1,128)S(1)} %source.1.src_ref, f32[1,272]{1,0:T(1,128)S(1)} %collective-permute-done.4.src_b_ref, f32[1024,640]{1,0:T(8,128)S(1)} %get-tuple-element.17.own_ref, f32[1024,640]{1,0:T(8,128)S(1)} %kept.1.sib_ref), custom_call_target="tpu_custom_call" | custom-call | flops 3019898880 | bytes 1310720 | tf_op jit(solution)/shard_map/bins/pallas_call | solution.py:293
  37.1 0.1 collective-permute-start.9
  37.2 4.1 %bins.9 = f32[16,72,128]{2,1,0:T(8,128)S(1)} custom-call(f32[1,272]{1,0:T(1,128)S(1)} %source.1.src_ref, f32[1,272]{1,0:T(1,128)S(1)} %collective-permute-done.4.src_b_ref, f32[1024,640]{1,0:T(8,128)S(1)} %get-tuple-element.17.own_ref, f32[1024,640]{1,0:T(8,128)S(1)} %kept.1.sib_ref), custom_call_target="tpu_custom_call" | custom-call | flops 3019898880 | bytes 1310720 | tf_op jit(solution)/shard_map/bins/pallas_call | solution.py:293
  41.3 0.0 collective-permute-done.8
  41.3 2.5 %collective-permute-done.9 = f32[8,72,128]{2,1,0:T(8,128)S(1)} collective-permute-done((f32[8,72,128]{2,1,0:T(8,128)S(1)}, f32[8,72,128]{2,1,0:T(8,128)S(1)}, u32[]{:S(2)}, u32[]{:S(2)}) %collective-permute-start.9) | collective-permute-done | bytes 294944 | tf_op jit(solution)/shard_map/ppermute | solution.py:335
  43.9 0.0 collective-permute-done.6
  43.9 0.0 collective-permute-done.7
  43.9 0.2 merged.2
  44.0 0.7 %collective-permute-start.10 = (f32[4,72,128]{2,1,0:T(8,128)S(1)}, f32[4,72,128]{2,1,0:T(8,128)S(1)}, u32[]{:S(2)}, u32[]{:S(2)}) collective-permute-start(f32[4,72,128]{2,1,0:T(8,128)S(1)} %get-tuple-element.19), channel_id=1, source_target_pairs={{0,8},{1,9},{2,10},{3,11},{4,12},{5,13},{6,14},{7,15},{8,0},{9,1},... | collective-permute-start | bytes 442376 | tf_op jit(solution)/shard_map/ppermute | solution.py:335
  44.8 1.0 %collective-permute-start.11 = (f32[4,72,128]{2,1,0:T(8,128)S(1)}, f32[4,72,128]{2,1,0:T(8,128)S(1)}, u32[]{:S(2)}, u32[]{:S(2)}) collective-permute-start(f32[4,72,128]{2,1,0:T(8,128)S(1)} %get-tuple-element.20), channel_id=1, source_target_pairs={{0,4},{1,5},{2,6},{3,7},{4,8},{5,9},{6,10},{7,11},{8,12},{9,13},{1... | collective-permute-start | bytes 442376 | tf_op jit(solution)/shard_map/ppermute | solution.py:335
  45.7 2.3 %collective-permute-start.12 = (f32[4,72,128]{2,1,0:T(8,128)S(1)}, f32[4,72,128]{2,1,0:T(8,128)S(1)}, u32[]{:S(2)}, u32[]{:S(2)}) collective-permute-start(f32[4,72,128]{2,1,0:T(8,128)S(1)} %get-tuple-element.21), channel_id=1, source_target_pairs={{0,12},{1,13},{2,14},{3,15},{4,0},{5,1},{6,2},{7,3},{8,4},{9,5},{1... | collective-permute-start | bytes 442376 | tf_op jit(solution)/shard_map/ppermute | solution.py:335
  48.0 2.9 %collective-permute-done.10.refs_0_ = f32[4,72,128]{2,1,0:T(8,128)S(1)} collective-permute-done((f32[4,72,128]{2,1,0:T(8,128)S(1)}, f32[4,72,128]{2,1,0:T(8,128)S(1)}, u32[]{:S(2)}, u32[]{:S(2)}) %collective-permute-start.10) | collective-permute-done | bytes 147488 | tf_op jit(solution)/shard_map/ppermute | solution.py:335
  50.9 1.5 %collective-permute-done.11.refs_1_ = f32[4,72,128]{2,1,0:T(8,128)S(1)} collective-permute-done((f32[4,72,128]{2,1,0:T(8,128)S(1)}, f32[4,72,128]{2,1,0:T(8,128)S(1)}, u32[]{:S(2)}, u32[]{:S(2)}) %collective-permute-start.11) | collective-permute-done | bytes 147488 | tf_op jit(solution)/shard_map/ppermute | solution.py:335
  52.4 0.0 collective-permute-done.12.refs_2_
  52.4 0.1 collective-permute-start.13
  52.5 2.5 %collective-permute-start.14 = (f32[72,128]{1,0:T(8,128)S(1)}, f32[72,128]{1,0:T(8,128)S(1)}, u32[]{:S(2)}, u32[]{:S(2)}) collective-permute-start(f32[72,128]{1,0:T(8,128)S(1)} %get-tuple-element.24), channel_id=1, source_target_pairs={{0,1},{1,2},{2,3},{3,0},{4,5},{5,6},{6,7},{7,4},{8,9},{9,10},{10,1... | collective-permute-start | bytes 110600 | tf_op jit(solution)/shard_map/ppermute | solution.py:335
  55.0 1.6 %collective-permute-start.15 = (f32[72,128]{1,0:T(8,128)S(1)}, f32[72,128]{1,0:T(8,128)S(1)}, u32[]{:S(2)}, u32[]{:S(2)}) collective-permute-start(f32[72,128]{1,0:T(8,128)S(1)} %get-tuple-element.25), channel_id=1, source_target_pairs={{0,3},{1,0},{2,1},{3,2},{4,7},{5,4},{6,5},{7,6},{8,11},{9,8},{10,9... | collective-permute-start | bytes 110600 | tf_op jit(solution)/shard_map/ppermute | solution.py:335
  56.6 1.3 %collective-permute-done.13 = f32[72,128]{1,0:T(8,128)S(1)} collective-permute-done((f32[72,128]{1,0:T(8,128)S(1)}, f32[72,128]{1,0:T(8,128)S(1)}, u32[]{:S(2)}, u32[]{:S(2)}) %collective-permute-start.13) | collective-permute-done | bytes 36896 | tf_op jit(solution)/shard_map/ppermute | solution.py:335
  57.9 0.6 collective-permute-done.14
  58.5 0.4 collective-permute-done.15
  59.0 0.1 copy.6
  59.1 0.1 reshape.37
  59.3 0.1 slice_add_fusion
  59.4 0.2 copy.8
  59.6 0.1 reshape.39
  59.7 0.6 %slice.14 = f32[16,512]{1,0:T(8,128)} slice(f32[16,525]{1,0:T(8,128)S(1)} %reshape.39), slice={[0:16], [0:512]} | slice | bytes 65536 | tf_op jit(solution)/shard_map/slice | solution.py:390
  (5 shorter events, 0.1 us)
Async XLA Ops:
  0.0 17.0 %copy-start = (s32[272]{0:T(512)S(1)}, s32[272]{0:T(512)}, u32[]{:S(2)}) copy-start(s32[272]{0:T(512)} %index_ref.1) | copy-start | bytes 3268
  6.0 11.3 %collective-permute-start.5 = (f32[1024,640]{1,0:T(8,128)S(1)}, f32[1024,640]{1,0:T(8,128)S(1)}, u32[]{:S(2)}, u32[]{:S(2)}) collective-permute-start(f32[1024,640]{1,0:T(8,128)S(1)} %get-tuple-element.18), channel_id=1, source_target_pairs={{0,16},{16,0},{1,17},{17,1},{2,18},{18,2},{3,19},{19,3},{4,20},{20... | collective-permute-start | bytes 7864328 | tf_op jit(solution)/shard_map/ppermute | solution.py:384
  6.0 9.9 %collective-permute-start.3 = (f32[8,128]{1,0:T(8,128)S(1)}, f32[8,128]{1,0:T(8,128)S(1)}, u32[]{:S(2)}, u32[]{:S(2)}) collective-permute-start(f32[8,128]{1,0:T(8,128)S(1)} %get-tuple-element.16.own_ref), channel_id=1, source_target_pairs={{0,15},{1,2},{2,1},{3,4},{4,3},{5,6},{6,5},{7,8},{8,7},{9,10},{10,... | collective-permute-start | bytes 12296 | tf_op jit(solution)/shard_map/ppermute | solution.py:207
  12.7 3.6 %collective-permute-start.2 = (f32[8,128]{1,0:T(8,128)S(1)}, f32[8,128]{1,0:T(8,128)S(1)}, u32[]{:S(2)}, u32[]{:S(2)}) collective-permute-start(f32[8,128]{1,0:T(8,128)S(1)} %get-tuple-element.16.own_ref), channel_id=1, source_target_pairs={{0,1},{1,0},{2,3},{3,2},{4,5},{5,4},{6,7},{7,6},{8,9},{9,8},{10,11... | collective-permute-start | bytes 12296 | tf_op jit(solution)/shard_map/ppermute | solution.py:207
  12.7 4.2 %collective-permute-start.1 = (f32[8,128]{1,0:T(8,128)S(1)}, f32[8,128]{1,0:T(8,128)S(1)}, u32[]{:S(2)}, u32[]{:S(2)}) collective-permute-start(f32[8,128]{1,0:T(8,128)S(1)} %get-tuple-element.16.own_ref), channel_id=1, source_target_pairs={{0,112},{1,113},{2,114},{3,115},{4,116},{5,117},{6,118},{7,119},{8... | collective-permute-start | bytes 12296 | tf_op jit(solution)/shard_map/ppermute | solution.py:207
  15.2 1.7 %collective-permute-start = (f32[8,128]{1,0:T(8,128)S(1)}, f32[8,128]{1,0:T(8,128)S(1)}, u32[]{:S(2)}, u32[]{:S(2)}) collective-permute-start(f32[8,128]{1,0:T(8,128)S(1)} %get-tuple-element.16.own_ref), channel_id=1, source_target_pairs={{0,16},{1,17},{2,18},{3,19},{4,20},{5,21},{6,22},{7,23},{8,24},{9,... | collective-permute-start | bytes 12296 | tf_op jit(solution)/shard_map/ppermute | solution.py:207
  17.3 1.2 %collective-permute-start.4 = (f32[1,272]{1,0:T(1,128)S(1)}, f32[1,272]{1,0:T(1,128)S(1)}, u32[]{:S(2)}, u32[]{:S(2)}) collective-permute-start(f32[1,272]{1,0:T(1,128)S(1)} %source.1.src_ref), channel_id=1, source_target_pairs={{0,16},{16,0},{1,17},{17,1},{2,18},{18,2},{3,19},{19,3},{4,20},{20... | collective-permute-start | bytes 3272 | tf_op jit(solution)/shard_map/ppermute | solution.py:386
  22.6 21.3 %collective-permute-start.6 = (f32[16,72,128]{2,1,0:T(8,128)S(1)}, f32[16,72,128]{2,1,0:T(8,128)S(1)}, u32[]{:S(2)}, u32[]{:S(2)}) collective-permute-start(f32[16,72,128]{2,1,0:T(8,128)S(1)} %bins.5), channel_id=1, source_target_pairs={{0,64},{1,65},{2,66},{3,67},{4,68},{5,69},{6,70},{7,71},{8,72},{9,... | collective-permute-start | bytes 1769480 | tf_op jit(solution)/shard_map/ppermute | solution.py:335
  29.2 14.7 %collective-permute-start.7 = (f32[16,72,128]{2,1,0:T(8,128)S(1)}, f32[16,72,128]{2,1,0:T(8,128)S(1)}, u32[]{:S(2)}, u32[]{:S(2)}) collective-permute-start(f32[16,72,128]{2,1,0:T(8,128)S(1)} %bins.6), channel_id=1, source_target_pairs={{0,32},{1,33},{2,34},{3,35},{4,36},{5,37},{6,38},{7,39},{8,40},{9,... | collective-permute-start | bytes 1769480 | tf_op jit(solution)/shard_map/ppermute | solution.py:335
  32.8 8.6 %collective-permute-start.8 = (f32[8,72,128]{2,1,0:T(8,128)S(1)}, f32[8,72,128]{2,1,0:T(8,128)S(1)}, u32[]{:S(2)}, u32[]{:S(2)}) collective-permute-start(f32[8,72,128]{2,1,0:T(8,128)S(1)} %bins.7), channel_id=1, source_target_pairs={{0,96},{1,97},{2,98},{3,99},{4,100},{5,101},{6,102},{7,103},{8,104... | collective-permute-start | bytes 884744 | tf_op jit(solution)/shard_map/ppermute | solution.py:335
  37.1 6.8 %collective-permute-start.9 = (f32[8,72,128]{2,1,0:T(8,128)S(1)}, f32[8,72,128]{2,1,0:T(8,128)S(1)}, u32[]{:S(2)}, u32[]{:S(2)}) collective-permute-start(f32[8,72,128]{2,1,0:T(8,128)S(1)} %bins.8), channel_id=1, source_target_pairs={{0,96},{1,97},{2,98},{3,99},{4,100},{5,101},{6,102},{7,103},{8,104... | collective-permute-start | bytes 884744 | tf_op jit(solution)/shard_map/ppermute | solution.py:335
  44.0 6.8 %collective-permute-start.10 = (f32[4,72,128]{2,1,0:T(8,128)S(1)}, f32[4,72,128]{2,1,0:T(8,128)S(1)}, u32[]{:S(2)}, u32[]{:S(2)}) collective-permute-start(f32[4,72,128]{2,1,0:T(8,128)S(1)} %get-tuple-element.19), channel_id=1, source_target_pairs={{0,8},{1,9},{2,10},{3,11},{4,12},{5,13},{6,14},{7,15},{8,0},{9,1},... | collective-permute-start | bytes 442376 | tf_op jit(solution)/shard_map/ppermute | solution.py:335
  44.8 7.6 %collective-permute-start.11 = (f32[4,72,128]{2,1,0:T(8,128)S(1)}, f32[4,72,128]{2,1,0:T(8,128)S(1)}, u32[]{:S(2)}, u32[]{:S(2)}) collective-permute-start(f32[4,72,128]{2,1,0:T(8,128)S(1)} %get-tuple-element.20), channel_id=1, source_target_pairs={{0,4},{1,5},{2,6},{3,7},{4,8},{5,9},{6,10},{7,11},{8,12},{9,13},{1... | collective-permute-start | bytes 442376 | tf_op jit(solution)/shard_map/ppermute | solution.py:335
  45.7 6.6 %collective-permute-start.12 = (f32[4,72,128]{2,1,0:T(8,128)S(1)}, f32[4,72,128]{2,1,0:T(8,128)S(1)}, u32[]{:S(2)}, u32[]{:S(2)}) collective-permute-start(f32[4,72,128]{2,1,0:T(8,128)S(1)} %get-tuple-element.21), channel_id=1, source_target_pairs={{0,12},{1,13},{2,14},{3,15},{4,0},{5,1},{6,2},{7,3},{8,4},{9,5},{1... | collective-permute-start | bytes 442376 | tf_op jit(solution)/shard_map/ppermute | solution.py:335
  52.4 5.5 %collective-permute-start.13 = (f32[72,128]{1,0:T(8,128)S(1)}, f32[72,128]{1,0:T(8,128)S(1)}, u32[]{:S(2)}, u32[]{:S(2)}) collective-permute-start(f32[72,128]{1,0:T(8,128)S(1)} %get-tuple-element.23), channel_id=1, source_target_pairs={{0,2},{1,3},{2,0},{3,1},{4,6},{5,7},{6,4},{7,5},{8,10},{9,11},{10,... | collective-permute-start | bytes 110600 | tf_op jit(solution)/shard_map/ppermute | solution.py:335
  52.5 6.0 %collective-permute-start.14 = (f32[72,128]{1,0:T(8,128)S(1)}, f32[72,128]{1,0:T(8,128)S(1)}, u32[]{:S(2)}, u32[]{:S(2)}) collective-permute-start(f32[72,128]{1,0:T(8,128)S(1)} %get-tuple-element.24), channel_id=1, source_target_pairs={{0,1},{1,2},{2,3},{3,0},{4,5},{5,6},{6,7},{7,4},{8,9},{9,10},{10,1... | collective-permute-start | bytes 110600 | tf_op jit(solution)/shard_map/ppermute | solution.py:335
  55.0 4.0 %collective-permute-start.15 = (f32[72,128]{1,0:T(8,128)S(1)}, f32[72,128]{1,0:T(8,128)S(1)}, u32[]{:S(2)}, u32[]{:S(2)}) collective-permute-start(f32[72,128]{1,0:T(8,128)S(1)} %get-tuple-element.25), channel_id=1, source_target_pairs={{0,3},{1,0},{2,1},{3,2},{4,7},{5,4},{6,5},{7,6},{8,11},{9,8},{10,9... | collective-permute-start | bytes 110600 | tf_op jit(solution)/shard_map/ppermute | solution.py:335
